TPU v7x, 512 devices: a whole 4x4x16 slice. The times are simulated.
512 devices in a mesh: dp: 64 (over x_lo, z, core), head: 8 (over x_hi, y).
Axes of the slice: x: 4 (x_hi: 2, x_lo: 2; x = x_hi * 2 + x_lo), y: 4, z: 16, core: 2. Of those that a mesh axis runs over, the one named last changes fastest.
Arguments:
- q_in: bfloat16 [65536, 3072], P(('dp', 'head'))
- k_in: bfloat16 [65536, 3072], P(('dp', 'head'))
- v_in: bfloat16 [65536, 3072], P(('dp', 'head')), may hold values from -6 to 6
- grad_out: bfloat16 [65536, 3072], P(('dp', 'head')), may hold values from -6 to 6
- q_gain: float32 [3072], replicated, may hold values from 0.5 to 2
- k_gain: float32 [3072], replicated, may hold values from 0.5 to 2
- res_len: int32 [64], replicated, may hold values from 1 to 960, as said below
- move_len: int32 [64], replicated, may hold values from 1 to 64, as said below
- step_index: int32 [64, 2], replicated, may hold values from 0 to 999
- dest_group: int32 [64], replicated, may hold values from 0 to 63, each once
- loss_weight: float32 [1000], replicated, may hold values from 0.25 to 4
Outputs:
- grad_q: bfloat16 [65536, 3072], P(('dp', 'head'))
- grad_k: bfloat16 [65536, 3072], P(('dp', 'head'))
- grad_q_gain: float32 [3072], P('head')
- grad_k_gain: float32 [3072], P('head')
Inputs may be any that keep to these rules, and one draw needn't show every extreme that they name: `res_len`: staying clip lengths; some group's clip fills all 8 * 120 slots. `move_len`: leaving clip lengths; some group's clip fills all 8 * 8 slots. `dest_group`: A permutation of the groups.
All inputs are finite; a program needn't handle non-finite values.
Results may differ from a plain program's by a relative error of at most 0.009.
The roundings to bfloat16 on the way count: a program that leaves them out, or rounds other values in their place, can miss the bound.
Values may be sent and summed in bfloat16 or wider, within the bound.
No kernel may reach another device: no remote copies, remote signals or barrier semaphores. Data moves between devices by JAX's collectives and lax.ppermute only.
A program may use at most 64 MiB of HBM per device.

v0:
```python
import math

import jax
import jax.numpy as jnp
from jax import lax
from jax.sharding import PartitionSpec as P

HEAD_DIM = 128
TOK_DEV = 128
MOV = 8
RES = 120


EPS = 1e-06


def clip_grads(norm_query, norm_key, values, weighted, length, head_dim):
    row_count = norm_query.shape[0]
    head_count = norm_query.shape[1] // head_dim
    score_scale = 1.0 / math.sqrt(head_dim)
    key_live = jnp.arange(row_count, dtype=jnp.int32) < length

    def head_step(head_index, carried):
        query_grad, key_grad = carried
        offset = jnp.asarray(head_index, jnp.int32) * head_dim

        def take_head(block):
            return lax.dynamic_slice_in_dim(block, offset, head_dim, 1)

        queries, key_rows, value_rows, grad_rows = (
            take_head(norm_query),
            take_head(norm_key),
            take_head(values),
            take_head(weighted),
        )
        scores = (
            lax.dot_general(
                queries, key_rows, (((1,), (1,)), ((), ())), preferred_element_type=jnp.float32
            )
            * score_scale
        )
        scores = jnp.where(key_live[None, :], scores, jnp.float32(-1e30))
        row_max = jnp.max(scores, axis=1, keepdims=True)
        raw_weights = jnp.exp(scores - row_max)
        weights = raw_weights / jnp.sum(raw_weights, axis=1, keepdims=True)
        attended = jnp.dot(
            weights.astype(jnp.bfloat16), value_rows, preferred_element_type=jnp.float32
        )
        offset_term = jnp.sum(grad_rows.astype(jnp.float32) * attended, axis=1, keepdims=True)
        weight_grad = lax.dot_general(
            grad_rows, value_rows, (((1,), (1,)), ((), ())), preferred_element_type=jnp.float32
        )
        score_grad = (weights * (weight_grad - offset_term)).astype(jnp.bfloat16)
        query_part = (
            jnp.dot(score_grad, key_rows, preferred_element_type=jnp.float32) * score_scale
        ).astype(jnp.bfloat16)
        key_part = (
            lax.dot_general(
                score_grad, queries, (((0,), (0,)), ((), ())), preferred_element_type=jnp.float32
            )
            * score_scale
        ).astype(jnp.bfloat16)
        query_grad = lax.dynamic_update_slice_in_dim(query_grad, query_part, offset, 1)
        key_grad = lax.dynamic_update_slice_in_dim(key_grad, key_part, offset, 1)
        return (query_grad, key_grad)

    zero_block = jnp.zeros(norm_query.shape, jnp.bfloat16)
    return lax.fori_loop(0, head_count, head_step, (zero_block, zero_block))


def local(
    q_in,
    k_in,
    v_in,
    grad_out,
    q_gain,
    k_gain,
    res_len,
    move_len,
    step_index,
    dest_group,
    loss_weight,
):
    group_count = lax.axis_size("dp")
    head_ways = lax.axis_size("head")
    my_group = lax.axis_index("dp")
    my_slot = lax.axis_index("head")
    groups = jnp.arange(group_count, dtype=jnp.int32)
    source = jnp.sum(jnp.where(dest_group == my_group, groups, 0))
    width = q_in.shape[1]
    local_width = width // head_ways
    leaving = (q_in[RES:][None], k_in[RES:][None], v_in[RES:][None])
    portions = (
        lax.all_gather(leaving[0], "dp", axis=0, tiled=True),
        lax.all_gather(leaving[1], "dp", axis=0, tiled=True),
        lax.all_gather(leaving[2], "dp", axis=0, tiled=True),
    )
    chosen = jnp.arange(portions[0].shape[0], dtype=jnp.int32) == source
    arrived = tuple(
        (
            jnp.sum(jnp.where(chosen[:, None, None], portion, jnp.zeros((), portion.dtype)), axis=0)
            for portion in portions
        )
    )
    queries = jnp.concatenate([q_in[:RES], arrived[0]], axis=0)
    key_rows = jnp.concatenate([k_in[:RES], arrived[1]], axis=0)
    value_rows = jnp.concatenate([v_in[:RES], arrived[2]], axis=0)
    stay_here = jnp.sum(jnp.where(groups == my_group, res_len, 0))
    move_here = jnp.sum(jnp.where(groups == source, move_len, 0))
    step_stay = jnp.sum(jnp.where(groups == my_group, step_index[:, 0], 0))
    step_move = jnp.sum(jnp.where(groups == source, step_index[:, 1], 0))
    table = jnp.arange(loss_weight.shape[0], dtype=jnp.int32)
    weight_stay = jnp.sum(jnp.where(table == step_stay, loss_weight, jnp.float32(0.0)))
    weight_move = jnp.sum(jnp.where(table == step_move, loss_weight, jnp.float32(0.0)))
    rows = jnp.arange(TOK_DEV, dtype=jnp.int32)
    stay_pos = my_slot * RES + rows
    move_pos = my_slot * MOV + rows - RES
    token_weight = jnp.where(
        rows < RES,
        jnp.where(stay_pos < stay_here, weight_stay, jnp.float32(0.0)),
        jnp.where(move_pos < move_here, weight_move, jnp.float32(0.0)),
    )
    weighted = (grad_out.astype(jnp.float32) * token_weight[:, None]).astype(jnp.bfloat16)
    q_float = queries.astype(jnp.float32)
    k_float = key_rows.astype(jnp.float32)
    gain_start = my_slot * local_width
    q_scale = lax.rsqrt(jnp.mean(q_float * q_float, axis=1, keepdims=True) + EPS)
    k_scale = lax.rsqrt(jnp.mean(k_float * k_float, axis=1, keepdims=True) + EPS)
    outgoing = (
        (q_float * q_scale * q_gain).astype(jnp.bfloat16),
        (k_float * k_scale * k_gain).astype(jnp.bfloat16),
    )
    spread = (
        lax.all_to_all(outgoing[0], "head", split_axis=1, concat_axis=0, tiled=True),
        lax.all_to_all(outgoing[1], "head", split_axis=1, concat_axis=0, tiled=True),
        lax.all_to_all(value_rows, "head", split_axis=1, concat_axis=0, tiled=True),
        lax.all_to_all(weighted, "head", split_axis=1, concat_axis=0, tiled=True),
    )
    norm_q, norm_k = (spread[0], spread[1])

    def split_clips(block):
        shaped = block.reshape(head_ways, TOK_DEV, block.shape[1])
        return (
            shaped[:, :RES].reshape(head_ways * RES, block.shape[1]),
            shaped[:, RES:].reshape(head_ways * MOV, block.shape[1]),
        )

    clip_parts = [split_clips(block) for block in (norm_q, norm_k, spread[2], spread[3])]
    stay_query, stay_key = clip_grads(
        clip_parts[0][0], clip_parts[1][0], clip_parts[2][0], clip_parts[3][0], stay_here, HEAD_DIM
    )
    move_query, move_key = clip_grads(
        clip_parts[0][1], clip_parts[1][1], clip_parts[2][1], clip_parts[3][1], move_here, HEAD_DIM
    )

    def join_clips(staying, moving):
        joined = jnp.concatenate(
            [
                staying.reshape(head_ways, RES, local_width),
                moving.reshape(head_ways, MOV, local_width),
            ],
            axis=1,
        )
        return joined.reshape(head_ways * TOK_DEV, local_width)

    dq_norm = join_clips(stay_query, move_query)
    dk_norm = join_clips(stay_key, move_key)
    returned = (dq_norm, dk_norm)
    back = (
        lax.all_to_all(returned[0], "head", split_axis=0, concat_axis=1, tiled=True),
        lax.all_to_all(returned[1], "head", split_axis=0, concat_axis=1, tiled=True),
    )
    grad_qn = back[0].astype(jnp.float32)
    grad_kn = back[1].astype(jnp.float32)
    dots_q = jnp.sum(q_float * q_gain * grad_qn, axis=1, keepdims=True)
    dots_k = jnp.sum(k_float * k_gain * grad_kn, axis=1, keepdims=True)
    out_q = (
        q_scale * (q_gain * grad_qn) - q_float * (q_scale * q_scale * q_scale) * dots_q / width
    ).astype(jnp.bfloat16)
    out_k = (
        k_scale * (k_gain * grad_kn) - k_float * (k_scale * k_scale * k_scale) * dots_k / width
    ).astype(jnp.bfloat16)
    totals = lax.psum(
        (
            jnp.sum(grad_qn * q_float * q_scale, axis=0),
            jnp.sum(grad_kn * k_float * k_scale, axis=0),
        ),
        ("dp", "head"),
    )
    gain_q = lax.dynamic_slice_in_dim(totals[0], gain_start, local_width, 0)
    gain_k = lax.dynamic_slice_in_dim(totals[1], gain_start, local_width, 0)
    return (out_q, out_k, gain_q, gain_k)


def solution(mesh):
    placed = (
        P(("dp", "head"), None),
        P(("dp", "head"), None),
        P(("dp", "head"), None),
        P(("dp", "head"), None),
        P(),
        P(),
        P(),
        P(),
        P(),
        P(),
        P(),
    )
    return jax.shard_map(
        local,
        mesh=mesh,
        in_specs=placed,
        out_specs=(P(("dp", "head"), None), P(("dp", "head"), None), P("head"), P("head")),
        check_vma=False,
    )
```

profile of v0, /device:TPU:1, one launch (start us, length us, event | category | flops | bytes accessed | tf_op | source)
XLA Modules:
  0.0 653.0 jit_solution(168117324119416508)
XLA Ops:
  7.2 1.4 slice.58
  8.7 1.4 slice.52
  10.2 1.4 slice.49
  11.6 1.3 fusion.86
  12.9 2.0 select_reduce_fusion.2
  14.9 2.1 fusion.85
  17.0 2.7 select_reduce_fusion.1
  19.7 2.5 compare_select_fusion.2
  22.2 1.3 multiply_convert_fusion.1
  24.5 7.6 %all-to-all-start.2 = ((bf16[128,8,384]{2,0,1:T(8,128)(2,1)}), bf16[128,8,384]{2,0,1:T(8,128)(2,1)}, u32[]{:S(2)}, u32[]{:S(2)}) async-start(bf16[128,8,384]{2,0,1:T(8,128)(2,1)} %bitcast.77), calls=%async_computation.2 | async-start | bytes 1572864 | tf_op jit(solution)/shard_map/all_to_all | solution.py:137
  33.8 106.3 %all-gather.11.cloned.1.call-done = bf16[512,3072]{1,0:T(8,128)(2,1)} async-done(((bf16[8,3072]{1,0:T(8,128)(2,1)}), bf16[512,3072]{1,0:T(8,128)(2,1)}) %all-gather.11.cloned.1.call-update) | async-done | bytes 3145744 | tf_op jit(solution)/shard_map/all_gather | solution.py:96
  140.1 121.9 %all-gather.9.cloned.1.call-done = bf16[512,3072]{1,0:T(8,128)(2,1)} async-done(((bf16[8,3072]{1,0:T(8,128)(2,1)}), bf16[512,3072]{1,0:T(8,128)(2,1)}) %all-gather.9.cloned.1.call-update) | async-done | bytes 3145744 | tf_op jit(solution)/shard_map/all_gather | solution.py:95
  262.0 122.1 %all-gather.7.cloned.1.call-done = bf16[512,3072]{1,0:T(8,128)(2,1)} async-done(((bf16[8,3072]{1,0:T(8,128)(2,1)}), bf16[512,3072]{1,0:T(8,128)(2,1)}) %all-gather.7.cloned.1.call-update) | async-done | bytes 3145744 | tf_op jit(solution)/shard_map/all_gather | solution.py:94
  384.0 4.6 fusion.57
  390.8 6.3 all-to-all-start
  397.5 1.4 copy.74
  400.7 1.0 copy.62
  401.7 7.4 %all-to-all-done = bf16[128,8,384]{2,0,1:T(8,128)(2,1)} async-done(((bf16[128,8,384]{2,0,1:T(8,128)(2,1)}), bf16[128,8,384]{2,0,1:T(8,128)(2,1)}, u32[]{:S(2)}, u32[]{:S(2)}) %all-to-all-start) | async-done | bytes 786464 | tf_op jit(solution)/shard_map/all_to_all | solution.py:134
  409.1 5.5 all-to-all-start.1
  414.6 1.1 slice-done
  416.7 9.2 %all-to-all-done.1 = bf16[128,8,384]{2,0,1:T(8,128)(2,1)} async-done(((bf16[128,8,384]{2,0,1:T(8,128)(2,1)}), bf16[128,8,384]{2,0,1:T(8,128)(2,1)}, u32[]{:S(2)}, u32[]{:S(2)}) %all-to-all-start.1) | async-done | bytes 786464 | tf_op jit(solution)/shard_map/all_to_all | solution.py:135
  425.9 6.1 all-to-all-start.3
  432.0 2.1 slice.66
  434.8 2.1 slice.64
  436.9 2.1 slice.65
  440.6 2.7 all-to-all-done.3
  443.3 1.4 slice_bitcast_fusion
  444.7 2.1 slice.67
  446.7 9.1 %while.33 = (s32[]{:T(128)}, bf16[64,384]{1,0:T(8,128)(2,1)S(1)}, bf16[64,384]{1,0:T(8,128)(2,1)S(1)}, bf16[64,384]{1,0:T(8,128)(2,1)S(1)}, bf16[64,384]{1,0:T(8...) while((s32[]{:T(128)}, bf16[64,384]{1,0:T(8,128)(2,1)S(1)}, ...), condition=%wide.region_21.22_spmd.clone, body=%wide.region_17.21_spmd.clone.sunk | while | flops 5353350 | bytes 295663 | solution.py:68
  447.6 1.0 fusion.143
  450.6 1.0 fusion.143
  453.7 1.0 fusion.143
  457.8 34.4 %while.32 = (s32[]{:T(128)}, bf16[960,384]{1,0:T(8,128)(2,1)}, bf16[960,384]{1,0:T(8,128)(2,1)}, bf16[960,384]{1,0:T(8,128)(2,1)}, bf16[960,384]{1,0:T(8,128)(2,...) while((s32[]{:T(128)}, bf16[960,384]{1,0:T(8,128)(2,1)}, ...), condition=%wide.region_16.17_spmd.clone, body=%wide.region_12.16_spmd.clone.sunk | while | flops 1198016640 | bytes 35189856 | solution.py:68
  458.4 1.8 fusion.128
  461.5 1.5 fusion.130
  463.1 1.7 multiply_convert_fusion.3
  464.8 1.8 fusion.131
  466.6 2.6 fusion.132
  469.9 1.8 fusion.128
  473.0 1.5 fusion.130
  474.6 1.7 multiply_convert_fusion.3
  476.3 1.8 fusion.131
  478.1 2.6 fusion.132
  481.3 1.8 fusion.128
  484.4 1.5 fusion.130
  486.0 1.7 multiply_convert_fusion.3
  487.7 1.8 fusion.131
  489.6 2.6 fusion.132
  492.2 2.1 pad_maximum_fusion.5
  494.3 6.1 all-to-all-start.4
  500.4 2.1 pad_maximum_fusion.6
  502.5 9.2 %all-to-all-done.4 = bf16[8,128,384]{2,1,0:T(8,128)(2,1)} async-done(((bf16[8,128,384]{2,1,0:T(8,128)(2,1)}), bf16[8,128,384]{2,1,0:T(8,128)(2,1)}, u32[]{:S(2)}, u32[]{:S(2)}) %all-to-all-start.4) | async-done | bytes 786464 | tf_op jit(solution)/shard_map/all_to_all | solution.py:170
  511.7 6.1 all-to-all-start.5
  517.8 2.7 convert_bitcast_fusion.1
  520.6 3.0 copy.66
  523.6 2.9 fusion.75
  526.5 2.2 fusion.64
  528.7 2.3 copy.69
  531.0 2.7 convert_bitcast_fusion
  533.7 3.1 copy.68
  536.8 2.7 fusion.81
  539.5 1.4 fusion.69
  540.9 1.2 copy.70
  542.1 103.0 %all-reduce = (f32[3072]{0:T(1024)S(1)}, f32[3072]{0:T(1024)S(1)}) all-reduce(f32[3072]{0:T(1024)S(1)} %reduce_sum.224, f32[3072]{0:T(1024)S(1)} %reduce_sum.226), channel_id=1, replica_groups=mesh['dp'=64,'head'=8] {'dp','head'}, use_global_device_ids=true, to_apply=%region_25.26 | all-reduce | flops 6144 | bytes 49152 | tf_op jit(solution)/shard_map/psum | solution.py:183
  (106 shorter events, 25.4 us)
Async XLA Ops:
  7.2 132.9 %all-gather.11.cloned.1.call-start = ((), (), s32[]{:S(2)}) async-start(), calls=%async_computation.8 | async-start | bytes 3194880 | tf_op jit(solution)/shard_map/all_gather | solution.py:96
  8.7 253.3 %all-gather.9.cloned.1.call-start = ((), (), s32[]{:S(2)}) async-start(), calls=%async_computation.7 | async-start | bytes 3194880 | tf_op jit(solution)/shard_map/all_gather | solution.py:95
  10.1 373.9 %all-gather.7.cloned.1.call-start = ((), (), s32[]{:S(2)}) async-start(), calls=%async_computation.6 | async-start | bytes 3194880 | tf_op jit(solution)/shard_map/all_gather | solution.py:94
  24.5 7.6 %copy-start.9 = (f32[3072]{0:T(1024)S(1)}, f32[3072]{0:T(1024)}, u32[]{:S(2)}) copy-start(f32[3072]{0:T(1024)} %param.19) | copy-start | bytes 36868
  24.5 7.6 %slice-start.1 = ((bf16[128,3072]{1,0:T(8,128)(2,1)}), bf16[120,3072]{1,0:T(8,128)(2,1)S(1)}, s32[]{:S(2)}) async-start(bf16[128,3072]{1,0:T(8,128)(2,1)} %param.15), calls=%async_computation.10 | async-start | bytes 1474560 | tf_op jit(solution)/shard_map/slice | solution.py:105
  24.5 366.3 %all-to-all-start.2 = ((bf16[128,8,384]{2,0,1:T(8,128)(2,1)}), bf16[128,8,384]{2,0,1:T(8,128)(2,1)}, u32[]{:S(2)}, u32[]{:S(2)}) async-start(bf16[128,8,384]{2,0,1:T(8,128)(2,1)} %bitcast.77), calls=%async_computation.2 | async-start | bytes 1572864 | tf_op jit(solution)/shard_map/all_to_all | solution.py:137
  33.1 356.5 %copy-start = (bf16[120,8,384]{2,1,0:T(8,128)(2,1)}, bf16[120,8,384]{2,1,0:T(8,128)(2,1)S(1)}, u32[]{:S(2)}) copy-start(bf16[120,8,384]{2,1,0:T(8,128)(2,1)S(1)} %copy.73) | copy-start | bytes 2211844
  390.8 6.3 copy-start.10
  390.8 6.3 slice-start.2
  390.8 18.2 %all-to-all-start = ((bf16[128,8,384]{2,0,1:T(8,128)(2,1)}), bf16[128,8,384]{2,0,1:T(8,128)(2,1)}, u32[]{:S(2)}, u32[]{:S(2)}) async-start(bf16[128,8,384]{2,0,1:T(8,128)(2,1)} %copy.57), calls=%async_computation | async-start | bytes 1572864 | tf_op jit(solution)/shard_map/all_to_all | solution.py:134
  399.3 1.1 copy-start.1
  409.1 16.8 %all-to-all-start.1 = ((bf16[128,8,384]{2,0,1:T(8,128)(2,1)}), bf16[128,8,384]{2,0,1:T(8,128)(2,1)}, u32[]{:S(2)}, u32[]{:S(2)}) async-start(bf16[128,8,384]{2,0,1:T(8,128)(2,1)} %copy.62), calls=%async_computation.1 | async-start | bytes 1572864 | tf_op jit(solution)/shard_map/all_to_all | solution.py:135
  414.6 1.1 slice-start
  425.9 17.4 %all-to-all-start.3 = ((bf16[128,8,384]{2,0,1:T(8,128)(2,1)}), bf16[128,8,384]{2,0,1:T(8,128)(2,1)}, u32[]{:S(2)}, u32[]{:S(2)}) async-start(bf16[128,8,384]{2,0,1:T(8,128)(2,1)} %bitcast.89), calls=%async_computation.3 | async-start | bytes 1572864 | tf_op jit(solution)/shard_map/all_to_all | solution.py:136
  460.2 1.1 copy-start.7
  460.2 1.3 copy-start.8
  463.1 1.7 copy-start.5
  466.6 2.7 copy-start.6
  471.7 1.1 copy-start.7
  471.7 1.3 copy-start.8
  474.6 1.7 copy-start.5
  478.1 2.6 copy-start.6
  483.1 1.1 copy-start.7
  483.1 1.3 copy-start.8
  486.0 1.7 copy-start.5
  489.5 2.6 copy-start.6
  494.3 17.4 %all-to-all-start.4 = ((bf16[8,128,384]{2,1,0:T(8,128)(2,1)}), bf16[8,128,384]{2,1,0:T(8,128)(2,1)}, u32[]{:S(2)}, u32[]{:S(2)}) async-start(bf16[8,128,384]{2,1,0:T(8,128)(2,1)} %pad_maximum_fusion.5), calls=%async_computation.4 | async-start | bytes 1572864 | tf_op jit(solution)/shard_map/all_to_all | solution.py:170
  511.7 19.3 %all-to-all-start.5 = ((bf16[8,128,384]{2,1,0:T(8,128)(2,1)}), bf16[8,128,384]{2,1,0:T(8,128)(2,1)}, u32[]{:S(2)}, u32[]{:S(2)}) async-start(bf16[8,128,384]{2,1,0:T(8,128)(2,1)} %pad_maximum_fusion.6), calls=%async_computation.5 | async-start | bytes 1572864 | tf_op jit(solution)/shard_map/all_to_all | solution.py:171
  523.6 2.9 copy-start.3
  533.7 3.1 copy-start.2
  536.8 2.7 copy-start.4
Sparse Core Ops, SparseCore 0:
  10.7 129.2 all-gather.10
  142.2 119.7 all-gather.8
  264.1 119.8 all-gather.6
where the time goes:
time: 655 us; the launch traced here: 653 us
  waiting for transfers between devices  379 us (58%)
  blocking collectives  103 us (16%)
  other arithmetic  44 us (7%)
  local copies, waits for them, and re-layouts  39.5 us (6%)
  starting transfers between devices  37.9 us (6%)
  matrix products  35.4 us (5%)
  between operations  14 us (2%)
    all_gather x1, waiting for transfers between devices, local(): lax.all_gather(leaving[0], 'dp', axis=0, tiled=True)  122 us
    all_gather x1, waiting for transfers between devices, local(): lax.all_gather(leaving[1], 'dp', axis=0, tiled=True)  122 us
    all_gather x1, waiting for transfers between devices, local(): lax.all_gather(leaving[2], 'dp', axis=0, tiled=True)  106 us
    psum x1, blocking collectives, local(): lax.psum((jnp.sum(grad_qn * q_float * q_scale, axis=0), jnp.sum(grad_kn *...  103 us
  transfers between devices with their start and end apart: 9, of which 7 were waited for; matrix products, arithmetic and copies ran while one was open for 8% of the time, Pallas kernels for 0%

commit v1 on v0

v1 whole, which is shorter than its diff:
```python
import math

import jax
import jax.numpy as jnp
from jax import lax
from jax.experimental import pallas as pl
from jax.experimental.pallas import tpu as pltpu
from jax.sharding import PartitionSpec as P

HEAD_DIM = 128
TOK_DEV = 128
MOV = 8
RES = 120
EPS = 1e-06
WAYS = 8
GROUPS = 64
HD = 3072
LOCAL = HD // WAYS
HEADS = LOCAL // HEAD_DIM
BLOCKS = HD // 128
SCALE = 1.0 / math.sqrt(HEAD_DIM)
F32 = jnp.float32
BF16 = jnp.bfloat16
VMEM_LIMIT = 56 * 1024 * 1024

PLANE = [[xl * 32 + z * 2 + c for xl in range(2) for c in range(2)] for z in range(16)]
ZRING = [[xl * 32 + z * 2 + c for z in range(16)] for xl in range(2) for c in range(2)]

SMEM = pl.BlockSpec(memory_space=pltpu.SMEM)


def params(count=0):
    return pltpu.CompilerParams(
        vmem_limit_bytes=VMEM_LIMIT,
        dimension_semantics=("arbitrary",) * count if count else None,
    )


def find_source(dest_ref, group):
    return lax.fori_loop(
        0, GROUPS, lambda g, found: jnp.where(dest_ref[g] == group, g, found), jnp.int32(0)
    )


def pack_kernel(q_ref, k_ref, v_ref, out_ref):
    q = q_ref[...].astype(F32)[8:16]
    k = k_ref[...].astype(F32)[8:16]
    v = v_ref[...].astype(F32)[8:16]
    pair = jnp.concatenate([q, k], axis=0).astype(BF16)
    half = HD // 2
    tail = jnp.concatenate([v[:, :half], v[:, half:]], axis=0).astype(BF16)
    for c in range(BLOCKS):
        out_ref[c] = pair[:, c * 128 : (c + 1) * 128]
    for c in range(BLOCKS // 2):
        out_ref[BLOCKS + c] = tail[:, c * 128 : (c + 1) * 128]
    rest = GROUPS - BLOCKS - BLOCKS // 2
    out_ref[pl.ds(BLOCKS + BLOCKS // 2, rest)] = jnp.zeros((rest, 16, 128), BF16)


def pack_short(q_in, k_in, v_in):
    spec = pl.BlockSpec((16, HD), lambda i: (TOK_DEV // 16 - 1, 0))
    return pl.pallas_call(
        pack_kernel,
        grid=(1,),
        in_specs=[spec] * 3,
        out_specs=pl.BlockSpec((GROUPS, 16, 128), lambda i: (0, 0, 0)),
        out_shape=jax.ShapeDtypeStruct((GROUPS, 16, 128), BF16),
        compiler_params=params(1),
        name="pack_short",
    )(q_in, k_in, v_in)


def scatter_kernel(dest_ref, in_ref, out_ref):
    def step(g, carry):
        out_ref[dest_ref[g]] = in_ref[g]
        return carry

    lax.fori_loop(0, GROUPS, step, 0)


def scatter_short(dest_group, parts):
    whole = pl.BlockSpec(memory_space=pltpu.VMEM)
    return pl.pallas_call(
        scatter_kernel,
        in_specs=[SMEM, whole],
        out_specs=whole,
        out_shape=jax.ShapeDtypeStruct(parts.shape, BF16),
        compiler_params=params(),
        name="scatter_short",
    )(dest_group, parts)


def norm_rows(rows, gain):
    scale = lax.rsqrt(jnp.sum(rows * rows, axis=1, keepdims=True) / HD + EPS)
    return rows * scale * gain


def unpack_kernel(in_ref, qg_ref, kg_ref, send_ref, raw_ref):
    pair = jnp.concatenate([in_ref[c] for c in range(BLOCKS)], axis=1).astype(F32)
    tail = jnp.concatenate([in_ref[BLOCKS + c] for c in range(BLOCKS // 2)], axis=1).astype(F32)
    q, k = pair[0:8], pair[8:16]
    v = jnp.concatenate([tail[0:8], tail[8:16]], axis=1)
    qn = norm_rows(q, qg_ref[...])
    kn = norm_rows(k, kg_ref[...])
    zero = jnp.zeros((8, HD), F32)
    first = jnp.concatenate([qn, kn], axis=0).astype(BF16)
    second = jnp.concatenate([v, zero], axis=0).astype(BF16)
    for p in range(WAYS):
        send_ref[p, 0:16, :] = first[:, p * LOCAL : (p + 1) * LOCAL]
        send_ref[p, 16:32, :] = second[:, p * LOCAL : (p + 1) * LOCAL]
    raw_ref[0] = jnp.concatenate([zero, q], axis=0).astype(BF16)
    raw_ref[1] = jnp.concatenate([zero, k], axis=0).astype(BF16)


def unpack_short(parts, q_gain, k_gain):
    whole = pl.BlockSpec(memory_space=pltpu.VMEM)
    return pl.pallas_call(
        unpack_kernel,
        in_specs=[whole] * 3,
        out_specs=[whole] * 2,
        out_shape=[
            jax.ShapeDtypeStruct((WAYS, 32, LOCAL), BF16),
            jax.ShapeDtypeStruct((2, 16, HD), BF16),
        ],
        compiler_params=params(),
        name="unpack_short",
    )(parts, q_gain, k_gain)


PRE_ROWS = 32


def pre_kernel(
    dest_ref, res_ref, move_ref, step_ref, table_ref,
    q_ref, k_ref, v_ref, go_ref, qg_ref, kg_ref,
    *rest,
):
    outs, (qn_ref, kn_ref) = rest[:WAYS], rest[WAYS:]
    group = lax.axis_index("dp")
    slot = lax.axis_index("head")
    source = find_source(dest_ref, group)
    stay_weight = table_ref[step_ref[group, 0]]
    move_weight = table_ref[step_ref[source, 1]]
    rows = pl.program_id(0) * PRE_ROWS + lax.broadcasted_iota(jnp.int32, (PRE_ROWS, 1), 0)
    stay = jnp.where(slot * RES + rows < res_ref[group], stay_weight, 0.0)
    move = jnp.where(slot * MOV + rows - RES < move_ref[source], move_weight, 0.0)
    weight = jnp.where(rows < RES, stay, move)
    qn_ref[...] = norm_rows(q_ref[...].astype(F32), qg_ref[...]).astype(BF16)
    kn_ref[...] = norm_rows(k_ref[...].astype(F32), kg_ref[...]).astype(BF16)
    for s in range(WAYS):
        start = pl.multiple_of(jnp.bitwise_xor(slot, s) * LOCAL, 128)
        cols = pl.ds(start, LOCAL)
        outs[s][0] = qn_ref[:, cols]
        outs[s][1] = kn_ref[:, cols]
        outs[s][2] = v_ref[:, cols]
        outs[s][3] = (go_ref[:, cols].astype(F32) * weight).astype(BF16)


def prepare(dest, res_len, move_len, steps, table, q_in, k_in, v_in, grad_out, q_gain, k_gain):
    rows = pl.BlockSpec((PRE_ROWS, HD), lambda i: (i, 0))
    gain = pl.BlockSpec((1, HD), lambda i: (0, 0))
    return pl.pallas_call(
        pre_kernel,
        grid=(TOK_DEV // PRE_ROWS,),
        in_specs=[SMEM] * 5 + [rows] * 4 + [gain] * 2,
        out_specs=[pl.BlockSpec((4, PRE_ROWS, LOCAL), lambda i: (0, i, 0))] * WAYS,
        out_shape=[jax.ShapeDtypeStruct((4, TOK_DEV, LOCAL), BF16)] * WAYS,
        scratch_shapes=[pltpu.VMEM((PRE_ROWS, HD), BF16)] * 2,
        compiler_params=params(1),
        cost_estimate=pl.CostEstimate(flops=20_000_000, bytes_accessed=6_300_000, transcendentals=0),
        name="prepare",
    )(dest, res_len, move_len, steps, table, q_in, k_in, v_in, grad_out, q_gain, k_gain)


def nt(a, b):
    return lax.dot_general(a, b, (((1,), (1,)), ((), ())), preferred_element_type=F32)


def tn(a, b):
    return lax.dot_general(a, b, (((0,), (0,)), ((), ())), preferred_element_type=F32)


def grads(q, k, v, g, bias):
    scores = nt(q, k) * SCALE + bias
    top = jnp.max(scores, axis=1, keepdims=True)
    raw = jnp.exp(scores - top)
    weights = raw * (1.0 / jnp.sum(raw, axis=1, keepdims=True))
    attended = jnp.dot(weights.astype(BF16), v, preferred_element_type=F32)
    delta = jnp.sum(g.astype(F32) * attended, axis=1, keepdims=True)
    score_grad = (weights * (nt(g, v) - delta)).astype(BF16)
    query_grad = jnp.dot(score_grad, k, preferred_element_type=F32) * SCALE
    return query_grad, tn(score_grad, q)


QUERY_ROWS = 256
ALL = WAYS * TOK_DEV


def attention_kernel(dest_ref, res_ref, move_ref, *rest):
    slots, rest = rest[:WAYS], rest[WAYS:]
    short_ref, qg_ref, kg_ref, out_ref, gain_ref, q_ref, k_ref, v_ref, g_ref, dq_ref, dk_ref = rest
    head = pl.program_id(0)
    group = lax.axis_index("dp")
    slot = lax.axis_index("head")
    source = find_source(dest_ref, group)
    stay_len = res_ref[group]
    move_len = move_ref[source]
    live_rows = lax.broadcasted_iota(jnp.int32, (TOK_DEV, 1), 0) < RES
    lanes = lax.broadcasted_iota(jnp.int32, (1, TOK_DEV), 1)
    biases = []
    for s in range(WAYS):
        here = pl.ds(s * TOK_DEV, TOK_DEV)
        q_ref[here] = slots[s][0]
        k_ref[here] = slots[s][1]
        v_ref[here] = slots[s][2]
        g_ref[here] = jnp.where(live_rows, slots[s][3].astype(F32), 0.0).astype(BF16)
        peer = jnp.bitwise_xor(slot, s)
        limit = jnp.minimum(stay_len - peer * RES, RES)
        biases.append(jnp.where(lanes < limit, 0.0, -1e30).astype(F32))
    bias = jnp.concatenate(biases, axis=1)
    dk_ref[...] = jnp.zeros_like(dk_ref)

    def block(i, carry):
        here = pl.ds(pl.multiple_of(i * QUERY_ROWS, QUERY_ROWS), QUERY_ROWS)
        dq, dk = grads(q_ref[here], k_ref[...], v_ref[...], g_ref[here], bias)
        dq_ref[here] = dq
        dk_ref[...] += dk
        return carry

    lax.fori_loop(0, ALL // QUERY_ROWS, block, 0)

    peers = [jnp.bitwise_xor(slot, s) for s in range(WAYS)]
    lines = [short_ref[p].astype(F32) for p in peers]
    short_q = jnp.concatenate([x[0:8] for x in lines], axis=0).astype(BF16)
    short_k = jnp.concatenate([x[8:16] for x in lines], axis=0).astype(BF16)
    short_v = jnp.concatenate([x[16:24] for x in lines], axis=0).astype(BF16)
    short_g = jnp.concatenate(
        [slots[s][3, pl.ds(112, 16)].astype(F32)[8:16] for s in range(WAYS)], axis=0
    ).astype(BF16)
    lane = lax.broadcasted_iota(jnp.int32, (1, WAYS * MOV), 1)
    position = jnp.bitwise_xor(lane // MOV, slot) * MOV + lane % MOV
    short_bias = jnp.where(position < move_len, 0.0, -1e30).astype(F32)
    short_dq, short_dk = grads(short_q, short_k, short_v, short_g, short_bias)
    short_dq = short_dq.astype(BF16).astype(F32)
    short_dk = (short_dk * SCALE).astype(BF16).astype(F32)

    dq = dq_ref[...].astype(BF16)
    dk = (dk_ref[...] * SCALE).astype(BF16)
    for s in range(WAYS):
        for n, stay, short in ((0, dq, short_dq), (1, dk, short_dk)):
            rows = stay[s * TOK_DEV : (s + 1) * TOK_DEV].astype(F32)
            rows = jnp.concatenate([rows[:RES], short[s * MOV : (s + 1) * MOV]], axis=0)
            out_ref[peers[s], n] = rows.astype(BF16)

    def total(stay, norm, short, short_norm, gain_ref):
        summed = jnp.sum(stay.astype(F32) * norm.astype(F32), axis=0, keepdims=True)
        summed += jnp.sum(short * short_norm.astype(F32), axis=0, keepdims=True)
        return summed / gain_ref[pl.ds(slot * HEADS + head, 1)]

    gain_ref[pl.ds(head, 1)] = total(dq, q_ref[...], short_dq, short_q, qg_ref)
    gain_ref[pl.ds(HEADS + head, 1)] = total(dk, k_ref[...], short_dk, short_k, kg_ref)


def attention(dest, res_len, move_len, slots, short, q_gain, k_gain):
    whole = lambda shape: pl.BlockSpec(shape, lambda b: (0,) * len(shape))
    return pl.pallas_call(
        attention_kernel,
        grid=(HEADS,),
        in_specs=[SMEM] * 3
        + [pl.BlockSpec((4, TOK_DEV, 128), lambda b: (0, 0, b))] * WAYS
        + [pl.BlockSpec((WAYS, 32, 128), lambda b: (0, 0, b))]
        + [whole((BLOCKS, 128))] * 2,
        out_specs=[
            pl.BlockSpec((WAYS, 2, TOK_DEV, 128), lambda b: (0, 0, 0, b)),
            whole((8, 128)),
        ],
        out_shape=[
            jax.ShapeDtypeStruct((WAYS, 2, TOK_DEV, LOCAL), BF16),
            jax.ShapeDtypeStruct((8, 128), F32),
        ],
        scratch_shapes=[pltpu.VMEM((ALL, 128), BF16)] * 4 + [pltpu.VMEM((ALL, 128), F32)] * 2,
        compiler_params=params(1),
        cost_estimate=pl.CostEstimate(
            flops=4_000_000_000, bytes_accessed=5_000_000, transcendentals=3_200_000
        ),
        name="attention",
    )(dest, res_len, move_len, *slots, short, q_gain, k_gain)


POST_ROWS = 32


def post_kernel(q_ref, k_ref, raw_ref, qg_ref, kg_ref, dq_ref, dk_ref, oq_ref, ok_ref):
    last = pl.program_id(0) == TOK_DEV // POST_ROWS - 1
    row = lax.broadcasted_iota(jnp.int32, (POST_ROWS, 1), 0)
    use_short = jnp.logical_and(last, row >= POST_ROWS - MOV)

    def one(in_ref, which, gain_ref, grad_ref, out_ref):
        short = raw_ref[which].astype(F32)
        short = jnp.concatenate([jnp.zeros((POST_ROWS - 16, HD), F32), short], axis=0)
        x = jnp.where(use_short, short, in_ref[...].astype(F32))
        scale = lax.rsqrt(jnp.sum(x * x, axis=1, keepdims=True) / HD + EPS)
        gain = gain_ref[...]
        grad = jnp.concatenate([grad_ref[p, 0].astype(F32) for p in range(WAYS)], axis=1) * gain
        dots = jnp.sum(x * grad, axis=1, keepdims=True)
        out_ref[...] = (scale * grad - x * ((scale * scale * scale) * dots / HD)).astype(BF16)

    one(q_ref, 0, qg_ref, dq_ref, oq_ref)
    one(k_ref, 1, kg_ref, dk_ref, ok_ref)


def finish(q_in, k_in, raw, q_gain, k_gain, back):
    rows = pl.BlockSpec((POST_ROWS, HD), lambda i: (i, 0))
    gain = pl.BlockSpec((1, HD), lambda i: (0, 0))
    return pl.pallas_call(
        post_kernel,
        grid=(TOK_DEV // POST_ROWS,),
        in_specs=[
            rows,
            rows,
            pl.BlockSpec((2, 16, HD), lambda i: (0, 0, 0)),
            gain,
            gain,
            pl.BlockSpec((WAYS, 1, POST_ROWS, LOCAL), lambda i: (0, 0, i, 0)),
            pl.BlockSpec((WAYS, 1, POST_ROWS, LOCAL), lambda i: (0, 1, i, 0)),
        ],
        out_specs=[rows, rows],
        out_shape=[jax.ShapeDtypeStruct((TOK_DEV, HD), BF16)] * 2,
        compiler_params=params(1),
        cost_estimate=pl.CostEstimate(flops=20_000_000, bytes_accessed=4_800_000, transcendentals=0),
        name="finish",
    )(q_in, k_in, raw, q_gain, k_gain, back, back)


def swap_all(x, axis):
    return lax.all_to_all(x, axis, split_axis=0, concat_axis=0, tiled=True)


def gather_sum(x, rings):
    return jnp.sum(lax.all_gather(x, "dp", axis_index_groups=rings), axis=0)


def local(
    q_in, k_in, v_in, grad_out, q_gain, k_gain,
    res_len, move_len, step_index, dest_group, loss_weight,
):
    gain_q, gain_k = q_gain.reshape(1, HD), k_gain.reshape(1, HD)
    spread = swap_all(pack_short(q_in, k_in, v_in), "dp")
    own, *outgoing = prepare(
        dest_group, res_len, move_len, step_index, loss_weight,
        q_in, k_in, v_in, grad_out, gain_q, gain_k,
    )
    arrived = [own] + [
        lax.ppermute(x, "head", [(i, i ^ (n + 1)) for i in range(WAYS)])
        for n, x in enumerate(outgoing)
    ]
    routed = swap_all(scatter_short(dest_group, spread), "dp")
    short, raw = unpack_short(routed, gain_q, gain_k)
    short = swap_all(short, "head")
    grad, part = attention(
        dest_group, res_len, move_len, arrived, short,
        q_gain.reshape(BLOCKS, 128), k_gain.reshape(BLOCKS, 128),
    )
    back = swap_all(grad, "head")
    total = gather_sum(gather_sum(part, PLANE), ZRING)
    out_q, out_k = finish(q_in, k_in, raw, gain_q, gain_k, back)
    return (
        out_q,
        out_k,
        total[:HEADS].reshape(LOCAL),
        total[HEADS : 2 * HEADS].reshape(LOCAL),
    )


def solution(mesh):
    tokens = P(("dp", "head"), None)
    return jax.shard_map(
        local,
        mesh=mesh,
        in_specs=(tokens,) * 4 + (P(),) * 7,
        out_specs=(tokens, tokens, P("head"), P("head")),
        check_vma=False,
    )
```

time: 655 us -> 194 us (0.30)
  the two profiles are of different devices: /device:TPU:1 before, /device:TPU:4 now
where the time goes in v1:
time: 194 us; the launch traced here: 193 us
  blocking collectives  86.5 us (45%)
  starting transfers between devices  45.2 us (23%)
  Pallas kernels  38.6 us (20%)
  waiting for transfers between devices  17.7 us (9%)
  local copies, waits for them, and re-layouts  3.81 us (2%)
    all_gather x2, blocking collectives, gather_sum(): return jnp.sum(lax.all_gather(x, 'dp', axis_index_groups=rings), axis=0)  48.3 us
    all_to_all x1, blocking collectives, swap_all(): return lax.all_to_all(x, axis, split_axis=0, concat_axis=0, tiled=True)  38.2 us
    ppermute x7, starting transfers between devices, local(): lax.ppermute(x, 'head', [(i, i ^ n + 1) for i in range(WAYS)])  27.7 us
    pallas_call x1, Pallas kernels, attention(): pl.pallas_call(attention_kernel, grid=(HEADS,), in_specs=[SMEM] * 3 + [pl...  21.5 us
    all_to_all x3, starting transfers between devices, swap_all(): return lax.all_to_all(x, axis, split_axis=0, concat_axis=0, tiled=True)  17.5 us
    ppermute x7, waiting for transfers between devices, local(): lax.ppermute(x, 'head', [(i, i ^ n + 1) for i in range(WAYS)])  15.9 us
    pallas_call x1, Pallas kernels, prepare(): pl.pallas_call(pre_kernel, grid=(TOK_DEV // PRE_ROWS,), in_specs=[SMEM] *...  6.9 us
    pallas_call x1, Pallas kernels, finish(): pl.pallas_call(post_kernel, grid=(TOK_DEV // POST_ROWS,), in_specs=[rows,...  4.58 us
  transfers between devices with their start and end apart: 10, of which 4 were waited for; matrix products, arithmetic and copies ran while one was open for 1% of the time, Pallas kernels for 5%

profile of v1, /device:TPU:4, one launch (start us, length us, event | category | flops | bytes accessed | tf_op | source)
XLA Modules:
  0.0 192.6 jit_solution(2655689925860940225)
XLA Ops:
  0.6 0.0 copy-start.4
  0.6 1.7 pack_short.1
  2.4 38.2 %all_to_all.20.in_ref = bf16[64,16,128]{2,1,0:T(8,128)(2,1)} all-to-all(bf16[64,16,128]{2,1,0:T(8,128)(2,1)} %pack_short.1), channel_id=1, replica_groups=mesh['dp'=64,'head'=8] {'dp'}, dimensions={0} | all-to-all | bytes 524288 | tf_op jit(solution)/shard_map/all_to_all | solution.py:336
  40.6 2.1 %scatter_short.1 = bf16[64,16,128]{2,1,0:T(8,128)(2,1)} custom-call(s32[64]{0:T(128)} %dest_ref.5, bf16[64,16,128]{2,1,0:T(8,128)(2,1)} %all_to_all.20.in_ref), custom_call_target="tpu_custom_call" | custom-call | tf_op jit(solution)/shard_map/scatter_short/pallas_call | solution.py:83
  42.6 4.9 %all-to-all-start.1 = ((bf16[64,16,128]{2,1,0:T(8,128)(2,1)}), bf16[64,16,128]{2,1,0:T(8,128)(2,1)S(1)}, u32[]{:S(2)}, u32[]{:S(2)}) async-start(bf16[64,16,128]{2,1,0:T(8,128)(2,1)} %scatter_short.1), calls=%async_computation.1 | async-start | bytes 524288 | tf_op jit(solution)/shard_map/all_to_all | solution.py:336
  47.6 0.0 copy-done.4
  47.6 0.7 copy.16.step_ref
  48.3 6.9 %prepare.1 = (bf16[4,128,384]{2,1,0:T(8,128)(2,1)}, bf16[4,128,384]{2,1,0:T(8,128)(2,1)}, bf16[4,128,384]{2,1,0:T(8,128)(2,1)}, bf16[4,128,384]{2,1,0:T(8,128)(2...) custom-call(s32[64]{0:T(128)} %dest_ref.5, ...), custom_call_target="tpu_custom_call" | custom-call | flops 20000000 | bytes 6300000 | tf_op jit(solution)/shard_map/prepare/pallas_call | solution.py:162
  55.2 3.5 %collective-permute-start = (bf16[4,128,384]{2,1,0:T(8,128)(2,1)}, bf16[4,128,384]{2,1,0:T(8,128)(2,1)S(1)}, u32[]{:S(2)}, u32[]{:S(2)}) collective-permute-start(bf16[4,128,384]{2,1,0:T(8,128)(2,1)} %get-tuple-element.20), channel_id=1, source_target_pairs={{0,1},{1,0},{2,3},{3,2},{4,5},{5,4},{6,7},{7,6},{8,9},{9,8},{10,11... | collective-permute-start | bytes 1179656 | tf_op jit(solution)/shard_map/ppermute | solution.py:354
  58.7 4.8 %collective-permute-start.1 = (bf16[4,128,384]{2,1,0:T(8,128)(2,1)}, bf16[4,128,384]{2,1,0:T(8,128)(2,1)S(1)}, u32[]{:S(2)}, u32[]{:S(2)}) collective-permute-start(bf16[4,128,384]{2,1,0:T(8,128)(2,1)} %get-tuple-element.21), channel_id=1, source_target_pairs={{0,2},{1,3},{2,0},{3,1},{4,6},{5,7},{6,4},{7,5},{8,10},{9,11},{10,... | collective-permute-start | bytes 1179656 | tf_op jit(solution)/shard_map/ppermute | solution.py:354
  63.5 2.1 %collective-permute-start.2 = (bf16[4,128,384]{2,1,0:T(8,128)(2,1)}, bf16[4,128,384]{2,1,0:T(8,128)(2,1)S(1)}, u32[]{:S(2)}, u32[]{:S(2)}) collective-permute-start(bf16[4,128,384]{2,1,0:T(8,128)(2,1)} %get-tuple-element.22), channel_id=1, source_target_pairs={{0,3},{1,2},{2,1},{3,0},{4,7},{5,6},{6,5},{7,4},{8,11},{9,10},{10,... | collective-permute-start | bytes 1179656 | tf_op jit(solution)/shard_map/ppermute | solution.py:354
  65.6 2.7 %collective-permute-start.3 = (bf16[4,128,384]{2,1,0:T(8,128)(2,1)}, bf16[4,128,384]{2,1,0:T(8,128)(2,1)S(1)}, u32[]{:S(2)}, u32[]{:S(2)}) collective-permute-start(bf16[4,128,384]{2,1,0:T(8,128)(2,1)} %get-tuple-element.23), channel_id=1, source_target_pairs={{0,4},{1,5},{2,6},{3,7},{4,0},{5,1},{6,2},{7,3},{8,12},{9,13},{10,... | collective-permute-start | bytes 1179656 | tf_op jit(solution)/shard_map/ppermute | solution.py:354
  68.3 4.5 %collective-permute-start.4 = (bf16[4,128,384]{2,1,0:T(8,128)(2,1)}, bf16[4,128,384]{2,1,0:T(8,128)(2,1)S(1)}, u32[]{:S(2)}, u32[]{:S(2)}) collective-permute-start(bf16[4,128,384]{2,1,0:T(8,128)(2,1)} %get-tuple-element.24), channel_id=1, source_target_pairs={{0,5},{1,4},{2,7},{3,6},{4,1},{5,0},{6,3},{7,2},{8,13},{9,12},{10,... | collective-permute-start | bytes 1179656 | tf_op jit(solution)/shard_map/ppermute | solution.py:354
  72.8 0.0 collective-permute-done.rest_1_
  72.8 0.0 copy-start.5
  72.8 6.3 %collective-permute-start.5 = (bf16[4,128,384]{2,1,0:T(8,128)(2,1)}, bf16[4,128,384]{2,1,0:T(8,128)(2,1)S(1)}, u32[]{:S(2)}, u32[]{:S(2)}) collective-permute-start(bf16[4,128,384]{2,1,0:T(8,128)(2,1)} %get-tuple-element.25), channel_id=1, source_target_pairs={{0,6},{1,7},{2,4},{3,5},{4,2},{5,3},{6,0},{7,1},{8,14},{9,15},{10,... | collective-permute-start | bytes 1179656 | tf_op jit(solution)/shard_map/ppermute | solution.py:354
  79.1 0.4 collective-permute-done.1.rest_2_
  79.5 0.0 copy-start.6
  79.5 3.9 %collective-permute-start.6 = (bf16[4,128,384]{2,1,0:T(8,128)(2,1)}, bf16[4,128,384]{2,1,0:T(8,128)(2,1)S(1)}, u32[]{:S(2)}, u32[]{:S(2)}) collective-permute-start(bf16[4,128,384]{2,1,0:T(8,128)(2,1)} %get-tuple-element.26), channel_id=1, source_target_pairs={{0,7},{1,6},{2,5},{3,4},{4,3},{5,2},{6,1},{7,0},{8,15},{9,14},{10,... | collective-permute-start | bytes 1179656 | tf_op jit(solution)/shard_map/ppermute | solution.py:354
  83.4 0.0 all-to-all-done.1.in_ref
  83.4 0.0 copy-start.1
  83.4 0.7 copy-done.1
  84.1 1.8 unpack_short.1
  85.9 7.3 %all-to-all-start.2 = ((bf16[8,32,384]{2,1,0:T(8,128)(2,1)}), bf16[8,32,384]{2,1,0:T(8,128)(2,1)S(1)}, u32[]{:S(2)}, u32[]{:S(2)}) async-start(bf16[8,32,384]{2,1,0:T(8,128)(2,1)} %get-tuple-element.27), calls=%async_computation.2 | async-start | bytes 393216 | tf_op jit(solution)/shard_map/all_to_all | solution.py:336
  93.2 0.0 collective-permute-done.2.rest_3_
  93.2 0.0 copy-start.7
  93.2 0.0 collective-permute-done.3.rest_4_
  93.2 0.0 copy-start.8
  93.2 0.0 collective-permute-done.4.rest_5_
  93.2 0.0 copy-start.9
  93.2 6.7 %collective-permute-done.5.rest_6_ = bf16[4,128,384]{2,1,0:T(8,128)(2,1)S(1)} collective-permute-done((bf16[4,128,384]{2,1,0:T(8,128)(2,1)}, bf16[4,128,384]{2,1,0:T(8,128)(2,1)S(1)}, u32[]{:S(2)}, u32[]{:S(2)}) %collective-permute-start.5) | collective-permute-done | bytes 393248 | tf_op jit(solution)/shard_map/ppermute | solution.py:354
  99.9 0.0 copy-start.10
  99.9 8.8 %collective-permute-done.6.rest_7_ = bf16[4,128,384]{2,1,0:T(8,128)(2,1)S(1)} collective-permute-done((bf16[4,128,384]{2,1,0:T(8,128)(2,1)}, bf16[4,128,384]{2,1,0:T(8,128)(2,1)S(1)}, u32[]{:S(2)}, u32[]{:S(2)}) %collective-permute-start.6) | collective-permute-done | bytes 393248 | tf_op jit(solution)/shard_map/ppermute | solution.py:354
  108.7 0.0 copy-start.11
  108.7 1.8 all-to-all-done.2.rest_8_
  110.4 0.0 copy-start.2
  110.4 0.0 copy-done.5
  110.4 0.0 copy-done.6
  110.4 0.0 copy-done.7
  110.4 0.0 copy-done.8
  110.5 0.0 copy-done.9
  110.5 0.0 copy-done.10
  110.5 0.0 copy-done.11
  110.5 0.6 copy-done.2
  111.1 21.5 %attention.1 = (bf16[8,2,128,384]{3,2,1,0:T(8,128)(2,1)}, f32[8,128]{1,0:T(8,128)}) custom-call(s32[64]{0:T(128)} %dest_ref.5, s32[64]{0:T(128)} %res_ref.3, s32[64]{0:T(128)} %move_ref.3, bf16[4,128,384]{2,1,0:T(8,128)(2,1)} %get-tuple-element.19.rest_0_, bf16[4,128,384]{2,1,0:T(8,128)(2,1)} %copy-done.5, bf16[4,128,384]{2,1,0:T(8,128)(2,1)} %copy-done.6, ...), custom_call_target="tpu_custom_call" | custom-call | flops 4000000000 | bytes 5000000 | tf_op jit(solution)/shard_map/attention/pallas_call | solution.py:266
  132.6 0.0 copy-start.3
  132.6 5.3 %all-to-all-start.3 = ((bf16[8,2,128,384]{3,2,1,0:T(8,128)(2,1)}), bf16[8,2,128,384]{3,2,1,0:T(8,128)(2,1)S(1)}, u32[]{:S(2)}, u32[]{:S(2)}) async-start(bf16[8,2,128,384]{3,2,1,0:T(8,128)(2,1)} %get-tuple-element.28), calls=%async_computation.3 | async-start | bytes 3145728 | tf_op jit(solution)/shard_map/all_to_all | solution.py:336
  138.0 0.0 copy-done.3
  138.0 18.7 %all-gather = f32[32,128]{1,0:T(8,128)S(1)} all-gather(f32[8,128]{1,0:T(8,128)S(1)} %copy-done.3), channel_id=2, replica_groups={{0,8,256,264},{16,24,272,280},{32,40,288,296},{48,56,304,312},{64,72,32..., dimensions={0}, use_global_device_ids=true | all-gather | bytes 20480 | tf_op jit(solution)/shard_map/all_gather | solution.py:340
  156.7 29.6 %all-gather.1 = f32[128,128]{1,0:T(8,128)S(1)} all-gather(f32[8,128]{1,0:T(8,128)S(1)} %bitcast_reduce_fusion.1), channel_id=3, replica_groups={{0,16,32,48,64,80,96,112,128,144,160,176,192,208,224,240},{8,24,40,56,7..., dimensions={0}, use_global_device_ids=true | all-gather | bytes 69632 | tf_op jit(solution)/shard_map/all_gather | solution.py:340
  186.3 0.6 slice_bitcast_fusion
  186.9 0.0 all-to-all-done.3.dq_ref.dk_ref
  186.9 0.0 copy-start
  186.9 1.2 copy-done
  188.1 4.6 %finish.1 = (bf16[128,3072]{1,0:T(8,128)(2,1)}, bf16[128,3072]{1,0:T(8,128)(2,1)}) custom-call(bf16[128,3072]{1,0:T(8,128)(2,1)} %q_ref.5, bf16[128,3072]{1,0:T(8,128)(2,1)} %k_ref.5, bf16[2,16,3072]{2,1,0:T(8,128)(2,1)} %get-tuple-element.18.raw_ref, f32[1,3072]{1,0:T(1,128)} %bitcast.15, f32[1,3072]{1,0:T(1,128)} %bitcast.19, ...), custom_call_target="tpu_custom_call" | custom-call | flops 20000000 | bytes 4800000 | tf_op jit(solution)/shard_map/finish/pallas_call | solution.py:315
  (2 shorter events, 0.0 us)
Async XLA Ops:
  0.6 46.9 %copy-start.4 = (s32[64,2]{0,1:T(2,128)S(1)}, s32[64,2]{0,1:T(2,128)}, u32[]{:S(2)}) copy-start(s32[64,2]{0,1:T(2,128)} %param.19) | copy-start | bytes 1540
  42.6 40.8 %all-to-all-start.1 = ((bf16[64,16,128]{2,1,0:T(8,128)(2,1)}), bf16[64,16,128]{2,1,0:T(8,128)(2,1)S(1)}, u32[]{:S(2)}, u32[]{:S(2)}) async-start(bf16[64,16,128]{2,1,0:T(8,128)(2,1)} %scatter_short.1), calls=%async_computation.1 | async-start | bytes 524288 | tf_op jit(solution)/shard_map/all_to_all | solution.py:336
  55.2 17.6 %collective-permute-start = (bf16[4,128,384]{2,1,0:T(8,128)(2,1)}, bf16[4,128,384]{2,1,0:T(8,128)(2,1)S(1)}, u32[]{:S(2)}, u32[]{:S(2)}) collective-permute-start(bf16[4,128,384]{2,1,0:T(8,128)(2,1)} %get-tuple-element.20), channel_id=1, source_target_pairs={{0,1},{1,0},{2,3},{3,2},{4,5},{5,4},{6,7},{7,6},{8,9},{9,8},{10,11... | collective-permute-start | bytes 1179656 | tf_op jit(solution)/shard_map/ppermute | solution.py:354
  58.7 20.8 %collective-permute-start.1 = (bf16[4,128,384]{2,1,0:T(8,128)(2,1)}, bf16[4,128,384]{2,1,0:T(8,128)(2,1)S(1)}, u32[]{:S(2)}, u32[]{:S(2)}) collective-permute-start(bf16[4,128,384]{2,1,0:T(8,128)(2,1)} %get-tuple-element.21), channel_id=1, source_target_pairs={{0,2},{1,3},{2,0},{3,1},{4,6},{5,7},{6,4},{7,5},{8,10},{9,11},{10,... | collective-permute-start | bytes 1179656 | tf_op jit(solution)/shard_map/ppermute | solution.py:354
  63.5 29.7 %collective-permute-start.2 = (bf16[4,128,384]{2,1,0:T(8,128)(2,1)}, bf16[4,128,384]{2,1,0:T(8,128)(2,1)S(1)}, u32[]{:S(2)}, u32[]{:S(2)}) collective-permute-start(bf16[4,128,384]{2,1,0:T(8,128)(2,1)} %get-tuple-element.22), channel_id=1, source_target_pairs={{0,3},{1,2},{2,1},{3,0},{4,7},{5,6},{6,5},{7,4},{8,11},{9,10},{10,... | collective-permute-start | bytes 1179656 | tf_op jit(solution)/shard_map/ppermute | solution.py:354
  65.6 27.5 %collective-permute-start.3 = (bf16[4,128,384]{2,1,0:T(8,128)(2,1)}, bf16[4,128,384]{2,1,0:T(8,128)(2,1)S(1)}, u32[]{:S(2)}, u32[]{:S(2)}) collective-permute-start(bf16[4,128,384]{2,1,0:T(8,128)(2,1)} %get-tuple-element.23), channel_id=1, source_target_pairs={{0,4},{1,5},{2,6},{3,7},{4,0},{5,1},{6,2},{7,3},{8,12},{9,13},{10,... | collective-permute-start | bytes 1179656 | tf_op jit(solution)/shard_map/ppermute | solution.py:354
  68.3 24.8 %collective-permute-start.4 = (bf16[4,128,384]{2,1,0:T(8,128)(2,1)}, bf16[4,128,384]{2,1,0:T(8,128)(2,1)S(1)}, u32[]{:S(2)}, u32[]{:S(2)}) collective-permute-start(bf16[4,128,384]{2,1,0:T(8,128)(2,1)} %get-tuple-element.24), channel_id=1, source_target_pairs={{0,5},{1,4},{2,7},{3,6},{4,1},{5,0},{6,3},{7,2},{8,13},{9,12},{10,... | collective-permute-start | bytes 1179656 | tf_op jit(solution)/shard_map/ppermute | solution.py:354
  72.8 37.6 %copy-start.5 = (bf16[4,128,384]{2,1,0:T(8,128)(2,1)}, bf16[4,128,384]{2,1,0:T(8,128)(2,1)S(1)}, u32[]{:S(2)}) copy-start(bf16[4,128,384]{2,1,0:T(8,128)(2,1)S(1)} %collective-permute-done.rest_1_) | copy-start | bytes 1179652
  72.8 27.1 %collective-permute-start.5 = (bf16[4,128,384]{2,1,0:T(8,128)(2,1)}, bf16[4,128,384]{2,1,0:T(8,128)(2,1)S(1)}, u32[]{:S(2)}, u32[]{:S(2)}) collective-permute-start(bf16[4,128,384]{2,1,0:T(8,128)(2,1)} %get-tuple-element.25), channel_id=1, source_target_pairs={{0,6},{1,7},{2,4},{3,5},{4,2},{5,3},{6,0},{7,1},{8,14},{9,15},{10,... | collective-permute-start | bytes 1179656 | tf_op jit(solution)/shard_map/ppermute | solution.py:354
  79.5 30.9 %copy-start.6 = (bf16[4,128,384]{2,1,0:T(8,128)(2,1)}, bf16[4,128,384]{2,1,0:T(8,128)(2,1)S(1)}, u32[]{:S(2)}) copy-start(bf16[4,128,384]{2,1,0:T(8,128)(2,1)S(1)} %collective-permute-done.1.rest_2_) | copy-start | bytes 1179652
  79.5 29.1 %collective-permute-start.6 = (bf16[4,128,384]{2,1,0:T(8,128)(2,1)}, bf16[4,128,384]{2,1,0:T(8,128)(2,1)S(1)}, u32[]{:S(2)}, u32[]{:S(2)}) collective-permute-start(bf16[4,128,384]{2,1,0:T(8,128)(2,1)} %get-tuple-element.26), channel_id=1, source_target_pairs={{0,7},{1,6},{2,5},{3,4},{4,3},{5,2},{6,1},{7,0},{8,15},{9,14},{10,... | collective-permute-start | bytes 1179656 | tf_op jit(solution)/shard_map/ppermute | solution.py:354
  83.4 0.7 copy-start.1
  85.9 24.5 %all-to-all-start.2 = ((bf16[8,32,384]{2,1,0:T(8,128)(2,1)}), bf16[8,32,384]{2,1,0:T(8,128)(2,1)S(1)}, u32[]{:S(2)}, u32[]{:S(2)}) async-start(bf16[8,32,384]{2,1,0:T(8,128)(2,1)} %get-tuple-element.27), calls=%async_computation.2 | async-start | bytes 393216 | tf_op jit(solution)/shard_map/all_to_all | solution.py:336
  93.2 17.3 %copy-start.7 = (bf16[4,128,384]{2,1,0:T(8,128)(2,1)}, bf16[4,128,384]{2,1,0:T(8,128)(2,1)S(1)}, u32[]{:S(2)}) copy-start(bf16[4,128,384]{2,1,0:T(8,128)(2,1)S(1)} %collective-permute-done.2.rest_3_) | copy-start | bytes 1179652
  93.2 17.3 %copy-start.8 = (bf16[4,128,384]{2,1,0:T(8,128)(2,1)}, bf16[4,128,384]{2,1,0:T(8,128)(2,1)S(1)}, u32[]{:S(2)}) copy-start(bf16[4,128,384]{2,1,0:T(8,128)(2,1)S(1)} %collective-permute-done.3.rest_4_) | copy-start | bytes 1179652
  93.2 17.3 %copy-start.9 = (bf16[4,128,384]{2,1,0:T(8,128)(2,1)}, bf16[4,128,384]{2,1,0:T(8,128)(2,1)S(1)}, u32[]{:S(2)}) copy-start(bf16[4,128,384]{2,1,0:T(8,128)(2,1)S(1)} %collective-permute-done.4.rest_5_) | copy-start | bytes 1179652
  99.9 10.6 %copy-start.10 = (bf16[4,128,384]{2,1,0:T(8,128)(2,1)}, bf16[4,128,384]{2,1,0:T(8,128)(2,1)S(1)}, u32[]{:S(2)}) copy-start(bf16[4,128,384]{2,1,0:T(8,128)(2,1)S(1)} %collective-permute-done.5.rest_6_) | copy-start | bytes 1179652
  108.7 1.8 copy-start.11
  110.4 0.7 copy-start.2
  132.6 5.4 %copy-start.3 = (f32[8,128]{1,0:T(8,128)S(1)}, f32[8,128]{1,0:T(8,128)}, u32[]{:S(2)}) copy-start(f32[8,128]{1,0:T(8,128)} %get-tuple-element.31) | copy-start | bytes 12292
  132.6 54.3 %all-to-all-start.3 = ((bf16[8,2,128,384]{3,2,1,0:T(8,128)(2,1)}), bf16[8,2,128,384]{3,2,1,0:T(8,128)(2,1)S(1)}, u32[]{:S(2)}, u32[]{:S(2)}) async-start(bf16[8,2,128,384]{3,2,1,0:T(8,128)(2,1)} %get-tuple-element.28), calls=%async_computation.3 | async-start | bytes 3145728 | tf_op jit(solution)/shard_map/all_to_all | solution.py:336
  186.9 1.2 copy-start

commit v2 on v1

--- a/solution.py
+++ b/solution.py
@@ -192,44 +192,64 @@
     return query_grad, tn(score_grad, q)
 
 
-QUERY_ROWS = 256
+QUERY_ROWS = 512
 ALL = WAYS * TOK_DEV
+ONES = 16
+POWER = SCALE * math.log2(math.e)
+
+
+def flip(block):
+    return block.astype(F32).T.astype(BF16)
 
 
 def attention_kernel(dest_ref, res_ref, move_ref, *rest):
     slots, rest = rest[:WAYS], rest[WAYS:]
-    short_ref, qg_ref, kg_ref, out_ref, gain_ref, q_ref, k_ref, v_ref, g_ref, dq_ref, dk_ref = rest
+    short_ref, qg_ref, kg_ref, out_ref, gain_ref, *rest = rest
+    q_ref, k_ref, v_ref, g_ref, qt_ref, kt_ref, vt_ref, gt_ref, dq_ref, dk_ref = rest
     head = pl.program_id(0)
     group = lax.axis_index("dp")
     slot = lax.axis_index("head")
     source = find_source(dest_ref, group)
     stay_len = res_ref[group]
     move_len = move_ref[source]
-    live_rows = lax.broadcasted_iota(jnp.int32, (TOK_DEV, 1), 0) < RES
-    lanes = lax.broadcasted_iota(jnp.int32, (1, TOK_DEV), 1)
-    biases = []
+    peers = [jnp.bitwise_xor(slot, s) for s in range(WAYS)]
+    rows = lax.broadcasted_iota(jnp.int32, (TOK_DEV, 1), 0)
+    first_lane = lax.broadcasted_iota(jnp.int32, (TOK_DEV, 128), 1) == 0
     for s in range(WAYS):
         here = pl.ds(s * TOK_DEV, TOK_DEV)
-        q_ref[here] = slots[s][0]
-        k_ref[here] = slots[s][1]
-        v_ref[here] = slots[s][2]
-        g_ref[here] = jnp.where(live_rows, slots[s][3].astype(F32), 0.0).astype(BF16)
-        peer = jnp.bitwise_xor(slot, s)
-        limit = jnp.minimum(stay_len - peer * RES, RES)
-        biases.append(jnp.where(lanes < limit, 0.0, -1e30).astype(F32))
-    bias = jnp.concatenate(biases, axis=1)
-    dk_ref[...] = jnp.zeros_like(dk_ref)
-
-    def block(i, carry):
-        here = pl.ds(pl.multiple_of(i * QUERY_ROWS, QUERY_ROWS), QUERY_ROWS)
-        dq, dk = grads(q_ref[here], k_ref[...], v_ref[...], g_ref[here], bias)
-        dq_ref[here] = dq
-        dk_ref[...] += dk
-        return carry
-
-    lax.fori_loop(0, ALL // QUERY_ROWS, block, 0)
-
-    peers = [jnp.bitwise_xor(slot, s) for s in range(WAYS)]
+        q, k, v = slots[s][0], slots[s][1], slots[s][2]
+        g = jnp.where(rows < RES, slots[s][3].astype(F32), 0.0)
+        limit = jnp.minimum(stay_len - peers[s] * RES, RES)
+        q_ref[here, 0:128] = q
+        q_ref[here, 128:256] = jnp.where(first_lane, 1.0, 0.0).astype(BF16)
+        k_ref[here, 0:128] = k
+        masked = jnp.logical_and(first_lane, rows >= limit)
+        k_ref[here, 128:256] = jnp.where(masked, -1e30, 0.0).astype(BF16)
+        v_ref[here] = v
+        g_ref[here] = g.astype(BF16)
+        qt_ref[:, here] = flip(q)
+        kt_ref[:, here] = flip(k)
+        vt_ref[0:128, here] = flip(v)
+        gt_ref[:, here] = g.T
+    ones = lax.broadcasted_iota(jnp.int32, (ONES, ALL), 0) == 0
+    vt_ref[128 : 128 + ONES, :] = jnp.where(ones, 1.0, 0.0).astype(BF16)
+
+    for i in range(ALL // QUERY_ROWS):
+        here = pl.ds(i * QUERY_ROWS, QUERY_ROWS)
+        scores = nt(k_ref[...], q_ref[here])
+        raw = jnp.exp2((scores - jnp.max(scores, axis=0, keepdims=True)) * POWER)
+        attended = jnp.dot(vt_ref[...], raw.astype(BF16), preferred_element_type=F32)
+        inverse = 1.0 / attended[128:129]
+        delta = jnp.sum(gt_ref[:, here] * attended[0:128], axis=0, keepdims=True) * inverse
+        score_grad = (raw * (nt(v_ref[...], g_ref[here]) - delta)).astype(BF16)
+        dq = jnp.dot(kt_ref[...], score_grad, preferred_element_type=F32) * (inverse * SCALE)
+        dq_ref[here] = dq.T
+        dk = nt(score_grad, (qt_ref[:, here].astype(F32) * inverse).astype(BF16))
+        if i == 0:
+            dk_ref[...] = dk
+        else:
+            dk_ref[...] += dk
+
     lines = [short_ref[p].astype(F32) for p in peers]
     short_q = jnp.concatenate([x[0:8] for x in lines], axis=0).astype(BF16)
     short_k = jnp.concatenate([x[8:16] for x in lines], axis=0).astype(BF16)
@@ -248,17 +268,17 @@
     dk = (dk_ref[...] * SCALE).astype(BF16)
     for s in range(WAYS):
         for n, stay, short in ((0, dq, short_dq), (1, dk, short_dk)):
-            rows = stay[s * TOK_DEV : (s + 1) * TOK_DEV].astype(F32)
-            rows = jnp.concatenate([rows[:RES], short[s * MOV : (s + 1) * MOV]], axis=0)
-            out_ref[peers[s], n] = rows.astype(BF16)
+            block = stay[s * TOK_DEV : (s + 1) * TOK_DEV].astype(F32)
+            block = jnp.concatenate([block[:RES], short[s * MOV : (s + 1) * MOV]], axis=0)
+            out_ref[peers[s], n] = block.astype(BF16)
 
     def total(stay, norm, short, short_norm, gain_ref):
         summed = jnp.sum(stay.astype(F32) * norm.astype(F32), axis=0, keepdims=True)
         summed += jnp.sum(short * short_norm.astype(F32), axis=0, keepdims=True)
         return summed / gain_ref[pl.ds(slot * HEADS + head, 1)]
 
-    gain_ref[pl.ds(head, 1)] = total(dq, q_ref[...], short_dq, short_q, qg_ref)
-    gain_ref[pl.ds(HEADS + head, 1)] = total(dk, k_ref[...], short_dk, short_k, kg_ref)
+    gain_ref[pl.ds(head, 1)] = total(dq, q_ref[:, 0:128], short_dq, short_q, qg_ref)
+    gain_ref[pl.ds(HEADS + head, 1)] = total(dk, k_ref[:, 0:128], short_dk, short_k, kg_ref)
 
 
 def attention(dest, res_len, move_len, slots, short, q_gain, k_gain):
@@ -278,7 +298,11 @@
             jax.ShapeDtypeStruct((WAYS, 2, TOK_DEV, LOCAL), BF16),
             jax.ShapeDtypeStruct((8, 128), F32),
         ],
-        scratch_shapes=[pltpu.VMEM((ALL, 128), BF16)] * 4 + [pltpu.VMEM((ALL, 128), F32)] * 2,
+        scratch_shapes=[pltpu.VMEM((ALL, 256), BF16)] * 2
+        + [pltpu.VMEM((ALL, 128), BF16)] * 2
+        + [pltpu.VMEM((128, ALL), BF16)] * 2
+        + [pltpu.VMEM((128 + ONES, ALL), BF16), pltpu.VMEM((128, ALL), F32)]
+        + [pltpu.VMEM((ALL, 128), F32)] * 2,
         compiler_params=params(1),
         cost_estimate=pl.CostEstimate(
             flops=4_000_000_000, bytes_accessed=5_000_000, transcendentals=3_200_000
@@ -332,6 +356,9 @@
     )(q_in, k_in, raw, q_gain, k_gain, back, back)
 
 
+AHEAD = 4
+
+
 def swap_all(x, axis):
     return lax.all_to_all(x, axis, split_axis=0, concat_axis=0, tiled=True)
 
@@ -345,15 +372,18 @@
     res_len, move_len, step_index, dest_group, loss_weight,
 ):
     gain_q, gain_k = q_gain.reshape(1, HD), k_gain.reshape(1, HD)
-    spread = swap_all(pack_short(q_in, k_in, v_in), "dp")
+    packed, grad_rows = lax.optimization_barrier((pack_short(q_in, k_in, v_in), grad_out))
+    spread = swap_all(packed, "dp")
     own, *outgoing = prepare(
         dest_group, res_len, move_len, step_index, loss_weight,
-        q_in, k_in, v_in, grad_out, gain_q, gain_k,
+        q_in, k_in, v_in, grad_rows, gain_q, gain_k,
     )
     arrived = [own] + [
         lax.ppermute(x, "head", [(i, i ^ (n + 1)) for i in range(WAYS)])
         for n, x in enumerate(outgoing)
     ]
+    held = lax.optimization_barrier((spread, *arrived[1 : 1 + AHEAD]))
+    spread, arrived[1 : 1 + AHEAD] = held[0], held[1:]
     routed = swap_all(scatter_short(dest_group, spread), "dp")
     short, raw = unpack_short(routed, gain_q, gain_k)
     short = swap_all(short, "head")
@@ -362,7 +392,7 @@
         q_gain.reshape(BLOCKS, 128), k_gain.reshape(BLOCKS, 128),
     )
     back = swap_all(grad, "head")
-    total = gather_sum(gather_sum(part, PLANE), ZRING)
+    total = gather_sum(gather_sum(part, ZRING), PLANE)
     out_q, out_k = finish(q_in, k_in, raw, gain_q, gain_k, back)
     return (
         out_q,

time: 194 us -> 177 us (0.912)
  the two profiles are of different devices: /device:TPU:4 before, /device:TPU:1 now
where the time goes in v2:
time: 177 us; the launch traced here: 176 us
  starting transfers between devices  70.3 us (40%)
  blocking collectives  35.2 us (20%)
  Pallas kernels  33.6 us (19%)
  waiting for transfers between devices  31.5 us (18%)
  local copies, waits for them, and re-layouts  4.58 us (3%)
    all_to_all x4, starting transfers between devices, swap_all(): return lax.all_to_all(x, axis, split_axis=0, concat_axis=0, tiled=True)  42.1 us
    all_gather x2, blocking collectives, gather_sum(): return jnp.sum(lax.all_gather(x, 'dp', axis_index_groups=rings), axis=0)  35.2 us
    ppermute x7, starting transfers between devices, local(): lax.ppermute(x, 'head', [(i, i ^ n + 1) for i in range(WAYS)])  28.2 us
    ppermute x7, waiting for transfers between devices, local(): lax.ppermute(x, 'head', [(i, i ^ n + 1) for i in range(WAYS)])  21.2 us
    pallas_call x1, Pallas kernels, attention(): pl.pallas_call(attention_kernel, grid=(HEADS,), in_specs=[SMEM] * 3 + [pl...  16.5 us
    all_to_all x4, waiting for transfers between devices, swap_all(): return lax.all_to_all(x, axis, split_axis=0, concat_axis=0, tiled=True)  10.3 us
    pallas_call x1, Pallas kernels, prepare(): pl.pallas_call(pre_kernel, grid=(TOK_DEV // PRE_ROWS,), in_specs=[SMEM] *...  6.9 us
    pallas_call x1, Pallas kernels, finish(): pl.pallas_call(post_kernel, grid=(TOK_DEV // POST_ROWS,), in_specs=[rows,...  4.58 us
  transfers between devices with their start and end apart: 11, of which 5 were waited for; matrix products, arithmetic and copies ran while one was open for 1% of the time, Pallas kernels for 5%

profile of v2, /device:TPU:1, one launch (start us, length us, event | category | flops | bytes accessed | tf_op | source)
XLA Modules:
  0.0 176.0 jit_solution(4230524568065989422)
XLA Ops:
  0.6 0.0 copy-start.5
  0.6 1.7 pack_short.1
  2.4 18.1 %all-to-all-start = ((bf16[64,16,128]{2,1,0:T(8,128)(2,1)}), bf16[64,16,128]{2,1,0:T(8,128)(2,1)S(1)}, u32[]{:S(2)}, u32[]{:S(2)}) async-start(bf16[64,16,128]{2,1,0:T(8,128)(2,1)} %pack_short.1), calls=%async_computation | async-start | bytes 524288 | tf_op jit(solution)/shard_map/all_to_all | solution.py:363
  20.4 0.0 copy-done.5
  20.5 0.7 copy.16.step_ref
  21.2 6.9 %prepare.1 = (bf16[4,128,384]{2,1,0:T(8,128)(2,1)}, bf16[4,128,384]{2,1,0:T(8,128)(2,1)}, bf16[4,128,384]{2,1,0:T(8,128)(2,1)}, bf16[4,128,384]{2,1,0:T(8,128)(2...) custom-call(s32[64]{0:T(128)} %dest_ref.5, ...), custom_call_target="tpu_custom_call" | custom-call | flops 20000000 | bytes 6300000 | tf_op jit(solution)/shard_map/prepare/pallas_call | solution.py:162
  28.1 3.2 %collective-permute-start = (bf16[4,128,384]{2,1,0:T(8,128)(2,1)}, bf16[4,128,384]{2,1,0:T(8,128)(2,1)S(1)}, u32[]{:S(2)}, u32[]{:S(2)}) collective-permute-start(bf16[4,128,384]{2,1,0:T(8,128)(2,1)} %get-tuple-element.27), channel_id=1, source_target_pairs={{0,1},{1,0},{2,3},{3,2},{4,5},{5,4},{6,7},{7,6},{8,9},{9,8},{10,11... | collective-permute-start | bytes 1179656 | tf_op jit(solution)/shard_map/ppermute | solution.py:382
  31.3 4.5 %collective-permute-start.1 = (bf16[4,128,384]{2,1,0:T(8,128)(2,1)}, bf16[4,128,384]{2,1,0:T(8,128)(2,1)S(1)}, u32[]{:S(2)}, u32[]{:S(2)}) collective-permute-start(bf16[4,128,384]{2,1,0:T(8,128)(2,1)} %get-tuple-element.28), channel_id=1, source_target_pairs={{0,2},{1,3},{2,0},{3,1},{4,6},{5,7},{6,4},{7,5},{8,10},{9,11},{10,... | collective-permute-start | bytes 1179656 | tf_op jit(solution)/shard_map/ppermute | solution.py:382
  35.8 1.9 %collective-permute-start.2 = (bf16[4,128,384]{2,1,0:T(8,128)(2,1)}, bf16[4,128,384]{2,1,0:T(8,128)(2,1)S(1)}, u32[]{:S(2)}, u32[]{:S(2)}) collective-permute-start(bf16[4,128,384]{2,1,0:T(8,128)(2,1)} %get-tuple-element.29), channel_id=1, source_target_pairs={{0,3},{1,2},{2,1},{3,0},{4,7},{5,6},{6,5},{7,4},{8,11},{9,10},{10,... | collective-permute-start | bytes 1179656 | tf_op jit(solution)/shard_map/ppermute | solution.py:382
  37.8 4.4 %collective-permute-start.3 = (bf16[4,128,384]{2,1,0:T(8,128)(2,1)}, bf16[4,128,384]{2,1,0:T(8,128)(2,1)S(1)}, u32[]{:S(2)}, u32[]{:S(2)}) collective-permute-start(bf16[4,128,384]{2,1,0:T(8,128)(2,1)} %get-tuple-element.30), channel_id=1, source_target_pairs={{0,4},{1,5},{2,6},{3,7},{4,0},{5,1},{6,2},{7,3},{8,12},{9,13},{10,... | collective-permute-start | bytes 1179656 | tf_op jit(solution)/shard_map/ppermute | solution.py:382
  42.1 0.0 collective-permute-done.rest_1_
  42.1 0.0 copy-start.6
  42.1 9.2 %collective-permute-done.1.rest_2_ = bf16[4,128,384]{2,1,0:T(8,128)(2,1)S(1)} collective-permute-done((bf16[4,128,384]{2,1,0:T(8,128)(2,1)}, bf16[4,128,384]{2,1,0:T(8,128)(2,1)S(1)}, u32[]{:S(2)}, u32[]{:S(2)}) %collective-permute-start.1) | collective-permute-done | bytes 393248 | tf_op jit(solution)/shard_map/ppermute | solution.py:382
  51.3 0.0 copy-start.7
  51.3 6.0 %collective-permute-done.2.rest_3_ = bf16[4,128,384]{2,1,0:T(8,128)(2,1)S(1)} collective-permute-done((bf16[4,128,384]{2,1,0:T(8,128)(2,1)}, bf16[4,128,384]{2,1,0:T(8,128)(2,1)S(1)}, u32[]{:S(2)}, u32[]{:S(2)}) %collective-permute-start.2) | collective-permute-done | bytes 393248 | tf_op jit(solution)/shard_map/ppermute | solution.py:382
  57.4 0.0 copy-start.8
  57.4 0.0 collective-permute-done.3.rest_4_
  57.4 0.0 copy-start.9
  57.4 0.0 all-to-all-done.in_ref
  57.4 0.0 copy-start.1
  57.4 0.7 copy-done.1
  58.1 2.1 %scatter_short.1 = bf16[64,16,128]{2,1,0:T(8,128)(2,1)} custom-call(s32[64]{0:T(128)} %dest_ref.5, bf16[64,16,128]{2,1,0:T(8,128)(2,1)} %copy-done.1), custom_call_target="tpu_custom_call" | custom-call | tf_op jit(solution)/shard_map/scatter_short/pallas_call | solution.py:83
  60.2 15.0 %all-to-all-start.1 = ((bf16[64,16,128]{2,1,0:T(8,128)(2,1)}), bf16[64,16,128]{2,1,0:T(8,128)(2,1)S(1)}, u32[]{:S(2)}, u32[]{:S(2)}) async-start(bf16[64,16,128]{2,1,0:T(8,128)(2,1)} %scatter_short.1), calls=%async_computation.1 | async-start | bytes 524288 | tf_op jit(solution)/shard_map/all_to_all | solution.py:363
  75.2 2.7 %collective-permute-start.4 = (bf16[4,128,384]{2,1,0:T(8,128)(2,1)}, bf16[4,128,384]{2,1,0:T(8,128)(2,1)S(1)}, u32[]{:S(2)}, u32[]{:S(2)}) collective-permute-start(bf16[4,128,384]{2,1,0:T(8,128)(2,1)} %get-tuple-element.38), channel_id=1, source_target_pairs={{0,5},{1,4},{2,7},{3,6},{4,1},{5,0},{6,3},{7,2},{8,13},{9,12},{10,... | collective-permute-start | bytes 1179656 | tf_op jit(solution)/shard_map/ppermute | solution.py:382
  77.9 4.7 %collective-permute-start.5 = (bf16[4,128,384]{2,1,0:T(8,128)(2,1)}, bf16[4,128,384]{2,1,0:T(8,128)(2,1)S(1)}, u32[]{:S(2)}, u32[]{:S(2)}) collective-permute-start(bf16[4,128,384]{2,1,0:T(8,128)(2,1)} %get-tuple-element.39), channel_id=1, source_target_pairs={{0,6},{1,7},{2,4},{3,5},{4,2},{5,3},{6,0},{7,1},{8,14},{9,15},{10,... | collective-permute-start | bytes 1179656 | tf_op jit(solution)/shard_map/ppermute | solution.py:382
  82.6 6.7 %collective-permute-start.6 = (bf16[4,128,384]{2,1,0:T(8,128)(2,1)}, bf16[4,128,384]{2,1,0:T(8,128)(2,1)S(1)}, u32[]{:S(2)}, u32[]{:S(2)}) collective-permute-start(bf16[4,128,384]{2,1,0:T(8,128)(2,1)} %get-tuple-element.40), channel_id=1, source_target_pairs={{0,7},{1,6},{2,5},{3,4},{4,3},{5,2},{6,1},{7,0},{8,15},{9,14},{10,... | collective-permute-start | bytes 1179656 | tf_op jit(solution)/shard_map/ppermute | solution.py:382
  89.4 8.1 %all-to-all-done.1.in_ref = bf16[64,16,128]{2,1,0:T(8,128)(2,1)S(1)} async-done(((bf16[64,16,128]{2,1,0:T(8,128)(2,1)}), bf16[64,16,128]{2,1,0:T(8,128)(2,1)S(1)}, u32[]{:S(2)}, u32[]{:S(2)}) %all-to-all-start.1) | async-done | bytes 262176 | tf_op jit(solution)/shard_map/all_to_all | solution.py:363
  97.5 0.0 copy-start.2
  97.5 0.7 copy-done.2
  98.2 1.8 %unpack_short.1 = (bf16[8,32,384]{2,1,0:T(8,128)(2,1)}, bf16[2,16,3072]{2,1,0:T(8,128)(2,1)}) custom-call(bf16[64,16,128]{2,1,0:T(8,128)(2,1)} %copy-done.2, f32[1,3072]{1,0:T(1,128)} %bitcast.13, f32[1,3072]{1,0:T(1,128)} %bitcast.17), custom_call_target="tpu_custom_call" | custom-call | tf_op jit(solution)/shard_map/unpack_short/pallas_call | solution.py:117
  100.0 3.7 %all-to-all-start.2 = ((bf16[8,32,384]{2,1,0:T(8,128)(2,1)}), bf16[8,32,384]{2,1,0:T(8,128)(2,1)S(1)}, u32[]{:S(2)}, u32[]{:S(2)}) async-start(bf16[8,32,384]{2,1,0:T(8,128)(2,1)} %get-tuple-element.41), calls=%async_computation.2 | async-start | bytes 393216 | tf_op jit(solution)/shard_map/all_to_all | solution.py:363
  103.7 0.0 collective-permute-done.4.rest_5_
  103.7 0.0 copy-start.10
  103.7 0.0 collective-permute-done.5.rest_6_
  103.7 0.0 copy-start.11
  103.7 5.9 %collective-permute-done.6.rest_7_ = bf16[4,128,384]{2,1,0:T(8,128)(2,1)S(1)} collective-permute-done((bf16[4,128,384]{2,1,0:T(8,128)(2,1)}, bf16[4,128,384]{2,1,0:T(8,128)(2,1)S(1)}, u32[]{:S(2)}, u32[]{:S(2)}) %collective-permute-start.6) | collective-permute-done | bytes 393248 | tf_op jit(solution)/shard_map/ppermute | solution.py:382
  109.6 0.0 copy-start.12
  109.7 2.2 %all-to-all-done.2.rest_8_ = bf16[8,32,384]{2,1,0:T(8,128)(2,1)S(1)} async-done(((bf16[8,32,384]{2,1,0:T(8,128)(2,1)}), bf16[8,32,384]{2,1,0:T(8,128)(2,1)S(1)}, u32[]{:S(2)}, u32[]{:S(2)}) %all-to-all-start.2) | async-done | bytes 196640 | tf_op jit(solution)/shard_map/all_to_all | solution.py:363
  111.9 0.0 copy-start.3
  111.9 0.0 copy-done.6
  111.9 0.0 copy-done.7
  111.9 0.0 copy-done.8
  111.9 0.0 copy-done.9
  111.9 0.0 copy-done.10
  111.9 0.0 copy-done.11
  111.9 0.0 copy-done.12
  111.9 0.6 copy-done.3
  112.6 16.5 %attention.1 = (bf16[8,2,128,384]{3,2,1,0:T(8,128)(2,1)}, f32[8,128]{1,0:T(8,128)}) custom-call(s32[64]{0:T(128)} %dest_ref.5, s32[64]{0:T(128)} %res_ref.3, s32[64]{0:T(128)} %move_ref.3, bf16[4,128,384]{2,1,0:T(8,128)(2,1)} %get-tuple-element.33.rest_0_, bf16[4,128,384]{2,1,0:T(8,128)(2,1)} %copy-done.6, bf16[4,128,384]{2,1,0:T(8,128)(2,1)} %copy-done.7, ...), custom_call_target="tpu_custom_call" | custom-call | flops 4000000000 | bytes 5000000 | tf_op jit(solution)/shard_map/attention/pallas_call | solution.py:286
  129.1 0.0 copy-start.4
  129.1 5.3 %all-to-all-start.3 = ((bf16[8,2,128,384]{3,2,1,0:T(8,128)(2,1)}), bf16[8,2,128,384]{3,2,1,0:T(8,128)(2,1)S(1)}, u32[]{:S(2)}, u32[]{:S(2)}) async-start(bf16[8,2,128,384]{3,2,1,0:T(8,128)(2,1)} %get-tuple-element.42), calls=%async_computation.3 | async-start | bytes 3145728 | tf_op jit(solution)/shard_map/all_to_all | solution.py:363
  134.4 0.0 copy-done.4
  134.4 24.0 %all-gather = f32[128,128]{1,0:T(8,128)S(1)} all-gather(f32[8,128]{1,0:T(8,128)S(1)} %copy-done.4), channel_id=2, replica_groups={{0,16,32,48,64,80,96,112,128,144,160,176,192,208,224,240},{8,24,40,56,7..., dimensions={0}, use_global_device_ids=true | all-gather | bytes 69632 | tf_op jit(solution)/shard_map/all_gather | solution.py:367
  158.4 11.2 %all-gather.1 = f32[32,128]{1,0:T(8,128)S(1)} all-gather(f32[8,128]{1,0:T(8,128)S(1)} %bitcast_reduce_fusion), channel_id=3, replica_groups={{0,8,256,264},{16,24,272,280},{32,40,288,296},{48,56,304,312},{64,72,32..., dimensions={0}, use_global_device_ids=true | all-gather | bytes 20480 | tf_op jit(solution)/shard_map/all_gather | solution.py:367
  169.6 0.6 slice_bitcast_fusion
  170.2 0.0 all-to-all-done.3.dq_ref.dk_ref
  170.2 0.0 copy-start
  170.2 1.2 copy-done
  171.4 4.6 %finish.1 = (bf16[128,3072]{1,0:T(8,128)(2,1)}, bf16[128,3072]{1,0:T(8,128)(2,1)}) custom-call(bf16[128,3072]{1,0:T(8,128)(2,1)} %q_ref.5, bf16[128,3072]{1,0:T(8,128)(2,1)} %k_ref.5, bf16[2,16,3072]{2,1,0:T(8,128)(2,1)} %get-tuple-element.32.raw_ref, f32[1,3072]{1,0:T(1,128)} %bitcast.15, f32[1,3072]{1,0:T(1,128)} %bitcast.19, ...), custom_call_target="tpu_custom_call" | custom-call | flops 20000000 | bytes 4800000 | tf_op jit(solution)/shard_map/finish/pallas_call | solution.py:339
  (2 shorter events, 0.0 us)
Async XLA Ops:
  0.6 19.8 %copy-start.5 = (s32[64,2]{0,1:T(2,128)S(1)}, s32[64,2]{0,1:T(2,128)}, u32[]{:S(2)}) copy-start(s32[64,2]{0,1:T(2,128)} %param.19) | copy-start | bytes 1540
  2.4 55.0 %all-to-all-start = ((bf16[64,16,128]{2,1,0:T(8,128)(2,1)}), bf16[64,16,128]{2,1,0:T(8,128)(2,1)S(1)}, u32[]{:S(2)}, u32[]{:S(2)}) async-start(bf16[64,16,128]{2,1,0:T(8,128)(2,1)} %pack_short.1), calls=%async_computation | async-start | bytes 524288 | tf_op jit(solution)/shard_map/all_to_all | solution.py:363
  28.1 14.1 %collective-permute-start = (bf16[4,128,384]{2,1,0:T(8,128)(2,1)}, bf16[4,128,384]{2,1,0:T(8,128)(2,1)S(1)}, u32[]{:S(2)}, u32[]{:S(2)}) collective-permute-start(bf16[4,128,384]{2,1,0:T(8,128)(2,1)} %get-tuple-element.27), channel_id=1, source_target_pairs={{0,1},{1,0},{2,3},{3,2},{4,5},{5,4},{6,7},{7,6},{8,9},{9,8},{10,11... | collective-permute-start | bytes 1179656 | tf_op jit(solution)/shard_map/ppermute | solution.py:382
  31.3 20.0 %collective-permute-start.1 = (bf16[4,128,384]{2,1,0:T(8,128)(2,1)}, bf16[4,128,384]{2,1,0:T(8,128)(2,1)S(1)}, u32[]{:S(2)}, u32[]{:S(2)}) collective-permute-start(bf16[4,128,384]{2,1,0:T(8,128)(2,1)} %get-tuple-element.28), channel_id=1, source_target_pairs={{0,2},{1,3},{2,0},{3,1},{4,6},{5,7},{6,4},{7,5},{8,10},{9,11},{10,... | collective-permute-start | bytes 1179656 | tf_op jit(solution)/shard_map/ppermute | solution.py:382
  35.8 21.6 %collective-permute-start.2 = (bf16[4,128,384]{2,1,0:T(8,128)(2,1)}, bf16[4,128,384]{2,1,0:T(8,128)(2,1)S(1)}, u32[]{:S(2)}, u32[]{:S(2)}) collective-permute-start(bf16[4,128,384]{2,1,0:T(8,128)(2,1)} %get-tuple-element.29), channel_id=1, source_target_pairs={{0,3},{1,2},{2,1},{3,0},{4,7},{5,6},{6,5},{7,4},{8,11},{9,10},{10,... | collective-permute-start | bytes 1179656 | tf_op jit(solution)/shard_map/ppermute | solution.py:382
  37.8 19.6 %collective-permute-start.3 = (bf16[4,128,384]{2,1,0:T(8,128)(2,1)}, bf16[4,128,384]{2,1,0:T(8,128)(2,1)S(1)}, u32[]{:S(2)}, u32[]{:S(2)}) collective-permute-start(bf16[4,128,384]{2,1,0:T(8,128)(2,1)} %get-tuple-element.30), channel_id=1, source_target_pairs={{0,4},{1,5},{2,6},{3,7},{4,0},{5,1},{6,2},{7,3},{8,12},{9,13},{10,... | collective-permute-start | bytes 1179656 | tf_op jit(solution)/shard_map/ppermute | solution.py:382
  42.1 69.8 %copy-start.6 = (bf16[4,128,384]{2,1,0:T(8,128)(2,1)}, bf16[4,128,384]{2,1,0:T(8,128)(2,1)S(1)}, u32[]{:S(2)}) copy-start(bf16[4,128,384]{2,1,0:T(8,128)(2,1)S(1)} %collective-permute-done.rest_1_) | copy-start | bytes 1179652
  51.3 60.6 %copy-start.7 = (bf16[4,128,384]{2,1,0:T(8,128)(2,1)}, bf16[4,128,384]{2,1,0:T(8,128)(2,1)S(1)}, u32[]{:S(2)}) copy-start(bf16[4,128,384]{2,1,0:T(8,128)(2,1)S(1)} %collective-permute-done.1.rest_2_) | copy-start | bytes 1179652
  57.4 54.5 %copy-start.8 = (bf16[4,128,384]{2,1,0:T(8,128)(2,1)}, bf16[4,128,384]{2,1,0:T(8,128)(2,1)S(1)}, u32[]{:S(2)}) copy-start(bf16[4,128,384]{2,1,0:T(8,128)(2,1)S(1)} %collective-permute-done.2.rest_3_) | copy-start | bytes 1179652
  57.4 54.5 %copy-start.9 = (bf16[4,128,384]{2,1,0:T(8,128)(2,1)}, bf16[4,128,384]{2,1,0:T(8,128)(2,1)S(1)}, u32[]{:S(2)}) copy-start(bf16[4,128,384]{2,1,0:T(8,128)(2,1)S(1)} %collective-permute-done.3.rest_4_) | copy-start | bytes 1179652
  57.4 0.7 copy-start.1
  60.2 37.3 %all-to-all-start.1 = ((bf16[64,16,128]{2,1,0:T(8,128)(2,1)}), bf16[64,16,128]{2,1,0:T(8,128)(2,1)S(1)}, u32[]{:S(2)}, u32[]{:S(2)}) async-start(bf16[64,16,128]{2,1,0:T(8,128)(2,1)} %scatter_short.1), calls=%async_computation.1 | async-start | bytes 524288 | tf_op jit(solution)/shard_map/all_to_all | solution.py:363
  75.2 28.5 %collective-permute-start.4 = (bf16[4,128,384]{2,1,0:T(8,128)(2,1)}, bf16[4,128,384]{2,1,0:T(8,128)(2,1)S(1)}, u32[]{:S(2)}, u32[]{:S(2)}) collective-permute-start(bf16[4,128,384]{2,1,0:T(8,128)(2,1)} %get-tuple-element.38), channel_id=1, source_target_pairs={{0,5},{1,4},{2,7},{3,6},{4,1},{5,0},{6,3},{7,2},{8,13},{9,12},{10,... | collective-permute-start | bytes 1179656 | tf_op jit(solution)/shard_map/ppermute | solution.py:382
  77.9 25.7 %collective-permute-start.5 = (bf16[4,128,384]{2,1,0:T(8,128)(2,1)}, bf16[4,128,384]{2,1,0:T(8,128)(2,1)S(1)}, u32[]{:S(2)}, u32[]{:S(2)}) collective-permute-start(bf16[4,128,384]{2,1,0:T(8,128)(2,1)} %get-tuple-element.39), channel_id=1, source_target_pairs={{0,6},{1,7},{2,4},{3,5},{4,2},{5,3},{6,0},{7,1},{8,14},{9,15},{10,... | collective-permute-start | bytes 1179656 | tf_op jit(solution)/shard_map/ppermute | solution.py:382
  82.6 27.0 %collective-permute-start.6 = (bf16[4,128,384]{2,1,0:T(8,128)(2,1)}, bf16[4,128,384]{2,1,0:T(8,128)(2,1)S(1)}, u32[]{:S(2)}, u32[]{:S(2)}) collective-permute-start(bf16[4,128,384]{2,1,0:T(8,128)(2,1)} %get-tuple-element.40), channel_id=1, source_target_pairs={{0,7},{1,6},{2,5},{3,4},{4,3},{5,2},{6,1},{7,0},{8,15},{9,14},{10,... | collective-permute-start | bytes 1179656 | tf_op jit(solution)/shard_map/ppermute | solution.py:382
  97.5 0.7 copy-start.2
  100.0 11.9 %all-to-all-start.2 = ((bf16[8,32,384]{2,1,0:T(8,128)(2,1)}), bf16[8,32,384]{2,1,0:T(8,128)(2,1)S(1)}, u32[]{:S(2)}, u32[]{:S(2)}) async-start(bf16[8,32,384]{2,1,0:T(8,128)(2,1)} %get-tuple-element.41), calls=%async_computation.2 | async-start | bytes 393216 | tf_op jit(solution)/shard_map/all_to_all | solution.py:363
  103.7 8.2 %copy-start.10 = (bf16[4,128,384]{2,1,0:T(8,128)(2,1)}, bf16[4,128,384]{2,1,0:T(8,128)(2,1)S(1)}, u32[]{:S(2)}) copy-start(bf16[4,128,384]{2,1,0:T(8,128)(2,1)S(1)} %collective-permute-done.4.rest_5_) | copy-start | bytes 1179652
  103.7 8.2 %copy-start.11 = (bf16[4,128,384]{2,1,0:T(8,128)(2,1)}, bf16[4,128,384]{2,1,0:T(8,128)(2,1)S(1)}, u32[]{:S(2)}) copy-start(bf16[4,128,384]{2,1,0:T(8,128)(2,1)S(1)} %collective-permute-done.5.rest_6_) | copy-start | bytes 1179652
  109.6 2.3 %copy-start.12 = (bf16[4,128,384]{2,1,0:T(8,128)(2,1)}, bf16[4,128,384]{2,1,0:T(8,128)(2,1)S(1)}, u32[]{:S(2)}) copy-start(bf16[4,128,384]{2,1,0:T(8,128)(2,1)S(1)} %collective-permute-done.6.rest_7_) | copy-start | bytes 1179652
  111.9 0.7 copy-start.3
  129.1 5.3 %copy-start.4 = (f32[8,128]{1,0:T(8,128)S(1)}, f32[8,128]{1,0:T(8,128)}, u32[]{:S(2)}) copy-start(f32[8,128]{1,0:T(8,128)} %get-tuple-element.45) | copy-start | bytes 12292
  129.1 41.1 %all-to-all-start.3 = ((bf16[8,2,128,384]{3,2,1,0:T(8,128)(2,1)}), bf16[8,2,128,384]{3,2,1,0:T(8,128)(2,1)S(1)}, u32[]{:S(2)}, u32[]{:S(2)}) async-start(bf16[8,2,128,384]{3,2,1,0:T(8,128)(2,1)} %get-tuple-element.42), calls=%async_computation.3 | async-start | bytes 3145728 | tf_op jit(solution)/shard_map/all_to_all | solution.py:363
  170.2 1.2 copy-start

commit v3 on v2

--- a/solution.py
+++ b/solution.py
@@ -130,12 +130,7 @@
 PRE_ROWS = 32
 
 
-def pre_kernel(
-    dest_ref, res_ref, move_ref, step_ref, table_ref,
-    q_ref, k_ref, v_ref, go_ref, qg_ref, kg_ref,
-    *rest,
-):
-    outs, (qn_ref, kn_ref) = rest[:WAYS], rest[WAYS:]
+def split_kernel(dest_ref, res_ref, move_ref, step_ref, table_ref, v_ref, go_ref, *outs):
     group = lax.axis_index("dp")
     slot = lax.axis_index("head")
     source = find_source(dest_ref, group)
@@ -145,31 +140,47 @@
     stay = jnp.where(slot * RES + rows < res_ref[group], stay_weight, 0.0)
     move = jnp.where(slot * MOV + rows - RES < move_ref[source], move_weight, 0.0)
     weight = jnp.where(rows < RES, stay, move)
-    qn_ref[...] = norm_rows(q_ref[...].astype(F32), qg_ref[...]).astype(BF16)
-    kn_ref[...] = norm_rows(k_ref[...].astype(F32), kg_ref[...]).astype(BF16)
     for s in range(WAYS):
         start = pl.multiple_of(jnp.bitwise_xor(slot, s) * LOCAL, 128)
         cols = pl.ds(start, LOCAL)
-        outs[s][0] = qn_ref[:, cols]
-        outs[s][1] = kn_ref[:, cols]
-        outs[s][2] = v_ref[:, cols]
-        outs[s][3] = (go_ref[:, cols].astype(F32) * weight).astype(BF16)
-
-
-def prepare(dest, res_len, move_len, steps, table, q_in, k_in, v_in, grad_out, q_gain, k_gain):
+        outs[s][0] = v_ref[:, cols]
+        outs[s][1] = (go_ref[:, cols].astype(F32) * weight).astype(BF16)
+
+
+def split_rows(dest, res_len, move_len, steps, table, v_in, grad_out):
+    rows = pl.BlockSpec((PRE_ROWS, HD), lambda i: (i, 0))
+    return pl.pallas_call(
+        split_kernel,
+        grid=(TOK_DEV // PRE_ROWS,),
+        in_specs=[SMEM] * 5 + [rows] * 2,
+        out_specs=[pl.BlockSpec((2, PRE_ROWS, LOCAL), lambda i: (0, i, 0))] * WAYS,
+        out_shape=[jax.ShapeDtypeStruct((2, TOK_DEV, LOCAL), BF16)] * WAYS,
+        compiler_params=params(1),
+        cost_estimate=pl.CostEstimate(flops=1_000_000, bytes_accessed=3_200_000, transcendentals=0),
+        name="split_rows",
+    )(dest, res_len, move_len, steps, table, v_in, grad_out)
+
+
+def norm_kernel(q_ref, k_ref, qg_ref, kg_ref, out_ref):
+    for n, (in_ref, gain_ref) in enumerate(((q_ref, qg_ref), (k_ref, kg_ref))):
+        normed = norm_rows(in_ref[...].astype(F32), gain_ref[...]).astype(BF16)
+        for p in range(WAYS):
+            out_ref[p, n] = normed[:, p * LOCAL : (p + 1) * LOCAL]
+
+
+def norm_split(q_in, k_in, q_gain, k_gain):
     rows = pl.BlockSpec((PRE_ROWS, HD), lambda i: (i, 0))
     gain = pl.BlockSpec((1, HD), lambda i: (0, 0))
     return pl.pallas_call(
-        pre_kernel,
+        norm_kernel,
         grid=(TOK_DEV // PRE_ROWS,),
-        in_specs=[SMEM] * 5 + [rows] * 4 + [gain] * 2,
-        out_specs=[pl.BlockSpec((4, PRE_ROWS, LOCAL), lambda i: (0, i, 0))] * WAYS,
-        out_shape=[jax.ShapeDtypeStruct((4, TOK_DEV, LOCAL), BF16)] * WAYS,
-        scratch_shapes=[pltpu.VMEM((PRE_ROWS, HD), BF16)] * 2,
-        compiler_params=params(1),
-        cost_estimate=pl.CostEstimate(flops=20_000_000, bytes_accessed=6_300_000, transcendentals=0),
-        name="prepare",
-    )(dest, res_len, move_len, steps, table, q_in, k_in, v_in, grad_out, q_gain, k_gain)
+        in_specs=[rows] * 2 + [gain] * 2,
+        out_specs=pl.BlockSpec((WAYS, 2, PRE_ROWS, LOCAL), lambda i: (0, 0, i, 0)),
+        out_shape=jax.ShapeDtypeStruct((WAYS, 2, TOK_DEV, LOCAL), BF16),
+        compiler_params=params(1),
+        cost_estimate=pl.CostEstimate(flops=5_000_000, bytes_accessed=3_200_000, transcendentals=0),
+        name="norm_split",
+    )(q_in, k_in, q_gain, k_gain)
 
 
 def nt(a, b):
@@ -202,23 +213,20 @@
     return block.astype(F32).T.astype(BF16)
 
 
-def attention_kernel(dest_ref, res_ref, move_ref, *rest):
+def attention_kernel(res_ref, qk_ref, *rest):
     slots, rest = rest[:WAYS], rest[WAYS:]
-    short_ref, qg_ref, kg_ref, out_ref, gain_ref, *rest = rest
+    qg_ref, kg_ref, out_ref, gain_ref, *rest = rest
     q_ref, k_ref, v_ref, g_ref, qt_ref, kt_ref, vt_ref, gt_ref, dq_ref, dk_ref = rest
     head = pl.program_id(0)
-    group = lax.axis_index("dp")
     slot = lax.axis_index("head")
-    source = find_source(dest_ref, group)
-    stay_len = res_ref[group]
-    move_len = move_ref[source]
+    stay_len = res_ref[lax.axis_index("dp")]
     peers = [jnp.bitwise_xor(slot, s) for s in range(WAYS)]
     rows = lax.broadcasted_iota(jnp.int32, (TOK_DEV, 1), 0)
     first_lane = lax.broadcasted_iota(jnp.int32, (TOK_DEV, 128), 1) == 0
     for s in range(WAYS):
         here = pl.ds(s * TOK_DEV, TOK_DEV)
-        q, k, v = slots[s][0], slots[s][1], slots[s][2]
-        g = jnp.where(rows < RES, slots[s][3].astype(F32), 0.0)
+        q, k, v = qk_ref[peers[s], 0], qk_ref[peers[s], 1], slots[s][0]
+        g = jnp.where(rows < RES, slots[s][1].astype(F32), 0.0)
         limit = jnp.minimum(stay_len - peers[s] * RES, RES)
         q_ref[here, 0:128] = q
         q_ref[here, 128:256] = jnp.where(first_lane, 1.0, 0.0).astype(BF16)
@@ -250,50 +258,33 @@
         else:
             dk_ref[...] += dk
 
-    lines = [short_ref[p].astype(F32) for p in peers]
-    short_q = jnp.concatenate([x[0:8] for x in lines], axis=0).astype(BF16)
-    short_k = jnp.concatenate([x[8:16] for x in lines], axis=0).astype(BF16)
-    short_v = jnp.concatenate([x[16:24] for x in lines], axis=0).astype(BF16)
-    short_g = jnp.concatenate(
-        [slots[s][3, pl.ds(112, 16)].astype(F32)[8:16] for s in range(WAYS)], axis=0
-    ).astype(BF16)
-    lane = lax.broadcasted_iota(jnp.int32, (1, WAYS * MOV), 1)
-    position = jnp.bitwise_xor(lane // MOV, slot) * MOV + lane % MOV
-    short_bias = jnp.where(position < move_len, 0.0, -1e30).astype(F32)
-    short_dq, short_dk = grads(short_q, short_k, short_v, short_g, short_bias)
-    short_dq = short_dq.astype(BF16).astype(F32)
-    short_dk = (short_dk * SCALE).astype(BF16).astype(F32)
-
     dq = dq_ref[...].astype(BF16)
     dk = (dk_ref[...] * SCALE).astype(BF16)
     for s in range(WAYS):
-        for n, stay, short in ((0, dq, short_dq), (1, dk, short_dk)):
-            block = stay[s * TOK_DEV : (s + 1) * TOK_DEV].astype(F32)
-            block = jnp.concatenate([block[:RES], short[s * MOV : (s + 1) * MOV]], axis=0)
-            out_ref[peers[s], n] = block.astype(BF16)
-
-    def total(stay, norm, short, short_norm, gain_ref):
-        summed = jnp.sum(stay.astype(F32) * norm.astype(F32), axis=0, keepdims=True)
-        summed += jnp.sum(short * short_norm.astype(F32), axis=0, keepdims=True)
+        out_ref[peers[s], 0] = dq[s * TOK_DEV : (s + 1) * TOK_DEV]
+        out_ref[peers[s], 1] = dk[s * TOK_DEV : (s + 1) * TOK_DEV]
+
+    def total(grad, norm, gain_ref):
+        summed = jnp.sum(grad.astype(F32) * norm.astype(F32), axis=0, keepdims=True)
         return summed / gain_ref[pl.ds(slot * HEADS + head, 1)]
 
-    gain_ref[pl.ds(head, 1)] = total(dq, q_ref[:, 0:128], short_dq, short_q, qg_ref)
-    gain_ref[pl.ds(HEADS + head, 1)] = total(dk, k_ref[:, 0:128], short_dk, short_k, kg_ref)
-
-
-def attention(dest, res_len, move_len, slots, short, q_gain, k_gain):
-    whole = lambda shape: pl.BlockSpec(shape, lambda b: (0,) * len(shape))
+    gain_ref[pl.ds(head, 1)] = total(dq, q_ref[:, 0:128], qg_ref)
+    gain_ref[pl.ds(HEADS + head, 1)] = total(dk, k_ref[:, 0:128], kg_ref)
+
+
+def whole_block(shape):
+    return pl.BlockSpec(shape, lambda b: (0,) * len(shape))
+
+
+def attention(res_len, spread, slots, q_gain, k_gain):
+    heads = pl.BlockSpec((WAYS, 2, TOK_DEV, 128), lambda b: (0, 0, 0, b))
     return pl.pallas_call(
         attention_kernel,
         grid=(HEADS,),
-        in_specs=[SMEM] * 3
-        + [pl.BlockSpec((4, TOK_DEV, 128), lambda b: (0, 0, b))] * WAYS
-        + [pl.BlockSpec((WAYS, 32, 128), lambda b: (0, 0, b))]
-        + [whole((BLOCKS, 128))] * 2,
-        out_specs=[
-            pl.BlockSpec((WAYS, 2, TOK_DEV, 128), lambda b: (0, 0, 0, b)),
-            whole((8, 128)),
-        ],
+        in_specs=[SMEM, heads]
+        + [pl.BlockSpec((2, TOK_DEV, 128), lambda b: (0, 0, b))] * WAYS
+        + [whole_block((BLOCKS, 128))] * 2,
+        out_specs=[heads, whole_block((8, 128))],
         out_shape=[
             jax.ShapeDtypeStruct((WAYS, 2, TOK_DEV, LOCAL), BF16),
             jax.ShapeDtypeStruct((8, 128), F32),
@@ -308,7 +299,69 @@
             flops=4_000_000_000, bytes_accessed=5_000_000, transcendentals=3_200_000
         ),
         name="attention",
-    )(dest, res_len, move_len, *slots, short, q_gain, k_gain)
+    )(res_len, spread, *slots, q_gain, k_gain)
+
+
+def short_kernel(dest_ref, move_ref, short_ref, *rest):
+    slots, rest = rest[:WAYS], rest[WAYS:]
+    grad_ref, part_ref, qg_ref, kg_ref, out_ref, gain_ref = rest
+    head = pl.program_id(0)
+    slot = lax.axis_index("head")
+    move_len = move_ref[find_source(dest_ref, lax.axis_index("dp"))]
+    peers = [jnp.bitwise_xor(slot, s) for s in range(WAYS)]
+    lines = [short_ref[p].astype(F32) for p in peers]
+    q = jnp.concatenate([x[0:8] for x in lines], axis=0).astype(BF16)
+    k = jnp.concatenate([x[8:16] for x in lines], axis=0).astype(BF16)
+    v = jnp.concatenate([x[16:24] for x in lines], axis=0).astype(BF16)
+    g = jnp.concatenate([x[0].astype(F32)[8:16] for x in slots], axis=0).astype(BF16)
+    lane = lax.broadcasted_iota(jnp.int32, (1, WAYS * MOV), 1)
+    position = jnp.bitwise_xor(lane // MOV, slot) * MOV + lane % MOV
+    bias = jnp.where(position < move_len, 0.0, -1e30).astype(F32)
+    dq, dk = grads(q, k, v, g, bias)
+    dq = dq.astype(BF16).astype(F32)
+    dk = (dk * SCALE).astype(BF16).astype(F32)
+    for s in range(WAYS):
+        for n, grad in ((0, dq), (1, dk)):
+            kept = grad_ref[peers[s], n].astype(F32)[0:8]
+            block = jnp.concatenate([kept, grad[s * MOV : (s + 1) * MOV]], axis=0)
+            out_ref[peers[s], n] = block.astype(BF16)
+
+    @pl.when(head == 0)
+    def _():
+        gain_ref[...] = part_ref[...]
+
+    def total(grad, norm, gain_ref):
+        summed = jnp.sum(grad * norm.astype(F32), axis=0, keepdims=True)
+        return summed / gain_ref[pl.ds(slot * HEADS + head, 1)]
+
+    gain_ref[pl.ds(head, 1)] += total(dq, q, qg_ref)
+    gain_ref[pl.ds(HEADS + head, 1)] += total(dk, k, kg_ref)
+
+
+def short_attention(dest, move_len, short, slots, grad, part, q_gain, k_gain):
+    tail = TOK_DEV // 16 - 1
+    rows = pl.BlockSpec((WAYS, 2, 16, 128), lambda b: (0, 0, tail, b))
+    return pl.pallas_call(
+        short_kernel,
+        grid=(HEADS,),
+        in_specs=[SMEM] * 2
+        + [pl.BlockSpec((WAYS, 32, 128), lambda b: (0, 0, b))]
+        + [pl.BlockSpec((1, 16, 128), lambda b: (1, tail, b))] * WAYS
+        + [rows]
+        + [whole_block((8, 128))]
+        + [whole_block((BLOCKS, 128))] * 2,
+        out_specs=[rows, whole_block((8, 128))],
+        out_shape=[
+            jax.ShapeDtypeStruct(grad.shape, BF16),
+            jax.ShapeDtypeStruct((8, 128), F32),
+        ],
+        input_output_aliases={3 + WAYS: 0},
+        compiler_params=params(1),
+        cost_estimate=pl.CostEstimate(
+            flops=20_000_000, bytes_accessed=1_000_000, transcendentals=12_000
+        ),
+        name="short_attention",
+    )(dest, move_len, short, *slots, grad, part, q_gain, k_gain)
 
 
 POST_ROWS = 32
@@ -372,24 +425,32 @@
     res_len, move_len, step_index, dest_group, loss_weight,
 ):
     gain_q, gain_k = q_gain.reshape(1, HD), k_gain.reshape(1, HD)
-    packed, grad_rows = lax.optimization_barrier((pack_short(q_in, k_in, v_in), grad_out))
-    spread = swap_all(packed, "dp")
-    own, *outgoing = prepare(
-        dest_group, res_len, move_len, step_index, loss_weight,
-        q_in, k_in, v_in, grad_rows, gain_q, gain_k,
-    )
-    arrived = [own] + [
+    own, *outgoing = split_rows(
+        dest_group, res_len, move_len, step_index, loss_weight, v_in, grad_out
+    )
+    outgoing, v_rows = lax.optimization_barrier((outgoing, v_in))
+    spread = swap_all(pack_short(q_in, k_in, v_rows), "dp")
+    slots = [own] + [
         lax.ppermute(x, "head", [(i, i ^ (n + 1)) for i in range(WAYS)])
         for n, x in enumerate(outgoing)
     ]
-    held = lax.optimization_barrier((spread, *arrived[1 : 1 + AHEAD]))
-    spread, arrived[1 : 1 + AHEAD] = held[0], held[1:]
-    routed = swap_all(scatter_short(dest_group, spread), "dp")
+    normed = norm_split(q_in, k_in, gain_q, gain_k)
+    spread, normed, slots[1 : 1 + AHEAD] = lax.optimization_barrier(
+        (spread, normed, slots[1 : 1 + AHEAD])
+    )
+    placed = scatter_short(dest_group, spread)
+    blocks = swap_all(normed, "head")
+    placed, blocks, slots[1 + AHEAD :] = lax.optimization_barrier(
+        (placed, blocks, slots[1 + AHEAD :])
+    )
+    routed = swap_all(placed, "dp")
+    gain_q_rows, gain_k_rows = q_gain.reshape(BLOCKS, 128), k_gain.reshape(BLOCKS, 128)
+    grad, part = attention(res_len, blocks, slots, gain_q_rows, gain_k_rows)
+    routed, part = lax.optimization_barrier((routed, part))
     short, raw = unpack_short(routed, gain_q, gain_k)
     short = swap_all(short, "head")
-    grad, part = attention(
-        dest_group, res_len, move_len, arrived, short,
-        q_gain.reshape(BLOCKS, 128), k_gain.reshape(BLOCKS, 128),
+    grad, part = short_attention(
+        dest_group, move_len, short, slots, grad, part, gain_q_rows, gain_k_rows
     )
     back = swap_all(grad, "head")
     total = gather_sum(gather_sum(part, ZRING), PLANE)

time: 177 us -> 190 us (1.073)
  blocking collectives: 35.2 us -> 45.2 us
  Pallas kernels: 33.6 us -> 39.1 us
  starting transfers between devices: 70.3 us -> 66.3 us
    all_to_all x0 -> x1, blocking collectives: none -> 12.1 us  [swap_all(): return lax.all_to_all(x, axis, split_axis=0, concat_axis=0, tiled=True)]
    pallas_call x2 -> x4, Pallas kernels: 23.4 us -> 28.9 us  [the longest x1 13.2 us: attention(): pl.pallas_call(attention_kernel, grid=(HEADS,), in_specs=[SMEM, heads] +...]
    all_to_all x4, starting transfers between devices: 42.1 us -> 37.6 us  [swap_all(): return lax.all_to_all(x, axis, split_axis=0, concat_axis=0, tiled=True)]
    all_gather x2, blocking collectives: 35.2 us -> 33.1 us  [gather_sum(): return jnp.sum(lax.all_gather(x, 'dp', axis_index_groups=rings), axis=0)]
    unnamed x27 -> x39, local copies, waits for them, and re-layouts: 3.99 us -> 4.01 us
  transfers between devices with their start and end apart: 11 -> 11, of which waited for: 5 -> 6; matrix products, arithmetic and copies ran while one was open for 1% -> 0% of each run, Pallas kernels for 5% -> 10%
where the time goes in v3:
time: 190 us; the launch traced here: 188 us
  starting transfers between devices  66.3 us (35%)
  blocking collectives  45.2 us (24%)
  Pallas kernels  39.1 us (21%)
  waiting for transfers between devices  32.4 us (17%)
  local copies, waits for them, and re-layouts  4.6 us (2%)
    all_to_all x4, starting transfers between devices, swap_all(): return lax.all_to_all(x, axis, split_axis=0, concat_axis=0, tiled=True)  37.6 us
    all_gather x2, blocking collectives, gather_sum(): return jnp.sum(lax.all_gather(x, 'dp', axis_index_groups=rings), axis=0)  33.1 us
    ppermute x7, starting transfers between devices, local(): lax.ppermute(x, 'head', [(i, i ^ n + 1) for i in range(WAYS)])  28.7 us
    ppermute x7, waiting for transfers between devices, local(): lax.ppermute(x, 'head', [(i, i ^ n + 1) for i in range(WAYS)])  20.7 us
    pallas_call x1, Pallas kernels, attention(): pl.pallas_call(attention_kernel, grid=(HEADS,), in_specs=[SMEM, heads] +...  13.2 us
    all_to_all x1, blocking collectives, swap_all(): return lax.all_to_all(x, axis, split_axis=0, concat_axis=0, tiled=True)  12.1 us
    all_to_all x4, waiting for transfers between devices, swap_all(): return lax.all_to_all(x, axis, split_axis=0, concat_axis=0, tiled=True)  11.6 us
    pallas_call x1, Pallas kernels, short_attention(): pl.pallas_call(short_kernel, grid=(HEADS,), in_specs=[SMEM] * 2 + [pl.Blo...  5.88 us
  transfers between devices with their start and end apart: 11, of which 6 were waited for; matrix products, arithmetic and copies ran while one was open for 0% of the time, Pallas kernels for 10%

profile of v3, /device:TPU:1, one launch (start us, length us, event | category | flops | bytes accessed | tf_op | source)
XLA Modules:
  0.0 188.4 jit_solution(6720726772246062795)
XLA Ops:
  0.6 1.4 copy.17.step_ref
  2.0 5.7 %split_rows.1 = (bf16[2,128,384]{2,1,0:T(8,128)(2,1)}, bf16[2,128,384]{2,1,0:T(8,128)(2,1)}, bf16[2,128,384]{2,1,0:T(8,128)(2,1)}, bf16[2,128,384]{2,1,0:T(8,128...) custom-call(s32[64]{0:T(128)} %dest_ref.5, ...), custom_call_target="tpu_custom_call" | custom-call | flops 1000000 | bytes 3200000 | tf_op jit(solution)/shard_map/split_rows/pallas_call | solution.py:152
  7.7 0.0 copy-start.18
  7.8 0.0 copy-start.17
  7.8 0.0 copy-start.16
  7.8 0.0 copy-start.15
  7.8 1.8 pack_short.1
  9.6 18.1 %all-to-all-start = ((bf16[64,16,128]{2,1,0:T(8,128)(2,1)}), bf16[64,16,128]{2,1,0:T(8,128)(2,1)S(1)}, u32[]{:S(2)}, u32[]{:S(2)}) async-start(bf16[64,16,128]{2,1,0:T(8,128)(2,1)} %pack_short.1), calls=%async_computation | async-start | bytes 524288 | tf_op jit(solution)/shard_map/all_to_all | solution.py:416
  27.7 0.0 copy-done.18
  27.7 3.2 %collective-permute-start = (bf16[2,128,384]{2,1,0:T(8,128)(2,1)S(1)}, bf16[2,128,384]{2,1,0:T(8,128)(2,1)S(1)}, u32[]{:S(2)}, u32[]{:S(2)}) collective-permute-start(bf16[2,128,384]{2,1,0:T(8,128)(2,1)S(1)} %copy-done.18), channel_id=1, source_target_pairs={{0,1},{1,0},{2,3},{3,2},{4,5},{5,4},{6,7},{7,6},{8,9},{9,8},{10,11... | collective-permute-start | bytes 589832 | tf_op jit(solution)/shard_map/ppermute | solution.py:434
  30.9 0.0 copy-done.17
  30.9 4.5 %collective-permute-start.1 = (bf16[2,128,384]{2,1,0:T(8,128)(2,1)S(1)}, bf16[2,128,384]{2,1,0:T(8,128)(2,1)S(1)}, u32[]{:S(2)}, u32[]{:S(2)}) collective-permute-start(bf16[2,128,384]{2,1,0:T(8,128)(2,1)S(1)} %copy-done.17), channel_id=1, source_target_pairs={{0,2},{1,3},{2,0},{3,1},{4,6},{5,7},{6,4},{7,5},{8,10},{9,11},{10,... | collective-permute-start | bytes 589832 | tf_op jit(solution)/shard_map/ppermute | solution.py:434
  35.4 0.0 copy-done.16
  35.4 1.9 %collective-permute-start.2 = (bf16[2,128,384]{2,1,0:T(8,128)(2,1)S(1)}, bf16[2,128,384]{2,1,0:T(8,128)(2,1)S(1)}, u32[]{:S(2)}, u32[]{:S(2)}) collective-permute-start(bf16[2,128,384]{2,1,0:T(8,128)(2,1)S(1)} %copy-done.16), channel_id=1, source_target_pairs={{0,3},{1,2},{2,1},{3,0},{4,7},{5,6},{6,5},{7,4},{8,11},{9,10},{10,... | collective-permute-start | bytes 589832 | tf_op jit(solution)/shard_map/ppermute | solution.py:434
  37.4 0.0 copy-done.15
  37.4 4.4 %collective-permute-start.3 = (bf16[2,128,384]{2,1,0:T(8,128)(2,1)S(1)}, bf16[2,128,384]{2,1,0:T(8,128)(2,1)S(1)}, u32[]{:S(2)}, u32[]{:S(2)}) collective-permute-start(bf16[2,128,384]{2,1,0:T(8,128)(2,1)S(1)} %copy-done.15), channel_id=1, source_target_pairs={{0,4},{1,5},{2,6},{3,7},{4,0},{5,1},{6,2},{7,3},{8,12},{9,13},{10,... | collective-permute-start | bytes 589832 | tf_op jit(solution)/shard_map/ppermute | solution.py:434
  41.8 4.0 %norm_split.1 = bf16[8,2,128,384]{3,2,1,0:T(8,128)(2,1)} custom-call(bf16[128,3072]{1,0:T(8,128)(2,1)} %q_ref.5, bf16[128,3072]{1,0:T(8,128)(2,1)} %k_ref.5, f32[1,3072]{1,0:T(1,128)} %bitcast.12, f32[1,3072]{1,0:T(1,128)} %bitcast.17), custom_call_target="tpu_custom_call" | custom-call | flops 5000000 | bytes 3200000 | tf_op jit(solution)/shard_map/norm_split/pallas_call | solution.py:174
  45.8 0.0 copy-start.14
  45.8 0.0 copy-start.13
  45.8 0.0 copy-start.12
  45.8 0.0 collective-permute-done.rest_1_
  45.8 0.0 copy-start.4
  45.8 0.0 collective-permute-done.1.rest_2_
  45.8 0.0 copy-start.5
  45.9 1.4 collective-permute-done.2.rest_3_
  47.3 0.0 collective-permute-done.3.rest_4_
  47.3 2.6 %all-to-all-done.in_ref = bf16[64,16,128]{2,1,0:T(8,128)(2,1)S(1)} async-done(((bf16[64,16,128]{2,1,0:T(8,128)(2,1)}), bf16[64,16,128]{2,1,0:T(8,128)(2,1)S(1)}, u32[]{:S(2)}, u32[]{:S(2)}) %all-to-all-start) | async-done | bytes 262176 | tf_op jit(solution)/shard_map/all_to_all | solution.py:416
  49.9 0.0 copy-done.4
  49.9 0.0 copy-done.5
  49.9 0.0 copy-done.6
  49.9 0.0 copy-done.7
  49.9 0.7 copy-done.2
  50.6 6.4 %all-to-all-start.1 = ((bf16[8,2,128,384]{3,2,1,0:T(8,128)(2,1)}), bf16[8,2,128,384]{3,2,1,0:T(8,128)(2,1)S(1)}, u32[]{:S(2)}, u32[]{:S(2)}) async-start(bf16[8,2,128,384]{3,2,1,0:T(8,128)(2,1)} %norm_split.1), calls=%async_computation.1 | async-start | bytes 3145728 | tf_op jit(solution)/shard_map/all_to_all | solution.py:416
  57.0 0.0 copy-done.14
  57.0 5.8 %collective-permute-start.4 = (bf16[2,128,384]{2,1,0:T(8,128)(2,1)S(1)}, bf16[2,128,384]{2,1,0:T(8,128)(2,1)S(1)}, u32[]{:S(2)}, u32[]{:S(2)}) collective-permute-start(bf16[2,128,384]{2,1,0:T(8,128)(2,1)S(1)} %copy-done.14), channel_id=1, source_target_pairs={{0,5},{1,4},{2,7},{3,6},{4,1},{5,0},{6,3},{7,2},{8,13},{9,12},{10,... | collective-permute-start | bytes 589832 | tf_op jit(solution)/shard_map/ppermute | solution.py:434
  62.7 0.0 copy-done.13
  62.8 4.3 %collective-permute-start.5 = (bf16[2,128,384]{2,1,0:T(8,128)(2,1)S(1)}, bf16[2,128,384]{2,1,0:T(8,128)(2,1)S(1)}, u32[]{:S(2)}, u32[]{:S(2)}) collective-permute-start(bf16[2,128,384]{2,1,0:T(8,128)(2,1)S(1)} %copy-done.13), channel_id=1, source_target_pairs={{0,6},{1,7},{2,4},{3,5},{4,2},{5,3},{6,0},{7,1},{8,14},{9,15},{10,... | collective-permute-start | bytes 589832 | tf_op jit(solution)/shard_map/ppermute | solution.py:434
  67.1 0.0 copy-done.12
  67.1 4.6 %collective-permute-start.6 = (bf16[2,128,384]{2,1,0:T(8,128)(2,1)S(1)}, bf16[2,128,384]{2,1,0:T(8,128)(2,1)S(1)}, u32[]{:S(2)}, u32[]{:S(2)}) collective-permute-start(bf16[2,128,384]{2,1,0:T(8,128)(2,1)S(1)} %copy-done.12), channel_id=1, source_target_pairs={{0,7},{1,6},{2,5},{3,4},{4,3},{5,2},{6,1},{7,0},{8,15},{9,14},{10,... | collective-permute-start | bytes 589832 | tf_op jit(solution)/shard_map/ppermute | solution.py:434
  71.7 2.1 %scatter_short.1 = bf16[64,16,128]{2,1,0:T(8,128)(2,1)} custom-call(s32[64]{0:T(128)} %dest_ref.5, bf16[64,16,128]{2,1,0:T(8,128)(2,1)} %copy-done.2), custom_call_target="tpu_custom_call" | custom-call | tf_op jit(solution)/shard_map/scatter_short/pallas_call | solution.py:83
  73.7 9.4 %collective-permute-done.4.rest_5_ = bf16[2,128,384]{2,1,0:T(8,128)(2,1)S(1)} collective-permute-done((bf16[2,128,384]{2,1,0:T(8,128)(2,1)S(1)}, bf16[2,128,384]{2,1,0:T(8,128)(2,1)S(1)}, u32[]{:S(2)}, u32[]{:S(2)}) %collective-permute-start.4) | collective-permute-done | bytes 196640 | tf_op jit(solution)/shard_map/ppermute | solution.py:434
  83.1 5.7 %collective-permute-done.5.rest_6_ = bf16[2,128,384]{2,1,0:T(8,128)(2,1)S(1)} collective-permute-done((bf16[2,128,384]{2,1,0:T(8,128)(2,1)S(1)}, bf16[2,128,384]{2,1,0:T(8,128)(2,1)S(1)}, u32[]{:S(2)}, u32[]{:S(2)}) %collective-permute-start.5) | collective-permute-done | bytes 196640 | tf_op jit(solution)/shard_map/ppermute | solution.py:434
  88.8 4.3 %collective-permute-done.6.rest_7_ = bf16[2,128,384]{2,1,0:T(8,128)(2,1)S(1)} collective-permute-done((bf16[2,128,384]{2,1,0:T(8,128)(2,1)S(1)}, bf16[2,128,384]{2,1,0:T(8,128)(2,1)S(1)}, u32[]{:S(2)}, u32[]{:S(2)}) %collective-permute-start.6) | collective-permute-done | bytes 196640 | tf_op jit(solution)/shard_map/ppermute | solution.py:434
  93.0 0.0 all-to-all-done.1.qk_ref
  93.0 9.6 %all-to-all-start.2 = ((bf16[64,16,128]{2,1,0:T(8,128)(2,1)}), bf16[64,16,128]{2,1,0:T(8,128)(2,1)S(1)}, u32[]{:S(2)}, u32[]{:S(2)}) async-start(bf16[64,16,128]{2,1,0:T(8,128)(2,1)} %scatter_short.1), calls=%async_computation.2 | async-start | bytes 524288 | tf_op jit(solution)/shard_map/all_to_all | solution.py:416
  102.7 0.0 copy-done.8
  102.7 0.0 copy-done.9
  102.7 0.0 copy-done.10
  102.7 0.0 copy-done.1
  102.7 13.2 %attention.1 = (bf16[8,2,128,384]{3,2,1,0:T(8,128)(2,1)}, f32[8,128]{1,0:T(8,128)}) custom-call(s32[64]{0:T(128)} %res_ref.3, bf16[8,2,128,384]{3,2,1,0:T(8,128)(2,1)} %copy-done.1, bf16[2,128,384]{2,1,0:T(8,128)(2,1)} %get-tuple-element.60.rest_0_, bf16[2,128,384]{2,1,0:T(8,128)(2,1)} %copy-done.4, bf16[2,128,384]{2,1,0:T(8,128)(2,1)} %copy-done.5, ...), custom_call_target="tpu_custom_call" | custom-call | flops 4000000000 | bytes 5000000 | tf_op jit(solution)/shard_map/attention/pallas_call | solution.py:281
  115.9 9.0 %all-to-all-done.2.in_ref = bf16[64,16,128]{2,1,0:T(8,128)(2,1)S(1)} async-done(((bf16[64,16,128]{2,1,0:T(8,128)(2,1)}), bf16[64,16,128]{2,1,0:T(8,128)(2,1)S(1)}, u32[]{:S(2)}, u32[]{:S(2)}) %all-to-all-start.2) | async-done | bytes 262176 | tf_op jit(solution)/shard_map/all_to_all | solution.py:416
  124.9 0.7 copy-done.3
  125.6 1.8 unpack_short.1
  127.4 12.1 %all_to_all.25.short_ref = bf16[8,32,384]{2,1,0:T(8,128)(2,1)} all-to-all(bf16[8,32,384]{2,1,0:T(8,128)(2,1)} %get-tuple-element.71), channel_id=1, replica_groups=mesh['dp'=64,'head'=8] {'head'}, dimensions={0} | all-to-all | bytes 393216 | tf_op jit(solution)/shard_map/all_to_all | solution.py:416
  139.5 5.9 %short_attention.1 = (bf16[8,2,128,384]{3,2,1,0:T(8,128)(2,1)}, f32[8,128]{1,0:T(8,128)}) custom-call(s32[64]{0:T(128)} %dest_ref.5, s32[64]{0:T(128)} %move_ref.3, bf16[8,32,384]{2,1,0:T(8,128)(2,1)} %all_to_all.25.short_ref, bf16[2,128,384]{2,1,0:T(8,128)(2,1)} %get-tuple-element.60.rest_0_, ...), custom_call_target="tpu_custom_call", output_to_operand_aliasing={{0}: (11, {})} | custom-call | flops 20000000 | bytes 1000000 | tf_op jit(solution)/shard_map/short_attention/pallas_call | solution.py:344
  145.3 0.0 copy-start.11
  145.4 3.6 %all-to-all-start.4 = ((bf16[8,2,128,384]{3,2,1,0:T(8,128)(2,1)}), bf16[8,2,128,384]{3,2,1,0:T(8,128)(2,1)S(1)}, u32[]{:S(2)}, u32[]{:S(2)}) async-start(bf16[8,2,128,384]{3,2,1,0:T(8,128)(2,1)} %get-tuple-element.74), calls=%async_computation.4 | async-start | bytes 3145728 | tf_op jit(solution)/shard_map/all_to_all | solution.py:416
  149.0 0.0 copy-done.11
  149.0 21.3 %all-gather = f32[128,128]{1,0:T(8,128)S(1)} all-gather(f32[8,128]{1,0:T(8,128)S(1)} %copy-done.11), channel_id=2, replica_groups={{0,16,32,48,64,80,96,112,128,144,160,176,192,208,224,240},{8,24,40,56,7..., dimensions={0}, use_global_device_ids=true | all-gather | bytes 69632 | tf_op jit(solution)/shard_map/all_gather | solution.py:420
  170.3 11.8 %all-gather.1 = f32[32,128]{1,0:T(8,128)S(1)} all-gather(f32[8,128]{1,0:T(8,128)S(1)} %bitcast_reduce_fusion), channel_id=3, replica_groups={{0,8,256,264},{16,24,272,280},{32,40,288,296},{48,56,304,312},{64,72,32..., dimensions={0}, use_global_device_ids=true | all-gather | bytes 20480 | tf_op jit(solution)/shard_map/all_gather | solution.py:420
  182.1 0.6 slice_bitcast_fusion
  182.7 0.0 all-to-all-done.4.dq_ref.dk_ref
  182.7 1.2 copy-done
  183.9 4.6 %finish.1 = (bf16[128,3072]{1,0:T(8,128)(2,1)}, bf16[128,3072]{1,0:T(8,128)(2,1)}) custom-call(bf16[128,3072]{1,0:T(8,128)(2,1)} %q_ref.5, bf16[128,3072]{1,0:T(8,128)(2,1)} %k_ref.5, bf16[2,16,3072]{2,1,0:T(8,128)(2,1)} %get-tuple-element.70.raw_ref, f32[1,3072]{1,0:T(1,128)} %bitcast.16, f32[1,3072]{1,0:T(1,128)} %bitcast.21, ...), custom_call_target="tpu_custom_call" | custom-call | flops 20000000 | bytes 4800000 | tf_op jit(solution)/shard_map/finish/pallas_call | solution.py:392
  (11 shorter events, 0.0 us)
Async XLA Ops:
  7.7 19.9 %copy-start.18 = (bf16[2,128,384]{2,1,0:T(8,128)(2,1)S(1)}, bf16[2,128,384]{2,1,0:T(8,128)(2,1)}, u32[]{:S(2)}) copy-start(bf16[2,128,384]{2,1,0:T(8,128)(2,1)} %get-tuple-element.49) | copy-start | bytes 589828
  7.8 23.1 %copy-start.17 = (bf16[2,128,384]{2,1,0:T(8,128)(2,1)S(1)}, bf16[2,128,384]{2,1,0:T(8,128)(2,1)}, u32[]{:S(2)}) copy-start(bf16[2,128,384]{2,1,0:T(8,128)(2,1)} %get-tuple-element.50) | copy-start | bytes 589828
  7.8 27.7 %copy-start.16 = (bf16[2,128,384]{2,1,0:T(8,128)(2,1)S(1)}, bf16[2,128,384]{2,1,0:T(8,128)(2,1)}, u32[]{:S(2)}) copy-start(bf16[2,128,384]{2,1,0:T(8,128)(2,1)} %get-tuple-element.51) | copy-start | bytes 589828
  7.8 29.6 %copy-start.15 = (bf16[2,128,384]{2,1,0:T(8,128)(2,1)S(1)}, bf16[2,128,384]{2,1,0:T(8,128)(2,1)}, u32[]{:S(2)}) copy-start(bf16[2,128,384]{2,1,0:T(8,128)(2,1)} %get-tuple-element.52) | copy-start | bytes 589828
  9.6 40.3 %all-to-all-start = ((bf16[64,16,128]{2,1,0:T(8,128)(2,1)}), bf16[64,16,128]{2,1,0:T(8,128)(2,1)S(1)}, u32[]{:S(2)}, u32[]{:S(2)}) async-start(bf16[64,16,128]{2,1,0:T(8,128)(2,1)} %pack_short.1), calls=%async_computation | async-start | bytes 524288 | tf_op jit(solution)/shard_map/all_to_all | solution.py:416
  27.7 18.1 %collective-permute-start = (bf16[2,128,384]{2,1,0:T(8,128)(2,1)S(1)}, bf16[2,128,384]{2,1,0:T(8,128)(2,1)S(1)}, u32[]{:S(2)}, u32[]{:S(2)}) collective-permute-start(bf16[2,128,384]{2,1,0:T(8,128)(2,1)S(1)} %copy-done.18), channel_id=1, source_target_pairs={{0,1},{1,0},{2,3},{3,2},{4,5},{5,4},{6,7},{7,6},{8,9},{9,8},{10,11... | collective-permute-start | bytes 589832 | tf_op jit(solution)/shard_map/ppermute | solution.py:434
  30.9 14.9 %collective-permute-start.1 = (bf16[2,128,384]{2,1,0:T(8,128)(2,1)S(1)}, bf16[2,128,384]{2,1,0:T(8,128)(2,1)S(1)}, u32[]{:S(2)}, u32[]{:S(2)}) collective-permute-start(bf16[2,128,384]{2,1,0:T(8,128)(2,1)S(1)} %copy-done.17), channel_id=1, source_target_pairs={{0,2},{1,3},{2,0},{3,1},{4,6},{5,7},{6,4},{7,5},{8,10},{9,11},{10,... | collective-permute-start | bytes 589832 | tf_op jit(solution)/shard_map/ppermute | solution.py:434
  35.4 11.8 %collective-permute-start.2 = (bf16[2,128,384]{2,1,0:T(8,128)(2,1)S(1)}, bf16[2,128,384]{2,1,0:T(8,128)(2,1)S(1)}, u32[]{:S(2)}, u32[]{:S(2)}) collective-permute-start(bf16[2,128,384]{2,1,0:T(8,128)(2,1)S(1)} %copy-done.16), channel_id=1, source_target_pairs={{0,3},{1,2},{2,1},{3,0},{4,7},{5,6},{6,5},{7,4},{8,11},{9,10},{10,... | collective-permute-start | bytes 589832 | tf_op jit(solution)/shard_map/ppermute | solution.py:434
  37.4 9.9 %collective-permute-start.3 = (bf16[2,128,384]{2,1,0:T(8,128)(2,1)S(1)}, bf16[2,128,384]{2,1,0:T(8,128)(2,1)S(1)}, u32[]{:S(2)}, u32[]{:S(2)}) collective-permute-start(bf16[2,128,384]{2,1,0:T(8,128)(2,1)S(1)} %copy-done.15), channel_id=1, source_target_pairs={{0,4},{1,5},{2,6},{3,7},{4,0},{5,1},{6,2},{7,3},{8,12},{9,13},{10,... | collective-permute-start | bytes 589832 | tf_op jit(solution)/shard_map/ppermute | solution.py:434
  45.8 11.2 %copy-start.14 = (bf16[2,128,384]{2,1,0:T(8,128)(2,1)S(1)}, bf16[2,128,384]{2,1,0:T(8,128)(2,1)}, u32[]{:S(2)}) copy-start(bf16[2,128,384]{2,1,0:T(8,128)(2,1)} %get-tuple-element.55) | copy-start | bytes 589828
  45.8 16.9 %copy-start.13 = (bf16[2,128,384]{2,1,0:T(8,128)(2,1)S(1)}, bf16[2,128,384]{2,1,0:T(8,128)(2,1)}, u32[]{:S(2)}) copy-start(bf16[2,128,384]{2,1,0:T(8,128)(2,1)} %get-tuple-element.56) | copy-start | bytes 589828
  45.8 21.3 %copy-start.12 = (bf16[2,128,384]{2,1,0:T(8,128)(2,1)S(1)}, bf16[2,128,384]{2,1,0:T(8,128)(2,1)}, u32[]{:S(2)}) copy-start(bf16[2,128,384]{2,1,0:T(8,128)(2,1)} %get-tuple-element.57) | copy-start | bytes 589828
  45.8 4.1 %copy-start.4 = (bf16[2,128,384]{2,1,0:T(8,128)(2,1)}, bf16[2,128,384]{2,1,0:T(8,128)(2,1)S(1)}, u32[]{:S(2)}) copy-start(bf16[2,128,384]{2,1,0:T(8,128)(2,1)S(1)} %collective-permute-done.rest_1_) | copy-start | bytes 589828
  45.8 4.1 %copy-start.5 = (bf16[2,128,384]{2,1,0:T(8,128)(2,1)}, bf16[2,128,384]{2,1,0:T(8,128)(2,1)S(1)}, u32[]{:S(2)}) copy-start(bf16[2,128,384]{2,1,0:T(8,128)(2,1)S(1)} %collective-permute-done.1.rest_2_) | copy-start | bytes 589828
  47.3 2.7 %copy-start.6 = (bf16[2,128,384]{2,1,0:T(8,128)(2,1)}, bf16[2,128,384]{2,1,0:T(8,128)(2,1)S(1)}, u32[]{:S(2)}) copy-start(bf16[2,128,384]{2,1,0:T(8,128)(2,1)S(1)} %collective-permute-done.2.rest_3_) | copy-start | bytes 589828
  47.3 2.7 %copy-start.7 = (bf16[2,128,384]{2,1,0:T(8,128)(2,1)}, bf16[2,128,384]{2,1,0:T(8,128)(2,1)S(1)}, u32[]{:S(2)}) copy-start(bf16[2,128,384]{2,1,0:T(8,128)(2,1)S(1)} %collective-permute-done.3.rest_4_) | copy-start | bytes 589828
  49.9 0.7 copy-start.2
  50.6 42.4 %all-to-all-start.1 = ((bf16[8,2,128,384]{3,2,1,0:T(8,128)(2,1)}), bf16[8,2,128,384]{3,2,1,0:T(8,128)(2,1)S(1)}, u32[]{:S(2)}, u32[]{:S(2)}) async-start(bf16[8,2,128,384]{3,2,1,0:T(8,128)(2,1)} %norm_split.1), calls=%async_computation.1 | async-start | bytes 3145728 | tf_op jit(solution)/shard_map/all_to_all | solution.py:416
  57.0 26.1 %collective-permute-start.4 = (bf16[2,128,384]{2,1,0:T(8,128)(2,1)S(1)}, bf16[2,128,384]{2,1,0:T(8,128)(2,1)S(1)}, u32[]{:S(2)}, u32[]{:S(2)}) collective-permute-start(bf16[2,128,384]{2,1,0:T(8,128)(2,1)S(1)} %copy-done.14), channel_id=1, source_target_pairs={{0,5},{1,4},{2,7},{3,6},{4,1},{5,0},{6,3},{7,2},{8,13},{9,12},{10,... | collective-permute-start | bytes 589832 | tf_op jit(solution)/shard_map/ppermute | solution.py:434
  62.8 26.0 %collective-permute-start.5 = (bf16[2,128,384]{2,1,0:T(8,128)(2,1)S(1)}, bf16[2,128,384]{2,1,0:T(8,128)(2,1)S(1)}, u32[]{:S(2)}, u32[]{:S(2)}) collective-permute-start(bf16[2,128,384]{2,1,0:T(8,128)(2,1)S(1)} %copy-done.13), channel_id=1, source_target_pairs={{0,6},{1,7},{2,4},{3,5},{4,2},{5,3},{6,0},{7,1},{8,14},{9,15},{10,... | collective-permute-start | bytes 589832 | tf_op jit(solution)/shard_map/ppermute | solution.py:434
  67.1 26.0 %collective-permute-start.6 = (bf16[2,128,384]{2,1,0:T(8,128)(2,1)S(1)}, bf16[2,128,384]{2,1,0:T(8,128)(2,1)S(1)}, u32[]{:S(2)}, u32[]{:S(2)}) collective-permute-start(bf16[2,128,384]{2,1,0:T(8,128)(2,1)S(1)} %copy-done.12), channel_id=1, source_target_pairs={{0,7},{1,6},{2,5},{3,4},{4,3},{5,2},{6,1},{7,0},{8,15},{9,14},{10,... | collective-permute-start | bytes 589832 | tf_op jit(solution)/shard_map/ppermute | solution.py:434
  83.1 19.6 %copy-start.8 = (bf16[2,128,384]{2,1,0:T(8,128)(2,1)}, bf16[2,128,384]{2,1,0:T(8,128)(2,1)S(1)}, u32[]{:S(2)}) copy-start(bf16[2,128,384]{2,1,0:T(8,128)(2,1)S(1)} %collective-permute-done.4.rest_5_) | copy-start | bytes 589828
  88.8 13.9 %copy-start.9 = (bf16[2,128,384]{2,1,0:T(8,128)(2,1)}, bf16[2,128,384]{2,1,0:T(8,128)(2,1)S(1)}, u32[]{:S(2)}) copy-start(bf16[2,128,384]{2,1,0:T(8,128)(2,1)S(1)} %collective-permute-done.5.rest_6_) | copy-start | bytes 589828
  93.0 9.6 %copy-start.10 = (bf16[2,128,384]{2,1,0:T(8,128)(2,1)}, bf16[2,128,384]{2,1,0:T(8,128)(2,1)S(1)}, u32[]{:S(2)}) copy-start(bf16[2,128,384]{2,1,0:T(8,128)(2,1)S(1)} %collective-permute-done.6.rest_7_) | copy-start | bytes 589828
  93.0 9.6 %copy-start.1 = (bf16[8,2,128,384]{3,2,1,0:T(8,128)(2,1)}, bf16[8,2,128,384]{3,2,1,0:T(8,128)(2,1)S(1)}, u32[]{:S(2)}) copy-start(bf16[8,2,128,384]{3,2,1,0:T(8,128)(2,1)S(1)} %all-to-all-done.1.qk_ref) | copy-start | bytes 4718596
  93.0 31.9 %all-to-all-start.2 = ((bf16[64,16,128]{2,1,0:T(8,128)(2,1)}), bf16[64,16,128]{2,1,0:T(8,128)(2,1)S(1)}, u32[]{:S(2)}, u32[]{:S(2)}) async-start(bf16[64,16,128]{2,1,0:T(8,128)(2,1)} %scatter_short.1), calls=%async_computation.2 | async-start | bytes 524288 | tf_op jit(solution)/shard_map/all_to_all | solution.py:416
  124.9 0.7 copy-start.3
  145.3 3.6 %copy-start.11 = (f32[8,128]{1,0:T(8,128)S(1)}, f32[8,128]{1,0:T(8,128)}, u32[]{:S(2)}) copy-start(f32[8,128]{1,0:T(8,128)} %get-tuple-element.77) | copy-start | bytes 12292
  145.4 37.3 %all-to-all-start.4 = ((bf16[8,2,128,384]{3,2,1,0:T(8,128)(2,1)}), bf16[8,2,128,384]{3,2,1,0:T(8,128)(2,1)S(1)}, u32[]{:S(2)}, u32[]{:S(2)}) async-start(bf16[8,2,128,384]{3,2,1,0:T(8,128)(2,1)} %get-tuple-element.74), calls=%async_computation.4 | async-start | bytes 3145728 | tf_op jit(solution)/shard_map/all_to_all | solution.py:416
  182.7 1.2 copy-start

commit v4 on v2

v4 whole, which is shorter than its diff:
```python
import math

import jax
import jax.numpy as jnp
from jax import lax
from jax.experimental import pallas as pl
from jax.experimental.pallas import tpu as pltpu
from jax.sharding import PartitionSpec as P

HEAD_DIM = 128
TOK_DEV = 128
MOV = 8
RES = 120
EPS = 1e-06
WAYS = 8
GROUPS = 64
HD = 3072
LOCAL = HD // WAYS
HEADS = LOCAL // HEAD_DIM
BLOCKS = HD // 128
SCALE = 1.0 / math.sqrt(HEAD_DIM)
F32 = jnp.float32
BF16 = jnp.bfloat16
VMEM_LIMIT = 56 * 1024 * 1024

PLANE = [[xl * 32 + z * 2 + c for xl in range(2) for c in range(2)] for z in range(16)]
ZRING = [[xl * 32 + z * 2 + c for z in range(16)] for xl in range(2) for c in range(2)]

SMEM = pl.BlockSpec(memory_space=pltpu.SMEM)


def params(count=0):
    return pltpu.CompilerParams(
        vmem_limit_bytes=VMEM_LIMIT,
        dimension_semantics=("arbitrary",) * count if count else None,
    )


def find_source(dest_ref, group):
    return lax.fori_loop(
        0, GROUPS, lambda g, found: jnp.where(dest_ref[g] == group, g, found), jnp.int32(0)
    )


TAIL = TOK_DEV - 16
EXTRA = 4 * TOK_DEV
SENT = EXTRA + 16
PAIRS = WAYS // 2
SCALES = 3 * HEADS * PAIRS


def pack_kernel(q_ref, k_ref, v_ref, scale_ref, out_ref):
    def pair(ref, i, first):
        rows = [ref[j].astype(F32)[first : first + 8] for j in (2 * i, 2 * i + 1)]
        return jnp.concatenate(rows, axis=0).astype(BF16)

    for i in range(PAIRS):
        for n, ref in enumerate((q_ref, k_ref, v_ref)):
            rows = pair(ref, i, 8)
            for b in range(HEADS):
                out_ref[(n * HEADS + b) * PAIRS + i] = rows[:, b * 128 : (b + 1) * 128]
        out_ref[SCALES + i] = pair(scale_ref, i, 0)
    rest = GROUPS - SCALES - PAIRS
    out_ref[pl.ds(SCALES + PAIRS, rest)] = jnp.zeros((rest, 16, 128), BF16)


def pack_short(blocks):
    def rows(n, width):
        return pl.BlockSpec((WAYS, 16, width), lambda i: (0, n, 0))

    return pl.pallas_call(
        pack_kernel,
        grid=(1,),
        in_specs=[rows((n * TOK_DEV + TAIL) // 16, LOCAL) for n in range(3)]
        + [rows(EXTRA // 16, 128)],
        out_specs=pl.BlockSpec((GROUPS, 16, 128), lambda i: (0, 0, 0)),
        out_shape=jax.ShapeDtypeStruct((GROUPS, 16, 128), BF16),
        compiler_params=params(1),
        name="pack_short",
    )(blocks, blocks, blocks, blocks)


def scatter_kernel(dest_ref, in_ref, out_ref):
    def step(g, carry):
        out_ref[dest_ref[g]] = in_ref[g]
        return carry

    lax.fori_loop(0, GROUPS, step, 0)


def scatter_short(dest_group, parts):
    whole = pl.BlockSpec(memory_space=pltpu.VMEM)
    return pl.pallas_call(
        scatter_kernel,
        in_specs=[SMEM, whole],
        out_specs=whole,
        out_shape=jax.ShapeDtypeStruct(parts.shape, BF16),
        compiler_params=params(),
        name="scatter_short",
    )(dest_group, parts)


PRE_ROWS = 32


def row_scale(rows):
    return lax.rsqrt(jnp.sum(rows * rows, axis=1, keepdims=True) / HD + EPS)


def two_terms(scale):
    high = scale.astype(BF16).astype(F32)
    return high, scale - high


def pre_kernel(
    dest_ref, res_ref, move_ref, step_ref, table_ref,
    q_ref, k_ref, v_ref, go_ref, qg_ref, kg_ref, out_ref,
):
    step = pl.program_id(0)
    group = lax.axis_index("dp")
    slot = lax.axis_index("head")
    source = find_source(dest_ref, group)
    stay_weight = table_ref[step_ref[group, 0]]
    move_weight = table_ref[step_ref[source, 1]]
    rows = step * PRE_ROWS + lax.broadcasted_iota(jnp.int32, (PRE_ROWS, 1), 0)
    stay = jnp.where(slot * RES + rows < res_ref[group], stay_weight, 0.0)
    move = jnp.where(slot * MOV + rows - RES < move_ref[source], move_weight, 0.0)
    weight = jnp.where(rows < RES, stay, move)
    start = pl.multiple_of(step * PRE_ROWS, PRE_ROWS)

    def put(n, values):
        for p in range(WAYS):
            out_ref[p, pl.ds(n * TOK_DEV + start, PRE_ROWS), :] = values[
                :, p * LOCAL : (p + 1) * LOCAL
            ]

    terms = []
    for n, (in_ref, gain_ref) in enumerate(((q_ref, qg_ref), (k_ref, kg_ref))):
        x = in_ref[...].astype(F32)
        scale = row_scale(x)
        put(n, (x * scale * gain_ref[...]).astype(BF16))
        terms += two_terms(scale[PRE_ROWS - MOV :])
    put(2, v_ref[...])
    put(3, (go_ref[...].astype(F32) * weight).astype(BF16))

    @pl.when(step == TOK_DEV // PRE_ROWS - 1)
    def _():
        lane = lax.broadcasted_iota(jnp.int32, (MOV, LOCAL), 1)
        scales = jnp.zeros((MOV, LOCAL), F32)
        for n, term in enumerate(terms):
            scales = jnp.where(lane == n, term, scales)
        scales = jnp.concatenate([scales, jnp.zeros((16 - MOV, LOCAL), F32)], axis=0)
        for p in range(WAYS):
            out_ref[p, EXTRA:SENT, :] = scales.astype(BF16)


def prepare(dest, res_len, move_len, steps, table, q_in, k_in, v_in, grad_out, q_gain, k_gain):
    rows = pl.BlockSpec((PRE_ROWS, HD), lambda i: (i, 0))
    gain = pl.BlockSpec((1, HD), lambda i: (0, 0))
    return pl.pallas_call(
        pre_kernel,
        grid=(TOK_DEV // PRE_ROWS,),
        in_specs=[SMEM] * 5 + [rows] * 4 + [gain] * 2,
        out_specs=pl.BlockSpec((WAYS, SENT, LOCAL), lambda i: (0, 0, 0)),
        out_shape=jax.ShapeDtypeStruct((WAYS, SENT, LOCAL), BF16),
        compiler_params=params(1),
        cost_estimate=pl.CostEstimate(flops=20_000_000, bytes_accessed=6_300_000, transcendentals=0),
        name="prepare",
    )(dest, res_len, move_len, steps, table, q_in, k_in, v_in, grad_out, q_gain, k_gain)


def nt(a, b):
    return lax.dot_general(a, b, (((1,), (1,)), ((), ())), preferred_element_type=F32)


def tn(a, b):
    return lax.dot_general(a, b, (((0,), (0,)), ((), ())), preferred_element_type=F32)


def grads(q, k, v, g, bias):
    scores = nt(q, k) * SCALE + bias
    top = jnp.max(scores, axis=1, keepdims=True)
    raw = jnp.exp(scores - top)
    weights = raw * (1.0 / jnp.sum(raw, axis=1, keepdims=True))
    attended = jnp.dot(weights.astype(BF16), v, preferred_element_type=F32)
    delta = jnp.sum(g.astype(F32) * attended, axis=1, keepdims=True)
    score_grad = (weights * (nt(g, v) - delta)).astype(BF16)
    query_grad = jnp.dot(score_grad, k, preferred_element_type=F32) * SCALE
    return query_grad, tn(score_grad, q)


QUERY_ROWS = 512
ALL = WAYS * TOK_DEV
ONES = 16
POWER = SCALE * math.log2(math.e)


def flip(block):
    return block.astype(F32).T.astype(BF16)


BACK_MORE = 32
BACK_HEAD = 64
BACK = BACK_HEAD + 2 * TAIL


def attention_kernel(res_ref, in_ref, qg_ref, kg_ref, out_ref, gain_ref, *rest):
    q_ref, k_ref, v_ref, g_ref, qt_ref, kt_ref, vt_ref, gt_ref, dq_ref, dk_ref = rest
    head = pl.program_id(0)
    slot = lax.axis_index("head")
    stay_len = res_ref[lax.axis_index("dp")]
    rows = lax.broadcasted_iota(jnp.int32, (TOK_DEV, 1), 0)
    first_lane = lax.broadcasted_iota(jnp.int32, (TOK_DEV, 128), 1) == 0
    for s in range(WAYS):
        here = pl.ds(s * TOK_DEV, TOK_DEV)
        q, k, v, g = (in_ref[s, n * TOK_DEV : (n + 1) * TOK_DEV] for n in range(4))
        g = jnp.where(rows < RES, g.astype(F32), 0.0)
        limit = jnp.minimum(stay_len - s * RES, RES)
        q_ref[here, 0:128] = q
        q_ref[here, 128:256] = jnp.where(first_lane, 1.0, 0.0).astype(BF16)
        k_ref[here, 0:128] = k
        masked = jnp.logical_and(first_lane, rows >= limit)
        k_ref[here, 128:256] = jnp.where(masked, -1e30, 0.0).astype(BF16)
        v_ref[here] = v
        g_ref[here] = g.astype(BF16)
        qt_ref[:, here] = flip(q)
        kt_ref[:, here] = flip(k)
        vt_ref[0:128, here] = flip(v)
        gt_ref[:, here] = g.T
    ones = lax.broadcasted_iota(jnp.int32, (ONES, ALL), 0) == 0
    vt_ref[128 : 128 + ONES, :] = jnp.where(ones, 1.0, 0.0).astype(BF16)

    for i in range(ALL // QUERY_ROWS):
        here = pl.ds(i * QUERY_ROWS, QUERY_ROWS)
        scores = nt(k_ref[...], q_ref[here])
        raw = jnp.exp2((scores - jnp.max(scores, axis=0, keepdims=True)) * POWER)
        attended = jnp.dot(vt_ref[...], raw.astype(BF16), preferred_element_type=F32)
        inverse = 1.0 / attended[128:129]
        delta = jnp.sum(gt_ref[:, here] * attended[0:128], axis=0, keepdims=True) * inverse
        score_grad = (raw * (nt(v_ref[...], g_ref[here]) - delta)).astype(BF16)
        dq = jnp.dot(kt_ref[...], score_grad, preferred_element_type=F32) * (inverse * SCALE)
        dq_ref[here] = dq.T
        dk = nt(score_grad, (qt_ref[:, here].astype(F32) * inverse).astype(BF16))
        if i == 0:
            dk_ref[...] = dk
        else:
            dk_ref[...] += dk

    dq = dq_ref[...].astype(BF16)
    dk = (dk_ref[...] * SCALE).astype(BF16)
    for s in range(WAYS):
        for n, grad in enumerate((dq, dk)):
            block = grad[s * TOK_DEV : (s + 1) * TOK_DEV]
            out_ref[s, n * 16 : (n + 1) * 16] = block[TAIL:]
            out_ref[s, BACK_HEAD + n * TAIL : BACK_HEAD + (n + 1) * TAIL] = block[:TAIL]

    def total(grad, norm, gain_ref):
        summed = jnp.sum(grad.astype(F32) * norm.astype(F32), axis=0, keepdims=True)
        return summed / gain_ref[pl.ds(slot * HEADS + head, 1)]

    gain_ref[pl.ds(head, 1)] = total(dq, q_ref[:, 0:128], qg_ref)
    gain_ref[pl.ds(HEADS + head, 1)] = total(dk, k_ref[:, 0:128], kg_ref)


def whole_block(shape):
    return pl.BlockSpec(shape, lambda b: (0,) * len(shape))


def attention(res_len, blocks, q_gain, k_gain):
    return pl.pallas_call(
        attention_kernel,
        grid=(HEADS,),
        in_specs=[SMEM, pl.BlockSpec((WAYS, SENT, 128), lambda b: (0, 0, b))]
        + [whole_block((BLOCKS, 128))] * 2,
        out_specs=[
            pl.BlockSpec((WAYS, BACK, 128), lambda b: (0, 0, b)),
            whole_block((8, 128)),
        ],
        out_shape=[
            jax.ShapeDtypeStruct((WAYS, BACK, LOCAL), BF16),
            jax.ShapeDtypeStruct((8, 128), F32),
        ],
        scratch_shapes=[pltpu.VMEM((ALL, 256), BF16)] * 2
        + [pltpu.VMEM((ALL, 128), BF16)] * 2
        + [pltpu.VMEM((128, ALL), BF16)] * 2
        + [pltpu.VMEM((128 + ONES, ALL), BF16), pltpu.VMEM((128, ALL), F32)]
        + [pltpu.VMEM((ALL, 128), F32)] * 2,
        compiler_params=params(1),
        cost_estimate=pl.CostEstimate(
            flops=4_000_000_000, bytes_accessed=5_000_000, transcendentals=3_200_000
        ),
        name="attention",
    )(res_len, blocks, q_gain, k_gain)


def short_kernel(
    dest_ref, move_ref, parts_ref, g_ref, grad_ref, part_ref, qg_ref, kg_ref, out_ref, gain_ref
):
    head = pl.program_id(0)
    slot = lax.axis_index("head")
    move_len = move_ref[find_source(dest_ref, lax.axis_index("dp"))]
    count = WAYS * MOV
    lane = lax.broadcasted_iota(jnp.int32, (1, count), 1)
    bias = jnp.where(lane < move_len, 0.0, -1e30).astype(F32)

    def gathered(n):
        return parts_ref[pl.ds((n * HEADS + head) * PAIRS, PAIRS)].reshape(count, 128)

    def per_device(rows):
        return rows.reshape(WAYS, MOV, 128)

    q, k, v = gathered(0), gathered(1), gathered(2)
    q_float, k_float = q.astype(F32), k.astype(F32)
    weighted = g_ref[...].astype(F32)[:, 8:16].reshape(count, 128)
    dq, dk = grads(q, k, v, weighted.astype(BF16), bias)
    dq = dq.astype(BF16).astype(F32)
    dk = (dk * SCALE).astype(BF16).astype(F32)
    for n, grad in enumerate((dq, dk)):
        kept = grad_ref[:, n * 16 : (n + 1) * 16].astype(F32)[:, 0:8]
        both = jnp.concatenate([kept, per_device(grad)], axis=1)
        out_ref[:, n * 16 : (n + 1) * 16] = both.astype(BF16)
    norms = jnp.concatenate([per_device(q_float), per_device(k_float)], axis=1)
    out_ref[:, BACK_MORE : BACK_MORE + 16] = norms.astype(BF16)
    scales = parts_ref[SCALES : SCALES + PAIRS].astype(F32).reshape(WAYS, MOV, 128)
    scales = jnp.concatenate([scales, jnp.zeros_like(scales)], axis=1)
    out_ref[:, BACK_MORE + 16 : BACK_HEAD] = scales.astype(BF16)

    @pl.when(head == 0)
    def _():
        gain_ref[...] = part_ref[...]

    def total(grad, norm, gains):
        return jnp.sum(grad * norm, axis=0, keepdims=True) / gains[pl.ds(slot * HEADS + head, 1)]

    gain_ref[pl.ds(head, 1)] += total(dq, q_float, qg_ref)
    gain_ref[pl.ds(HEADS + head, 1)] += total(dk, k_float, kg_ref)


def short_attention(dest, move_len, parts, blocks, grad, part, q_gain, k_gain):
    head_rows = pl.BlockSpec((WAYS, BACK_HEAD, 128), lambda b: (0, 0, b))
    return pl.pallas_call(
        short_kernel,
        grid=(HEADS,),
        in_specs=[SMEM] * 2
        + [whole_block((GROUPS, 16, 128))]
        + [pl.BlockSpec((WAYS, 16, 128), lambda b: (0, (EXTRA - 16) // 16, b))]
        + [head_rows, whole_block((8, 128))]
        + [whole_block((BLOCKS, 128))] * 2,
        out_specs=[head_rows, whole_block((8, 128))],
        out_shape=[
            jax.ShapeDtypeStruct(grad.shape, BF16),
            jax.ShapeDtypeStruct((8, 128), F32),
        ],
        input_output_aliases={4: 0},
        compiler_params=params(1),
        cost_estimate=pl.CostEstimate(
            flops=20_000_000, bytes_accessed=1_000_000, transcendentals=12_000
        ),
        name="short_attention",
    )(dest, move_len, parts, blocks, grad, part, q_gain, k_gain)


POST_ROWS = 16


def post_kernel(
    q_ref, k_ref, more_ref, qg_ref, kg_ref, dq_ref, dk_ref, oq_ref, ok_ref, unit_ref, scale_ref
):
    last = pl.program_id(0) == TOK_DEV // POST_ROWS - 1

    def one(n, in_ref, gain_ref, grad_ref, out_ref):
        x = in_ref[...].astype(F32)
        scale = row_scale(x)
        scale_ref[...] = jnp.broadcast_to(scale, scale_ref.shape)
        unit_ref[...] = x * scale
        gain = gain_ref[...]

        @pl.when(last)
        def _():
            norms = jnp.concatenate(
                [more_ref[p, 0:16].astype(F32)[n * 8 : n * 8 + 8] for p in range(WAYS)], axis=1
            )
            unit_ref[8:16] = norms / gain
            terms = more_ref[0, 16:32, 0:128].astype(F32)[0:8]
            total = terms[:, 2 * n : 2 * n + 1] + terms[:, 2 * n + 1 : 2 * n + 2]
            scale_ref[8:16] = jnp.broadcast_to(total, (8, 128))

        unit = unit_ref[...]
        grad = jnp.concatenate([grad_ref[p].astype(F32) for p in range(WAYS)], axis=1) * gain
        dots = jnp.sum(unit * grad, axis=1, keepdims=True) / HD
        out_ref[...] = (scale_ref[:, 0:1] * (grad - unit * dots)).astype(BF16)

    one(0, q_ref, qg_ref, dq_ref, oq_ref)
    one(1, k_ref, kg_ref, dk_ref, ok_ref)


def finish(q_in, k_in, q_gain, k_gain, back):
    rows = pl.BlockSpec((POST_ROWS, HD), lambda i: (i, 0))
    gain = pl.BlockSpec((1, HD), lambda i: (0, 0))
    steps = TOK_DEV // POST_ROWS

    def grad_rows(n):
        first = (BACK_HEAD + n * TAIL) // 16
        return pl.BlockSpec(
            (WAYS, 16, LOCAL), lambda i: (0, jnp.where(i == steps - 1, n, first + i), 0)
        )

    return pl.pallas_call(
        post_kernel,
        grid=(steps,),
        in_specs=[
            rows,
            rows,
            pl.BlockSpec((WAYS, 32, LOCAL), lambda i: (0, BACK_MORE // 32, 0)),
            gain,
            gain,
            grad_rows(0),
            grad_rows(1),
        ],
        out_specs=[rows, rows],
        out_shape=[jax.ShapeDtypeStruct((TOK_DEV, HD), BF16)] * 2,
        scratch_shapes=[pltpu.VMEM((POST_ROWS, HD), F32), pltpu.VMEM((POST_ROWS, 128), F32)],
        compiler_params=params(1),
        cost_estimate=pl.CostEstimate(flops=20_000_000, bytes_accessed=4_800_000, transcendentals=0),
        name="finish",
    )(q_in, k_in, back, q_gain, k_gain, back, back)


def swap_all(x, axis):
    return lax.all_to_all(x, axis, split_axis=0, concat_axis=0, tiled=True)


def gather_sum(x, rings):
    return jnp.sum(lax.all_gather(x, "dp", axis_index_groups=rings), axis=0)


def local(
    q_in, k_in, v_in, grad_out, q_gain, k_gain,
    res_len, move_len, step_index, dest_group, loss_weight,
):
    gain_q, gain_k = q_gain.reshape(1, HD), k_gain.reshape(1, HD)
    gain_q_rows, gain_k_rows = q_gain.reshape(BLOCKS, 128), k_gain.reshape(BLOCKS, 128)
    sent = prepare(
        dest_group, res_len, move_len, step_index, loss_weight,
        q_in, k_in, v_in, grad_out, gain_q, gain_k,
    )
    blocks = swap_all(sent, "head")
    packed, blocks = lax.optimization_barrier((pack_short(blocks), blocks))
    spread = swap_all(packed, "dp")
    grad, part = attention(res_len, blocks, gain_q_rows, gain_k_rows)
    spread, part = lax.optimization_barrier((spread, part))
    parts = swap_all(scatter_short(dest_group, spread), "dp")
    grad, part = short_attention(
        dest_group, move_len, parts, blocks, grad, part, gain_q_rows, gain_k_rows
    )
    back = swap_all(grad, "head")
    total = gather_sum(gather_sum(part, ZRING), PLANE)
    out_q, out_k = finish(q_in, k_in, gain_q, gain_k, back)
    return (
        out_q,
        out_k,
        total[:HEADS].reshape(LOCAL),
        total[HEADS : 2 * HEADS].reshape(LOCAL),
    )


def solution(mesh):
    tokens = P(("dp", "head"), None)
    return jax.shard_map(
        local,
        mesh=mesh,
        in_specs=(tokens,) * 4 + (P(),) * 7,
        out_specs=(tokens, tokens, P("head"), P("head")),
        check_vma=False,
    )
```

time: 177 us -> 181 us (1.023)
  blocking collectives: 35.2 us -> 103 us
  starting transfers between devices: 70.3 us -> 25.1 us
  waiting for transfers between devices: 31.5 us -> 9.05 us
  Pallas kernels: 33.6 us -> 37.9 us
    all_to_all x0 -> x2, blocking collectives: none -> 71.1 us  [swap_all(): return lax.all_to_all(x, axis, split_axis=0, concat_axis=0, tiled=True)]
    ppermute x7 -> x0, starting transfers between devices: 28.2 us -> none  [local(): lax.ppermute(x, 'head', [(i, i ^ n + 1) for i in range(WAYS)])]
    ppermute x7 -> x0, waiting for transfers between devices: 21.2 us -> none  [local(): lax.ppermute(x, 'head', [(i, i ^ n + 1) for i in range(WAYS)])]
    all_to_all x4 -> x2, starting transfers between devices: 42.1 us -> 25.1 us  [swap_all(): return lax.all_to_all(x, axis, split_axis=0, concat_axis=0, tiled=True)]
    pallas_call x4, Pallas kernels: 24.6 us -> 28.5 us  [the longest x1 13.2 us: attention(): pl.pallas_call(attention_kernel, grid=(HEADS,), in_specs=[SMEM, pl.BlockS...]
    all_gather x2, blocking collectives: 35.2 us -> 32.4 us  [gather_sum(): return jnp.sum(lax.all_gather(x, 'dp', axis_index_groups=rings), axis=0)]
    all_to_all x4 -> x2, waiting for transfers between devices: 10.3 us -> 9.05 us  [swap_all(): return lax.all_to_all(x, axis, split_axis=0, concat_axis=0, tiled=True)]
    unnamed x27 -> x7, local copies, waits for them, and re-layouts: 3.99 us -> 3.33 us
  transfers between devices with their start and end apart: 11 -> 2, of which waited for: 5 -> 1; matrix products, arithmetic and copies ran while one was open for 1% -> 0% of each run, Pallas kernels for 5% -> 7%
where the time goes in v4:
time: 181 us; the launch traced here: 180 us
  blocking collectives  103 us (57%)
  Pallas kernels  37.9 us (21%)
  starting transfers between devices  25.1 us (14%)
  waiting for transfers between devices  9.05 us (5%)
  local copies, waits for them, and re-layouts  3.92 us (2%)
    all_to_all x2, blocking collectives, swap_all(): return lax.all_to_all(x, axis, split_axis=0, concat_axis=0, tiled=True)  71.1 us
    all_gather x2, blocking collectives, gather_sum(): return jnp.sum(lax.all_gather(x, 'dp', axis_index_groups=rings), axis=0)  32.4 us
    all_to_all x2, starting transfers between devices, swap_all(): return lax.all_to_all(x, axis, split_axis=0, concat_axis=0, tiled=True)  25.1 us
    pallas_call x1, Pallas kernels, attention(): pl.pallas_call(attention_kernel, grid=(HEADS,), in_specs=[SMEM, pl.BlockS...  13.2 us
    all_to_all x2, waiting for transfers between devices, swap_all(): return lax.all_to_all(x, axis, split_axis=0, concat_axis=0, tiled=True)  9.05 us
    pallas_call x1, Pallas kernels, finish(): pl.pallas_call(post_kernel, grid=(steps,), in_specs=[rows, rows, pl.Block...  7.6 us
    pallas_call x1, Pallas kernels, prepare(): pl.pallas_call(pre_kernel, grid=(TOK_DEV // PRE_ROWS,), in_specs=[SMEM] *...  7.37 us
    pallas_call x1, Pallas kernels, short_attention(): pl.pallas_call(short_kernel, grid=(HEADS,), in_specs=[SMEM] * 2 + [whole_...  5.97 us
  transfers between devices with their start and end apart: 2, of which 1 were waited for; matrix products, arithmetic and copies ran while one was open for 0% of the time, Pallas kernels for 7%

profile of v4, /device:TPU:1, one launch (start us, length us, event | category | flops | bytes accessed | tf_op | source)
XLA Modules:
  0.0 180.1 jit_solution(18218276520336409609)
XLA Ops:
  0.6 1.4 copy.17.step_ref
  2.0 7.4 %prepare.1 = bf16[8,528,384]{2,1,0:T(8,128)(2,1)} custom-call(s32[64]{0:T(128)} %dest_ref.5, s32[64]{0:T(128)} %res_ref.3, s32[64]{0:T(128)} %move_ref.3, s32[64,2]{1,0:T(8,128)} %copy.17.step_ref, f32[1000]{0:T(1024)} %table_ref.1, bf16[128,3072]{1,0:T(8,128)(2,1)} %q_ref.3, bf16[128,3072]{1,0:T(8,128)(2,1)} %k_ref.3, bf16[128,3072]{1,0:T(8,128)(2,1)} %v_ref.1, ...), custom_call_target="tpu_custom_call" | custom-call | flops 20000000 | bytes 6300000 | tf_op jit(solution)/shard_map/prepare/pallas_call | solution.py:160
  9.4 44.1 %all_to_all.20.q_ref.k_ref.v_ref.scale_ref.in_ref.g_ref = bf16[8,528,384]{2,1,0:T(8,128)(2,1)} all-to-all(bf16[8,528,384]{2,1,0:T(8,128)(2,1)} %prepare.1), channel_id=1, replica_groups=mesh['dp'=64,'head'=8] {'head'}, dimensions={0} | all-to-all | bytes 6488064 | tf_op jit(solution)/shard_map/all_to_all | solution.py:430
  53.5 1.7 pack_short.1
  55.2 21.3 %all-to-all-start.1 = ((bf16[64,16,128]{2,1,0:T(8,128)(2,1)}), bf16[64,16,128]{2,1,0:T(8,128)(2,1)S(1)}, u32[]{:S(2)}, u32[]{:S(2)}) async-start(bf16[64,16,128]{2,1,0:T(8,128)(2,1)} %pack_short.1), calls=%async_computation.1 | async-start | bytes 524288 | tf_op jit(solution)/shard_map/all_to_all | solution.py:430
  76.5 13.2 %attention.1 = (bf16[8,288,384]{2,1,0:T(8,128)(2,1)}, f32[8,128]{1,0:T(8,128)}) custom-call(s32[64]{0:T(128)} %res_ref.3, bf16[8,528,384]{2,1,0:T(8,128)(2,1)} %all_to_all.20.q_ref.k_ref.v_ref.scale_ref.in_ref.g_ref, f32[24,128]{1,0:T(8,128)} %bitcast.13, f32[24,128]{1,0:T(8,128)} %bitcast.17), custom_call_target="tpu_custom_call" | custom-call | flops 4000000000 | bytes 5000000 | tf_op jit(solution)/shard_map/attention/pallas_call | solution.py:270
  89.7 9.0 %all-to-all-done.1.in_ref = bf16[64,16,128]{2,1,0:T(8,128)(2,1)S(1)} async-done(((bf16[64,16,128]{2,1,0:T(8,128)(2,1)}), bf16[64,16,128]{2,1,0:T(8,128)(2,1)S(1)}, u32[]{:S(2)}, u32[]{:S(2)}) %all-to-all-start.1) | async-done | bytes 262176 | tf_op jit(solution)/shard_map/all_to_all | solution.py:430
  98.8 0.0 copy-start.1
  98.8 0.7 copy-done.1
  99.5 2.1 %scatter_short.1 = bf16[64,16,128]{2,1,0:T(8,128)(2,1)} custom-call(s32[64]{0:T(128)} %dest_ref.5, bf16[64,16,128]{2,1,0:T(8,128)(2,1)} %copy-done.1), custom_call_target="tpu_custom_call" | custom-call | tf_op jit(solution)/shard_map/scatter_short/pallas_call | solution.py:93
  101.5 27.0 %all_to_all.21.parts_ref = bf16[64,16,128]{2,1,0:T(8,128)(2,1)} all-to-all(bf16[64,16,128]{2,1,0:T(8,128)(2,1)} %scatter_short.1), channel_id=1, replica_groups=mesh['dp'=64,'head'=8] {'dp'}, dimensions={0} | all-to-all | bytes 524288 | tf_op jit(solution)/shard_map/all_to_all | solution.py:430
  128.5 6.0 %short_attention.1 = (bf16[8,288,384]{2,1,0:T(8,128)(2,1)}, f32[8,128]{1,0:T(8,128)}) custom-call(s32[64]{0:T(128)} %dest_ref.5, s32[64]{0:T(128)} %move_ref.3, bf16[64,16,128]{2,1,0:T(8,128)(2,1)} %all_to_all.21.parts_ref, bf16[8,528,384]{2,1,0:T(8,128)(2,1)} %all_to_all.20.q_ref.k_ref.v_ref.scale_ref.in_ref.g_ref, ...), custom_call_target="tpu_custom_call", output_to_operand_aliasing={{0}: (4, {})} | custom-call | flops 20000000 | bytes 1000000 | tf_op jit(solution)/shard_map/short_attention/pallas_call | solution.py:341
  134.5 0.0 copy-start.2
  134.5 3.7 %all-to-all-start.3 = ((bf16[8,288,384]{2,1,0:T(8,128)(2,1)}), bf16[8,288,384]{2,1,0:T(8,128)(2,1)S(1)}, u32[]{:S(2)}, u32[]{:S(2)}) async-start(bf16[8,288,384]{2,1,0:T(8,128)(2,1)} %get-tuple-element.20), calls=%async_computation.3 | async-start | bytes 3538944 | tf_op jit(solution)/shard_map/all_to_all | solution.py:430
  138.2 0.0 copy-done.2
  138.3 22.2 %all-gather = f32[128,128]{1,0:T(8,128)S(1)} all-gather(f32[8,128]{1,0:T(8,128)S(1)} %copy-done.2), channel_id=2, replica_groups={{0,16,32,48,64,80,96,112,128,144,160,176,192,208,224,240},{8,24,40,56,7..., dimensions={0}, use_global_device_ids=true | all-gather | bytes 69632 | tf_op jit(solution)/shard_map/all_gather | solution.py:434
  160.5 10.2 %all-gather.1 = f32[32,128]{1,0:T(8,128)S(1)} all-gather(f32[8,128]{1,0:T(8,128)S(1)} %bitcast_reduce_fusion), channel_id=3, replica_groups={{0,8,256,264},{16,24,272,280},{32,40,288,296},{48,56,304,312},{64,72,32..., dimensions={0}, use_global_device_ids=true | all-gather | bytes 20480 | tf_op jit(solution)/shard_map/all_gather | solution.py:434
  170.7 0.6 slice_bitcast_fusion
  171.3 0.0 all-to-all-done.3.more_ref.dq_ref.dk_ref
  171.3 0.0 copy-start
  171.3 1.2 copy-done
  172.5 7.6 %finish.1 = (bf16[128,3072]{1,0:T(8,128)(2,1)}, bf16[128,3072]{1,0:T(8,128)(2,1)}) custom-call(bf16[128,3072]{1,0:T(8,128)(2,1)} %q_ref.3, bf16[128,3072]{1,0:T(8,128)(2,1)} %k_ref.3, bf16[8,288,384]{2,1,0:T(8,128)(2,1)} %copy-done, f32[1,3072]{1,0:T(1,128)} %bitcast.15, f32[1,3072]{1,0:T(1,128)} %bitcast.19, bf16[8,288,384]{2,1,0:T(8,128)(2,1)} %copy-done, ...), custom_call_target="tpu_custom_call" | custom-call | flops 20000000 | bytes 4800000 | tf_op jit(solution)/shard_map/finish/pallas_call | solution.py:408
  (2 shorter events, 0.0 us)
Async XLA Ops:
  55.2 43.6 %all-to-all-start.1 = ((bf16[64,16,128]{2,1,0:T(8,128)(2,1)}), bf16[64,16,128]{2,1,0:T(8,128)(2,1)S(1)}, u32[]{:S(2)}, u32[]{:S(2)}) async-start(bf16[64,16,128]{2,1,0:T(8,128)(2,1)} %pack_short.1), calls=%async_computation.1 | async-start | bytes 524288 | tf_op jit(solution)/shard_map/all_to_all | solution.py:430
  98.8 0.7 copy-start.1
  134.5 3.7 %copy-start.2 = (f32[8,128]{1,0:T(8,128)S(1)}, f32[8,128]{1,0:T(8,128)}, u32[]{:S(2)}) copy-start(f32[8,128]{1,0:T(8,128)} %get-tuple-element.23) | copy-start | bytes 12292
  134.5 36.7 %all-to-all-start.3 = ((bf16[8,288,384]{2,1,0:T(8,128)(2,1)}), bf16[8,288,384]{2,1,0:T(8,128)(2,1)S(1)}, u32[]{:S(2)}, u32[]{:S(2)}) async-start(bf16[8,288,384]{2,1,0:T(8,128)(2,1)} %get-tuple-element.20), calls=%async_computation.3 | async-start | bytes 3538944 | tf_op jit(solution)/shard_map/all_to_all | solution.py:430
  171.3 1.2 copy-start

commit v5 on v2

--- a/solution.py
+++ b/solution.py
@@ -21,7 +21,7 @@
 SCALE = 1.0 / math.sqrt(HEAD_DIM)
 F32 = jnp.float32
 BF16 = jnp.bfloat16
-VMEM_LIMIT = 56 * 1024 * 1024
+VMEM_LIMIT = 63 * 1024 * 1024
 
 PLANE = [[xl * 32 + z * 2 + c for xl in range(2) for c in range(2)] for z in range(16)]
 ZRING = [[xl * 32 + z * 2 + c for z in range(16)] for xl in range(2) for c in range(2)]
@@ -127,7 +127,7 @@
     )(parts, q_gain, k_gain)
 
 
-PRE_ROWS = 32
+PRE_ROWS = 64
 
 
 def pre_kernel(
@@ -139,8 +139,8 @@
     group = lax.axis_index("dp")
     slot = lax.axis_index("head")
     source = find_source(dest_ref, group)
-    stay_weight = table_ref[step_ref[group, 0]]
-    move_weight = table_ref[step_ref[source, 1]]
+    stay_weight = table_ref[step_ref[group]]
+    move_weight = table_ref[step_ref[GROUPS + source]]
     rows = pl.program_id(0) * PRE_ROWS + lax.broadcasted_iota(jnp.int32, (PRE_ROWS, 1), 0)
     stay = jnp.where(slot * RES + rows < res_ref[group], stay_weight, 0.0)
     move = jnp.where(slot * MOV + rows - RES < move_ref[source], move_weight, 0.0)
@@ -202,23 +202,24 @@
     return block.astype(F32).T.astype(BF16)
 
 
-def attention_kernel(dest_ref, res_ref, move_ref, *rest):
+TAIL = TOK_DEV - 16
+
+
+def attention_kernel(res_ref, *rest):
     slots, rest = rest[:WAYS], rest[WAYS:]
-    short_ref, qg_ref, kg_ref, out_ref, gain_ref, *rest = rest
+    qg_ref, kg_ref, out_ref, gain_ref, short_g_ref, *rest = rest
     q_ref, k_ref, v_ref, g_ref, qt_ref, kt_ref, vt_ref, gt_ref, dq_ref, dk_ref = rest
     head = pl.program_id(0)
-    group = lax.axis_index("dp")
     slot = lax.axis_index("head")
-    source = find_source(dest_ref, group)
-    stay_len = res_ref[group]
-    move_len = move_ref[source]
+    stay_len = res_ref[lax.axis_index("dp")]
     peers = [jnp.bitwise_xor(slot, s) for s in range(WAYS)]
     rows = lax.broadcasted_iota(jnp.int32, (TOK_DEV, 1), 0)
     first_lane = lax.broadcasted_iota(jnp.int32, (TOK_DEV, 128), 1) == 0
     for s in range(WAYS):
         here = pl.ds(s * TOK_DEV, TOK_DEV)
-        q, k, v = slots[s][0], slots[s][1], slots[s][2]
-        g = jnp.where(rows < RES, slots[s][3].astype(F32), 0.0)
+        q, k, v, g = (slots[s][n] for n in range(4))
+        short_g_ref[peers[s]] = g[TAIL:]
+        g = jnp.where(rows < RES, g.astype(F32), 0.0)
         limit = jnp.minimum(stay_len - peers[s] * RES, RES)
         q_ref[here, 0:128] = q
         q_ref[here, 128:256] = jnp.where(first_lane, 1.0, 0.0).astype(BF16)
@@ -250,53 +251,41 @@
         else:
             dk_ref[...] += dk
 
-    lines = [short_ref[p].astype(F32) for p in peers]
-    short_q = jnp.concatenate([x[0:8] for x in lines], axis=0).astype(BF16)
-    short_k = jnp.concatenate([x[8:16] for x in lines], axis=0).astype(BF16)
-    short_v = jnp.concatenate([x[16:24] for x in lines], axis=0).astype(BF16)
-    short_g = jnp.concatenate(
-        [slots[s][3, pl.ds(112, 16)].astype(F32)[8:16] for s in range(WAYS)], axis=0
-    ).astype(BF16)
-    lane = lax.broadcasted_iota(jnp.int32, (1, WAYS * MOV), 1)
-    position = jnp.bitwise_xor(lane // MOV, slot) * MOV + lane % MOV
-    short_bias = jnp.where(position < move_len, 0.0, -1e30).astype(F32)
-    short_dq, short_dk = grads(short_q, short_k, short_v, short_g, short_bias)
-    short_dq = short_dq.astype(BF16).astype(F32)
-    short_dk = (short_dk * SCALE).astype(BF16).astype(F32)
-
     dq = dq_ref[...].astype(BF16)
     dk = (dk_ref[...] * SCALE).astype(BF16)
     for s in range(WAYS):
-        for n, stay, short in ((0, dq, short_dq), (1, dk, short_dk)):
-            block = stay[s * TOK_DEV : (s + 1) * TOK_DEV].astype(F32)
-            block = jnp.concatenate([block[:RES], short[s * MOV : (s + 1) * MOV]], axis=0)
-            out_ref[peers[s], n] = block.astype(BF16)
-
-    def total(stay, norm, short, short_norm, gain_ref):
-        summed = jnp.sum(stay.astype(F32) * norm.astype(F32), axis=0, keepdims=True)
-        summed += jnp.sum(short * short_norm.astype(F32), axis=0, keepdims=True)
+        for n, grad in enumerate((dq, dk)):
+            block = grad[s * TOK_DEV : (s + 1) * TOK_DEV]
+            out_ref[peers[s], n] = block
+
+    def total(grad, norm, gain_ref):
+        summed = jnp.sum(grad.astype(F32) * norm.astype(F32), axis=0, keepdims=True)
         return summed / gain_ref[pl.ds(slot * HEADS + head, 1)]
 
-    gain_ref[pl.ds(head, 1)] = total(dq, q_ref[:, 0:128], short_dq, short_q, qg_ref)
-    gain_ref[pl.ds(HEADS + head, 1)] = total(dk, k_ref[:, 0:128], short_dk, short_k, kg_ref)
-
-
-def attention(dest, res_len, move_len, slots, short, q_gain, k_gain):
-    whole = lambda shape: pl.BlockSpec(shape, lambda b: (0,) * len(shape))
+    gain_ref[pl.ds(head, 1)] = total(dq, q_ref[:, 0:128], qg_ref)
+    gain_ref[pl.ds(HEADS + head, 1)] = total(dk, k_ref[:, 0:128], kg_ref)
+
+
+def whole_block(shape):
+    return pl.BlockSpec(shape, lambda b: (0,) * len(shape))
+
+
+def attention(res_len, slots, q_gain, k_gain):
     return pl.pallas_call(
         attention_kernel,
         grid=(HEADS,),
-        in_specs=[SMEM] * 3
+        in_specs=[SMEM]
         + [pl.BlockSpec((4, TOK_DEV, 128), lambda b: (0, 0, b))] * WAYS
-        + [pl.BlockSpec((WAYS, 32, 128), lambda b: (0, 0, b))]
-        + [whole((BLOCKS, 128))] * 2,
+        + [whole_block((BLOCKS, 128))] * 2,
         out_specs=[
             pl.BlockSpec((WAYS, 2, TOK_DEV, 128), lambda b: (0, 0, 0, b)),
-            whole((8, 128)),
+            whole_block((8, 128)),
+            pl.BlockSpec((WAYS, 16, 128), lambda b: (0, 0, b)),
         ],
         out_shape=[
             jax.ShapeDtypeStruct((WAYS, 2, TOK_DEV, LOCAL), BF16),
             jax.ShapeDtypeStruct((8, 128), F32),
+            jax.ShapeDtypeStruct((WAYS, 16, LOCAL), BF16),
         ],
         scratch_shapes=[pltpu.VMEM((ALL, 256), BF16)] * 2
         + [pltpu.VMEM((ALL, 128), BF16)] * 2
@@ -308,10 +297,63 @@
             flops=4_000_000_000, bytes_accessed=5_000_000, transcendentals=3_200_000
         ),
         name="attention",
-    )(dest, res_len, move_len, *slots, short, q_gain, k_gain)
-
-
-POST_ROWS = 32
+    )(res_len, *slots, q_gain, k_gain)
+
+
+def short_kernel(
+    dest_ref, move_ref, short_ref, g_ref, grad_ref, part_ref, qg_ref, kg_ref, out_ref, gain_ref
+):
+    slot = lax.axis_index("head")
+    move_len = move_ref[find_source(dest_ref, lax.axis_index("dp"))]
+    count = WAYS * MOV
+    lane = lax.broadcasted_iota(jnp.int32, (1, count), 1)
+    bias = jnp.where(lane < move_len, 0.0, -1e30).astype(F32)
+    gain_ref[...] = part_ref[...]
+
+    def rows_at(values, first):
+        return values[:, first : first + MOV].reshape(count, 128)
+
+    for head in range(HEADS):
+        cols = slice(head * 128, (head + 1) * 128)
+        lines = short_ref[:, :, cols].astype(F32)
+        q, k, v = rows_at(lines, 0), rows_at(lines, 8), rows_at(lines, 16)
+        g = rows_at(g_ref[:, :, cols].astype(F32), 8)
+        dq, dk = grads(q.astype(BF16), k.astype(BF16), v.astype(BF16), g.astype(BF16), bias)
+        dq = dq.astype(BF16).astype(F32)
+        dk = (dk * SCALE).astype(BF16).astype(F32)
+        for n, grad, norm, gains in ((0, dq, q, qg_ref), (1, dk, k, kg_ref)):
+            kept = grad_ref[:, n, :, cols].astype(F32)[:, 0:8]
+            both = jnp.concatenate([kept, grad.reshape(WAYS, MOV, 128)], axis=1)
+            out_ref[:, n, :, cols] = both.astype(BF16)
+            total = jnp.sum(grad * norm, axis=0, keepdims=True)
+            total = total / gains[pl.ds(slot * HEADS + head, 1)]
+            gain_ref[n * HEADS + head : n * HEADS + head + 1] += total
+
+
+def short_attention(dest, move_len, short, short_g, grad, part, q_gain, k_gain):
+    tail = pl.BlockSpec((WAYS, 2, 16, LOCAL), lambda i: (0, 0, TAIL // 16, 0))
+    return pl.pallas_call(
+        short_kernel,
+        grid=(1,),
+        in_specs=[SMEM] * 2
+        + [whole_block((WAYS, 32, LOCAL)), whole_block((WAYS, 16, LOCAL))]
+        + [tail, whole_block((8, 128))]
+        + [whole_block((BLOCKS, 128))] * 2,
+        out_specs=[tail, whole_block((8, 128))],
+        out_shape=[
+            jax.ShapeDtypeStruct(grad.shape, BF16),
+            jax.ShapeDtypeStruct((8, 128), F32),
+        ],
+        input_output_aliases={4: 0},
+        compiler_params=params(1),
+        cost_estimate=pl.CostEstimate(
+            flops=20_000_000, bytes_accessed=1_000_000, transcendentals=12_000
+        ),
+        name="short_attention",
+    )(dest, move_len, short, short_g, grad, part, q_gain, k_gain)
+
+
+POST_ROWS = 64
 
 
 def post_kernel(q_ref, k_ref, raw_ref, qg_ref, kg_ref, dq_ref, dk_ref, oq_ref, ok_ref):
@@ -356,7 +398,8 @@
     )(q_in, k_in, raw, q_gain, k_gain, back, back)
 
 
-AHEAD = 4
+EARLY = (4, 1)
+LATE = (6, 3, 5, 2, 7)
 
 
 def swap_all(x, axis):
@@ -375,21 +418,23 @@
     packed, grad_rows = lax.optimization_barrier((pack_short(q_in, k_in, v_in), grad_out))
     spread = swap_all(packed, "dp")
     own, *outgoing = prepare(
-        dest_group, res_len, move_len, step_index, loss_weight,
+        dest_group, res_len, move_len, step_index.T.reshape(2 * GROUPS), loss_weight,
         q_in, k_in, v_in, grad_rows, gain_q, gain_k,
     )
-    arrived = [own] + [
-        lax.ppermute(x, "head", [(i, i ^ (n + 1)) for i in range(WAYS)])
-        for n, x in enumerate(outgoing)
-    ]
-    held = lax.optimization_barrier((spread, *arrived[1 : 1 + AHEAD]))
-    spread, arrived[1 : 1 + AHEAD] = held[0], held[1:]
+    slots = {0: own}
+    for n in EARLY + LATE:
+        slots[n] = lax.ppermute(outgoing[n - 1], "head", [(i, i ^ n) for i in range(WAYS)])
+    spread, *held = lax.optimization_barrier((spread, *(slots[n] for n in EARLY)))
+    slots.update(zip(EARLY, held, strict=True))
     routed = swap_all(scatter_short(dest_group, spread), "dp")
     short, raw = unpack_short(routed, gain_q, gain_k)
     short = swap_all(short, "head")
-    grad, part = attention(
-        dest_group, res_len, move_len, arrived, short,
-        q_gain.reshape(BLOCKS, 128), k_gain.reshape(BLOCKS, 128),
+    gain_q_rows, gain_k_rows = q_gain.reshape(BLOCKS, 128), k_gain.reshape(BLOCKS, 128)
+    grad, part, short_g = attention(
+        res_len, [slots[n] for n in range(WAYS)], gain_q_rows, gain_k_rows
+    )
+    grad, part = short_attention(
+        dest_group, move_len, short, short_g, grad, part, gain_q_rows, gain_k_rows
     )
     back = swap_all(grad, "head")
     total = gather_sum(gather_sum(part, ZRING), PLANE)

time: 177 us -> 167 us (0.944)
  waiting for transfers between devices: 31.5 us -> 21.6 us
  Pallas kernels: 33.6 us -> 31.6 us
  blocking collectives: 35.2 us -> 37 us
    all_to_all x4, waiting for transfers between devices: 10.3 us -> 1.27 us  [swap_all(): return lax.all_to_all(x, axis, split_axis=0, concat_axis=0, tiled=True)]
    unnamed x27 -> x12, local copies, waits for them, and re-layouts: 3.99 us -> 2.09 us
    all_gather x2, blocking collectives: 35.2 us -> 37 us  [gather_sum(): return jnp.sum(lax.all_gather(x, 'dp', axis_index_groups=rings), axis=0)]
    pallas_call x1 -> x2, Pallas kernels: 16.5 us -> 17.1 us  [the longest x1 13.3 us: attention(): pl.pallas_call(attention_kernel, grid=(HEADS,), in_specs=[SMEM] + [pl.Blo...]
  transfers between devices with their start and end apart: 11 -> 11, of which waited for: 5 -> 5; matrix products, arithmetic and copies ran while one was open for 1% -> 1% of each run, Pallas kernels for 5% -> 12%
where the time goes in v5:
time: 167 us; the launch traced here: 165 us
  starting transfers between devices  71 us (43%)
  blocking collectives  37 us (22%)
  Pallas kernels  31.6 us (19%)
  waiting for transfers between devices  21.6 us (13%)
  local copies, waits for them, and re-layouts  3.27 us (2%)
    all_to_all x4, starting transfers between devices, swap_all(): return lax.all_to_all(x, axis, split_axis=0, concat_axis=0, tiled=True)  42.5 us
    all_gather x2, blocking collectives, gather_sum(): return jnp.sum(lax.all_gather(x, 'dp', axis_index_groups=rings), axis=0)  37 us
    ppermute x7, starting transfers between devices, local(): lax.ppermute(outgoing[n - 1], 'head', [(i, i ^ n) for i in range(WAYS)])  28.5 us
    ppermute x7, waiting for transfers between devices, local(): lax.ppermute(outgoing[n - 1], 'head', [(i, i ^ n) for i in range(WAYS)])  20.3 us
    pallas_call x1, Pallas kernels, attention(): pl.pallas_call(attention_kernel, grid=(HEADS,), in_specs=[SMEM] + [pl.Blo...  13.3 us
    pallas_call x1, Pallas kernels, prepare(): pl.pallas_call(pre_kernel, grid=(TOK_DEV // PRE_ROWS,), in_specs=[SMEM] *...  5.21 us
    pallas_call x1, Pallas kernels, short_attention(): pl.pallas_call(short_kernel, grid=(1,), in_specs=[SMEM] * 2 + [whole_bloc...  3.81 us
    pallas_call x1, Pallas kernels, finish(): pl.pallas_call(post_kernel, grid=(TOK_DEV // POST_ROWS,), in_specs=[rows,...  3.72 us
  transfers between devices with their start and end apart: 11, of which 5 were waited for; matrix products, arithmetic and copies ran while one was open for 1% of the time, Pallas kernels for 12%

profile of v5, /device:TPU:1, one launch (start us, length us, event | category | flops | bytes accessed | tf_op | source)
XLA Modules:
  0.0 165.3 jit_solution(14964186038922593776)
XLA Ops:
  0.6 0.0 copy-start.5
  0.6 1.7 %pack_short.1 = bf16[64,16,128]{2,1,0:T(8,128)(2,1)} custom-call(bf16[128,3072]{1,0:T(8,128)(2,1)} %q_ref.5, bf16[128,3072]{1,0:T(8,128)(2,1)} %k_ref.5, bf16[128,3072]{1,0:T(8,128)(2,1)} %v_ref.3), custom_call_target="tpu_custom_call" | custom-call | tf_op jit(solution)/shard_map/pack_short/pallas_call | solution.py:62
  2.4 18.1 %all-to-all-start = ((bf16[64,16,128]{2,1,0:T(8,128)(2,1)}), bf16[64,16,128]{2,1,0:T(8,128)(2,1)S(1)}, u32[]{:S(2)}, u32[]{:S(2)}) async-start(bf16[64,16,128]{2,1,0:T(8,128)(2,1)} %pack_short.1), calls=%async_computation | async-start | bytes 524288 | tf_op jit(solution)/shard_map/all_to_all | solution.py:406
  20.5 0.0 copy-done.5
  20.5 0.6 reshape.29.step_ref
  21.1 5.2 %prepare.1 = (bf16[4,128,384]{2,1,0:T(8,128)(2,1)}, bf16[4,128,384]{2,1,0:T(8,128)(2,1)}, bf16[4,128,384]{2,1,0:T(8,128)(2,1)}, bf16[4,128,384]{2,1,0:T(8,128)(2...) custom-call(s32[64]{0:T(128)} %dest_ref.5, ...), custom_call_target="tpu_custom_call" | custom-call | flops 20000000 | bytes 6300000 | tf_op jit(solution)/shard_map/prepare/pallas_call | solution.py:162
  26.3 4.4 %collective-permute-start = (bf16[4,128,384]{2,1,0:T(8,128)(2,1)}, bf16[4,128,384]{2,1,0:T(8,128)(2,1)S(1)}, u32[]{:S(2)}, u32[]{:S(2)}) collective-permute-start(bf16[4,128,384]{2,1,0:T(8,128)(2,1)} %get-tuple-element.28), channel_id=1, source_target_pairs={{0,4},{1,5},{2,6},{3,7},{4,0},{5,1},{6,2},{7,3},{8,12},{9,13},{10,... | collective-permute-start | bytes 1179656 | tf_op jit(solution)/shard_map/ppermute | solution.py:426
  30.7 3.2 %collective-permute-start.1 = (bf16[4,128,384]{2,1,0:T(8,128)(2,1)}, bf16[4,128,384]{2,1,0:T(8,128)(2,1)}, u32[]{:S(2)}, u32[]{:S(2)}) collective-permute-start(bf16[4,128,384]{2,1,0:T(8,128)(2,1)} %get-tuple-element.29), channel_id=1, source_target_pairs={{0,1},{1,0},{2,3},{3,2},{4,5},{5,4},{6,7},{7,6},{8,9},{9,8},{10,11... | collective-permute-start | bytes 1179656 | tf_op jit(solution)/shard_map/ppermute | solution.py:426
  33.9 7.9 %collective-permute-done.rest_4_ = bf16[4,128,384]{2,1,0:T(8,128)(2,1)S(1)} collective-permute-done((bf16[4,128,384]{2,1,0:T(8,128)(2,1)}, bf16[4,128,384]{2,1,0:T(8,128)(2,1)S(1)}, u32[]{:S(2)}, u32[]{:S(2)}) %collective-permute-start) | collective-permute-done | bytes 393248 | tf_op jit(solution)/shard_map/ppermute | solution.py:426
  41.8 0.0 copy-start.4
  41.8 1.0 collective-permute-done.1.rest_1_
  42.8 0.0 all-to-all-done.in_ref
  42.8 0.0 copy-start
  42.8 0.7 copy-done
  43.5 2.1 %scatter_short.1 = bf16[64,16,128]{2,1,0:T(8,128)(2,1)} custom-call(s32[64]{0:T(128)} %dest_ref.5, bf16[64,16,128]{2,1,0:T(8,128)(2,1)} %copy-done), custom_call_target="tpu_custom_call" | custom-call | tf_op jit(solution)/shard_map/scatter_short/pallas_call | solution.py:83
  45.6 14.3 %all-to-all-start.1 = ((bf16[64,16,128]{2,1,0:T(8,128)(2,1)}), bf16[64,16,128]{2,1,0:T(8,128)(2,1)S(1)}, u32[]{:S(2)}, u32[]{:S(2)}) async-start(bf16[64,16,128]{2,1,0:T(8,128)(2,1)} %scatter_short.1), calls=%async_computation.1 | async-start | bytes 524288 | tf_op jit(solution)/shard_map/all_to_all | solution.py:406
  59.9 4.8 %collective-permute-start.2 = (bf16[4,128,384]{2,1,0:T(8,128)(2,1)}, bf16[4,128,384]{2,1,0:T(8,128)(2,1)}, u32[]{:S(2)}, u32[]{:S(2)}) collective-permute-start(bf16[4,128,384]{2,1,0:T(8,128)(2,1)} %get-tuple-element.35), channel_id=1, source_target_pairs={{0,2},{1,3},{2,0},{3,1},{4,6},{5,7},{6,4},{7,5},{8,10},{9,11},{10,... | collective-permute-start | bytes 1179656 | tf_op jit(solution)/shard_map/ppermute | solution.py:426
  64.7 2.7 %collective-permute-start.3 = (bf16[4,128,384]{2,1,0:T(8,128)(2,1)}, bf16[4,128,384]{2,1,0:T(8,128)(2,1)}, u32[]{:S(2)}, u32[]{:S(2)}) collective-permute-start(bf16[4,128,384]{2,1,0:T(8,128)(2,1)} %get-tuple-element.36), channel_id=1, source_target_pairs={{0,3},{1,2},{2,1},{3,0},{4,7},{5,6},{6,5},{7,4},{8,11},{9,10},{10,... | collective-permute-start | bytes 1179656 | tf_op jit(solution)/shard_map/ppermute | solution.py:426
  67.4 3.0 %collective-permute-start.4 = (bf16[4,128,384]{2,1,0:T(8,128)(2,1)}, bf16[4,128,384]{2,1,0:T(8,128)(2,1)}, u32[]{:S(2)}, u32[]{:S(2)}) collective-permute-start(bf16[4,128,384]{2,1,0:T(8,128)(2,1)} %get-tuple-element.38), channel_id=1, source_target_pairs={{0,5},{1,4},{2,7},{3,6},{4,1},{5,0},{6,3},{7,2},{8,13},{9,12},{10,... | collective-permute-start | bytes 1179656 | tf_op jit(solution)/shard_map/ppermute | solution.py:426
  70.4 6.3 %collective-permute-start.5 = (bf16[4,128,384]{2,1,0:T(8,128)(2,1)}, bf16[4,128,384]{2,1,0:T(8,128)(2,1)}, u32[]{:S(2)}, u32[]{:S(2)}) collective-permute-start(bf16[4,128,384]{2,1,0:T(8,128)(2,1)} %get-tuple-element.39), channel_id=1, source_target_pairs={{0,6},{1,7},{2,4},{3,5},{4,2},{5,3},{6,0},{7,1},{8,14},{9,15},{10,... | collective-permute-start | bytes 1179656 | tf_op jit(solution)/shard_map/ppermute | solution.py:426
  76.7 4.1 %collective-permute-start.6 = (bf16[4,128,384]{2,1,0:T(8,128)(2,1)}, bf16[4,128,384]{2,1,0:T(8,128)(2,1)}, u32[]{:S(2)}, u32[]{:S(2)}) collective-permute-start(bf16[4,128,384]{2,1,0:T(8,128)(2,1)} %get-tuple-element.40), channel_id=1, source_target_pairs={{0,7},{1,6},{2,5},{3,4},{4,3},{5,2},{6,1},{7,0},{8,15},{9,14},{10,... | collective-permute-start | bytes 1179656 | tf_op jit(solution)/shard_map/ppermute | solution.py:426
  80.9 1.3 all-to-all-done.1.in_ref
  82.1 0.0 copy-start.1
  82.1 0.7 copy-done.1
  82.8 1.8 %unpack_short.1 = (bf16[8,32,384]{2,1,0:T(8,128)(2,1)}, bf16[2,16,3072]{2,1,0:T(8,128)(2,1)}) custom-call(bf16[64,16,128]{2,1,0:T(8,128)(2,1)} %copy-done.1, f32[1,3072]{1,0:T(1,128)} %bitcast.14, f32[1,3072]{1,0:T(1,128)} %bitcast.19), custom_call_target="tpu_custom_call" | custom-call | tf_op jit(solution)/shard_map/unpack_short/pallas_call | solution.py:117
  84.6 5.6 %all-to-all-start.2 = ((bf16[8,32,384]{2,1,0:T(8,128)(2,1)}), bf16[8,32,384]{2,1,0:T(8,128)(2,1)S(1)}, u32[]{:S(2)}, u32[]{:S(2)}) async-start(bf16[8,32,384]{2,1,0:T(8,128)(2,1)} %get-tuple-element.32), calls=%async_computation.2 | async-start | bytes 393216 | tf_op jit(solution)/shard_map/all_to_all | solution.py:406
  90.3 0.0 collective-permute-done.2.rest_2_
  90.3 0.0 collective-permute-done.3.rest_3_
  90.3 0.0 collective-permute-done.4.rest_5_
  90.3 2.1 %collective-permute-done.5.rest_6_ = bf16[4,128,384]{2,1,0:T(8,128)(2,1)} collective-permute-done((bf16[4,128,384]{2,1,0:T(8,128)(2,1)}, bf16[4,128,384]{2,1,0:T(8,128)(2,1)}, u32[]{:S(2)}, u32[]{:S(2)}) %collective-permute-start.5) | collective-permute-done | bytes 393248 | tf_op jit(solution)/shard_map/ppermute | solution.py:426
  92.4 9.3 %collective-permute-done.6.rest_7_ = bf16[4,128,384]{2,1,0:T(8,128)(2,1)} collective-permute-done((bf16[4,128,384]{2,1,0:T(8,128)(2,1)}, bf16[4,128,384]{2,1,0:T(8,128)(2,1)}, u32[]{:S(2)}, u32[]{:S(2)}) %collective-permute-start.6) | collective-permute-done | bytes 393248 | tf_op jit(solution)/shard_map/ppermute | solution.py:426
  101.7 0.0 copy-done.4
  101.7 13.3 %attention.1 = (bf16[8,2,128,384]{3,2,1,0:T(8,128)(2,1)}, f32[8,128]{1,0:T(8,128)}, bf16[8,16,384]{2,1,0:T(8,128)(2,1)}) custom-call(s32[64]{0:T(128)} %res_ref.3, bf16[4,128,384]{2,1,0:T(8,128)(2,1)} %get-tuple-element.33.rest_0_, bf16[4,128,384]{2,1,0:T(8,128)(2,1)} %collective-permute-done.1.rest_1_, bf16[4,128,384]{2,1,0:T(8,128)(2,1)} %collective-permute-done.2.rest_2_, ...), custom_call_target="tpu_custom_call" | custom-call | flops 4000000000 | bytes 5000000 | tf_op jit(solution)/shard_map/attention/pallas_call | solution.py:274
  115.0 0.0 all-to-all-done.2.short_ref
  115.0 0.0 copy-start.2
  115.0 0.7 copy-done.2
  115.7 3.8 %short_attention.1 = (bf16[8,2,128,384]{3,2,1,0:T(8,128)(2,1)}, f32[8,128]{1,0:T(8,128)}) custom-call(s32[64]{0:T(128)} %dest_ref.5, s32[64]{0:T(128)} %move_ref.3, bf16[8,32,384]{2,1,0:T(8,128)(2,1)} %copy-done.2, bf16[8,16,384]{2,1,0:T(8,128)(2,1)} %get-tuple-element.41.g_ref, ...), custom_call_target="tpu_custom_call", output_to_operand_aliasing={{0}: (4, {})} | custom-call | flops 20000000 | bytes 1000000 | tf_op jit(solution)/shard_map/short_attention/pallas_call | solution.py:335
  119.5 0.0 copy-start.3
  119.5 4.4 %all-to-all-start.3 = ((bf16[8,2,128,384]{3,2,1,0:T(8,128)(2,1)}), bf16[8,2,128,384]{3,2,1,0:T(8,128)(2,1)}, u32[]{:S(2)}, u32[]{:S(2)}) async-start(bf16[8,2,128,384]{3,2,1,0:T(8,128)(2,1)} %get-tuple-element.44), calls=%async_computation.3 | async-start | bytes 3145728 | tf_op jit(solution)/shard_map/all_to_all | solution.py:406
  124.0 0.0 copy-done.3
  124.0 24.5 %all-gather = f32[128,128]{1,0:T(8,128)S(1)} all-gather(f32[8,128]{1,0:T(8,128)S(1)} %copy-done.3), channel_id=2, replica_groups={{0,16,32,48,64,80,96,112,128,144,160,176,192,208,224,240},{8,24,40,56,7..., dimensions={0}, use_global_device_ids=true | all-gather | bytes 69632 | tf_op jit(solution)/shard_map/all_gather | solution.py:410
  148.5 12.5 %all-gather.1 = f32[32,128]{1,0:T(8,128)S(1)} all-gather(f32[8,128]{1,0:T(8,128)S(1)} %bitcast_reduce_fusion), channel_id=3, replica_groups={{0,8,256,264},{16,24,272,280},{32,40,288,296},{48,56,304,312},{64,72,32..., dimensions={0}, use_global_device_ids=true | all-gather | bytes 20480 | tf_op jit(solution)/shard_map/all_gather | solution.py:410
  161.0 0.6 slice_bitcast_fusion
  161.6 0.0 all-to-all-done.3.dq_ref.dk_ref
  161.6 3.7 %finish.1 = (bf16[128,3072]{1,0:T(8,128)(2,1)}, bf16[128,3072]{1,0:T(8,128)(2,1)}) custom-call(bf16[128,3072]{1,0:T(8,128)(2,1)} %q_ref.5, bf16[128,3072]{1,0:T(8,128)(2,1)} %k_ref.5, bf16[2,16,3072]{2,1,0:T(8,128)(2,1)} %get-tuple-element.31.raw_ref, f32[1,3072]{1,0:T(1,128)} %bitcast.17, f32[1,3072]{1,0:T(1,128)} %bitcast.22, ...), custom_call_target="tpu_custom_call" | custom-call | flops 20000000 | bytes 4800000 | tf_op jit(solution)/shard_map/finish/pallas_call | solution.py:381
  (2 shorter events, 0.0 us)
Async XLA Ops:
  0.6 19.8 %copy-start.5 = (s32[64,2]{0,1:T(2,128)S(1)}, s32[64,2]{0,1:T(2,128)}, u32[]{:S(2)}) copy-start(s32[64,2]{0,1:T(2,128)} %param.19) | copy-start | bytes 1540
  2.4 40.4 %all-to-all-start = ((bf16[64,16,128]{2,1,0:T(8,128)(2,1)}), bf16[64,16,128]{2,1,0:T(8,128)(2,1)S(1)}, u32[]{:S(2)}, u32[]{:S(2)}) async-start(bf16[64,16,128]{2,1,0:T(8,128)(2,1)} %pack_short.1), calls=%async_computation | async-start | bytes 524288 | tf_op jit(solution)/shard_map/all_to_all | solution.py:406
  26.3 15.5 %collective-permute-start = (bf16[4,128,384]{2,1,0:T(8,128)(2,1)}, bf16[4,128,384]{2,1,0:T(8,128)(2,1)S(1)}, u32[]{:S(2)}, u32[]{:S(2)}) collective-permute-start(bf16[4,128,384]{2,1,0:T(8,128)(2,1)} %get-tuple-element.28), channel_id=1, source_target_pairs={{0,4},{1,5},{2,6},{3,7},{4,0},{5,1},{6,2},{7,3},{8,12},{9,13},{10,... | collective-permute-start | bytes 1179656 | tf_op jit(solution)/shard_map/ppermute | solution.py:426
  30.7 12.1 %collective-permute-start.1 = (bf16[4,128,384]{2,1,0:T(8,128)(2,1)}, bf16[4,128,384]{2,1,0:T(8,128)(2,1)}, u32[]{:S(2)}, u32[]{:S(2)}) collective-permute-start(bf16[4,128,384]{2,1,0:T(8,128)(2,1)} %get-tuple-element.29), channel_id=1, source_target_pairs={{0,1},{1,0},{2,3},{3,2},{4,5},{5,4},{6,7},{7,6},{8,9},{9,8},{10,11... | collective-permute-start | bytes 1179656 | tf_op jit(solution)/shard_map/ppermute | solution.py:426
  41.8 59.9 %copy-start.4 = (bf16[4,128,384]{2,1,0:T(8,128)(2,1)}, bf16[4,128,384]{2,1,0:T(8,128)(2,1)S(1)}, u32[]{:S(2)}) copy-start(bf16[4,128,384]{2,1,0:T(8,128)(2,1)S(1)} %collective-permute-done.rest_4_) | copy-start | bytes 1179652
  42.8 0.7 copy-start
  45.6 36.6 %all-to-all-start.1 = ((bf16[64,16,128]{2,1,0:T(8,128)(2,1)}), bf16[64,16,128]{2,1,0:T(8,128)(2,1)S(1)}, u32[]{:S(2)}, u32[]{:S(2)}) async-start(bf16[64,16,128]{2,1,0:T(8,128)(2,1)} %scatter_short.1), calls=%async_computation.1 | async-start | bytes 524288 | tf_op jit(solution)/shard_map/all_to_all | solution.py:406
  59.9 30.4 %collective-permute-start.2 = (bf16[4,128,384]{2,1,0:T(8,128)(2,1)}, bf16[4,128,384]{2,1,0:T(8,128)(2,1)}, u32[]{:S(2)}, u32[]{:S(2)}) collective-permute-start(bf16[4,128,384]{2,1,0:T(8,128)(2,1)} %get-tuple-element.35), channel_id=1, source_target_pairs={{0,2},{1,3},{2,0},{3,1},{4,6},{5,7},{6,4},{7,5},{8,10},{9,11},{10,... | collective-permute-start | bytes 1179656 | tf_op jit(solution)/shard_map/ppermute | solution.py:426
  64.7 25.5 %collective-permute-start.3 = (bf16[4,128,384]{2,1,0:T(8,128)(2,1)}, bf16[4,128,384]{2,1,0:T(8,128)(2,1)}, u32[]{:S(2)}, u32[]{:S(2)}) collective-permute-start(bf16[4,128,384]{2,1,0:T(8,128)(2,1)} %get-tuple-element.36), channel_id=1, source_target_pairs={{0,3},{1,2},{2,1},{3,0},{4,7},{5,6},{6,5},{7,4},{8,11},{9,10},{10,... | collective-permute-start | bytes 1179656 | tf_op jit(solution)/shard_map/ppermute | solution.py:426
  67.4 22.8 %collective-permute-start.4 = (bf16[4,128,384]{2,1,0:T(8,128)(2,1)}, bf16[4,128,384]{2,1,0:T(8,128)(2,1)}, u32[]{:S(2)}, u32[]{:S(2)}) collective-permute-start(bf16[4,128,384]{2,1,0:T(8,128)(2,1)} %get-tuple-element.38), channel_id=1, source_target_pairs={{0,5},{1,4},{2,7},{3,6},{4,1},{5,0},{6,3},{7,2},{8,13},{9,12},{10,... | collective-permute-start | bytes 1179656 | tf_op jit(solution)/shard_map/ppermute | solution.py:426
  70.4 22.0 %collective-permute-start.5 = (bf16[4,128,384]{2,1,0:T(8,128)(2,1)}, bf16[4,128,384]{2,1,0:T(8,128)(2,1)}, u32[]{:S(2)}, u32[]{:S(2)}) collective-permute-start(bf16[4,128,384]{2,1,0:T(8,128)(2,1)} %get-tuple-element.39), channel_id=1, source_target_pairs={{0,6},{1,7},{2,4},{3,5},{4,2},{5,3},{6,0},{7,1},{8,14},{9,15},{10,... | collective-permute-start | bytes 1179656 | tf_op jit(solution)/shard_map/ppermute | solution.py:426
  76.7 25.0 %collective-permute-start.6 = (bf16[4,128,384]{2,1,0:T(8,128)(2,1)}, bf16[4,128,384]{2,1,0:T(8,128)(2,1)}, u32[]{:S(2)}, u32[]{:S(2)}) collective-permute-start(bf16[4,128,384]{2,1,0:T(8,128)(2,1)} %get-tuple-element.40), channel_id=1, source_target_pairs={{0,7},{1,6},{2,5},{3,4},{4,3},{5,2},{6,1},{7,0},{8,15},{9,14},{10,... | collective-permute-start | bytes 1179656 | tf_op jit(solution)/shard_map/ppermute | solution.py:426
  82.1 0.7 copy-start.1
  84.6 30.4 %all-to-all-start.2 = ((bf16[8,32,384]{2,1,0:T(8,128)(2,1)}), bf16[8,32,384]{2,1,0:T(8,128)(2,1)S(1)}, u32[]{:S(2)}, u32[]{:S(2)}) async-start(bf16[8,32,384]{2,1,0:T(8,128)(2,1)} %get-tuple-element.32), calls=%async_computation.2 | async-start | bytes 393216 | tf_op jit(solution)/shard_map/all_to_all | solution.py:406
  115.0 0.7 copy-start.2
  119.5 4.4 %copy-start.3 = (f32[8,128]{1,0:T(8,128)S(1)}, f32[8,128]{1,0:T(8,128)}, u32[]{:S(2)}) copy-start(f32[8,128]{1,0:T(8,128)} %get-tuple-element.47) | copy-start | bytes 12292
  119.5 42.1 %all-to-all-start.3 = ((bf16[8,2,128,384]{3,2,1,0:T(8,128)(2,1)}), bf16[8,2,128,384]{3,2,1,0:T(8,128)(2,1)}, u32[]{:S(2)}, u32[]{:S(2)}) async-start(bf16[8,2,128,384]{3,2,1,0:T(8,128)(2,1)} %get-tuple-element.44), calls=%async_computation.3 | async-start | bytes 3145728 | tf_op jit(solution)/shard_map/all_to_all | solution.py:406

commit v6 on v5

--- a/solution.py
+++ b/solution.py
@@ -95,7 +95,14 @@
     return rows * scale * gain
 
 
-def unpack_kernel(in_ref, qg_ref, kg_ref, send_ref, raw_ref):
+def unpack_kernel(
+    dest_ref, move_ref, step_ref, table_ref, in_ref, go_ref, qg_ref, kg_ref, send_ref, raw_ref
+):
+    slot = lax.axis_index("head")
+    source = find_source(dest_ref, lax.axis_index("dp"))
+    position = slot * MOV + lax.broadcasted_iota(jnp.int32, (MOV, 1), 0)
+    weight = jnp.where(position < move_ref[source], table_ref[step_ref[GROUPS + source]], 0.0)
+    weighted = go_ref[...].astype(F32)[8:16] * weight
     pair = jnp.concatenate([in_ref[c] for c in range(BLOCKS)], axis=1).astype(F32)
     tail = jnp.concatenate([in_ref[BLOCKS + c] for c in range(BLOCKS // 2)], axis=1).astype(F32)
     q, k = pair[0:8], pair[8:16]
@@ -104,7 +111,7 @@
     kn = norm_rows(k, kg_ref[...])
     zero = jnp.zeros((8, HD), F32)
     first = jnp.concatenate([qn, kn], axis=0).astype(BF16)
-    second = jnp.concatenate([v, zero], axis=0).astype(BF16)
+    second = jnp.concatenate([v, weighted], axis=0).astype(BF16)
     for p in range(WAYS):
         send_ref[p, 0:16, :] = first[:, p * LOCAL : (p + 1) * LOCAL]
         send_ref[p, 16:32, :] = second[:, p * LOCAL : (p + 1) * LOCAL]
@@ -112,19 +119,26 @@
     raw_ref[1] = jnp.concatenate([zero, k], axis=0).astype(BF16)
 
 
-def unpack_short(parts, q_gain, k_gain):
-    whole = pl.BlockSpec(memory_space=pltpu.VMEM)
+def unpack_short(dest, move_len, steps, table, parts, grad_out, q_gain, k_gain):
+    gain = pl.BlockSpec((1, HD), lambda i: (0, 0))
     return pl.pallas_call(
         unpack_kernel,
-        in_specs=[whole] * 3,
-        out_specs=[whole] * 2,
+        grid=(1,),
+        in_specs=[SMEM] * 4
+        + [pl.BlockSpec((GROUPS, 16, 128), lambda i: (0, 0, 0))]
+        + [pl.BlockSpec((16, HD), lambda i: (TOK_DEV // 16 - 1, 0))]
+        + [gain] * 2,
+        out_specs=[
+            pl.BlockSpec((WAYS, 32, LOCAL), lambda i: (0, 0, 0)),
+            pl.BlockSpec((2, 16, HD), lambda i: (0, 0, 0)),
+        ],
         out_shape=[
             jax.ShapeDtypeStruct((WAYS, 32, LOCAL), BF16),
             jax.ShapeDtypeStruct((2, 16, HD), BF16),
         ],
-        compiler_params=params(),
+        compiler_params=params(1),
         name="unpack_short",
-    )(parts, q_gain, k_gain)
+    )(dest, move_len, steps, table, parts, grad_out, q_gain, k_gain)
 
 
 PRE_ROWS = 64
@@ -207,7 +221,7 @@
 
 def attention_kernel(res_ref, *rest):
     slots, rest = rest[:WAYS], rest[WAYS:]
-    qg_ref, kg_ref, out_ref, gain_ref, short_g_ref, *rest = rest
+    short_ref, part_ref, qg_ref, kg_ref, out_ref, gain_ref, *rest = rest
     q_ref, k_ref, v_ref, g_ref, qt_ref, kt_ref, vt_ref, gt_ref, dq_ref, dk_ref = rest
     head = pl.program_id(0)
     slot = lax.axis_index("head")
@@ -218,7 +232,6 @@
     for s in range(WAYS):
         here = pl.ds(s * TOK_DEV, TOK_DEV)
         q, k, v, g = (slots[s][n] for n in range(4))
-        short_g_ref[peers[s]] = g[TAIL:]
         g = jnp.where(rows < RES, g.astype(F32), 0.0)
         limit = jnp.minimum(stay_len - peers[s] * RES, RES)
         q_ref[here, 0:128] = q
@@ -256,36 +269,42 @@
     for s in range(WAYS):
         for n, grad in enumerate((dq, dk)):
             block = grad[s * TOK_DEV : (s + 1) * TOK_DEV]
-            out_ref[peers[s], n] = block
+            out_ref[peers[s], n, 0:TAIL] = block[:TAIL]
+            tail = block[TAIL:].astype(F32) + short_ref[peers[s], n].astype(F32)
+            out_ref[peers[s], n, TAIL:TOK_DEV] = tail.astype(BF16)
+
+    @pl.when(head == 0)
+    def _():
+        gain_ref[...] = part_ref[...]
 
     def total(grad, norm, gain_ref):
         summed = jnp.sum(grad.astype(F32) * norm.astype(F32), axis=0, keepdims=True)
         return summed / gain_ref[pl.ds(slot * HEADS + head, 1)]
 
-    gain_ref[pl.ds(head, 1)] = total(dq, q_ref[:, 0:128], qg_ref)
-    gain_ref[pl.ds(HEADS + head, 1)] = total(dk, k_ref[:, 0:128], kg_ref)
+    gain_ref[pl.ds(head, 1)] += total(dq, q_ref[:, 0:128], qg_ref)
+    gain_ref[pl.ds(HEADS + head, 1)] += total(dk, k_ref[:, 0:128], kg_ref)
 
 
 def whole_block(shape):
     return pl.BlockSpec(shape, lambda b: (0,) * len(shape))
 
 
-def attention(res_len, slots, q_gain, k_gain):
+def attention(res_len, slots, short, part, q_gain, k_gain):
     return pl.pallas_call(
         attention_kernel,
         grid=(HEADS,),
         in_specs=[SMEM]
         + [pl.BlockSpec((4, TOK_DEV, 128), lambda b: (0, 0, b))] * WAYS
+        + [pl.BlockSpec((WAYS, 2, 16, 128), lambda b: (0, 0, 0, b))]
+        + [whole_block((8, 128))]
         + [whole_block((BLOCKS, 128))] * 2,
         out_specs=[
             pl.BlockSpec((WAYS, 2, TOK_DEV, 128), lambda b: (0, 0, 0, b)),
             whole_block((8, 128)),
-            pl.BlockSpec((WAYS, 16, 128), lambda b: (0, 0, b)),
         ],
         out_shape=[
             jax.ShapeDtypeStruct((WAYS, 2, TOK_DEV, LOCAL), BF16),
             jax.ShapeDtypeStruct((8, 128), F32),
-            jax.ShapeDtypeStruct((WAYS, 16, LOCAL), BF16),
         ],
         scratch_shapes=[pltpu.VMEM((ALL, 256), BF16)] * 2
         + [pltpu.VMEM((ALL, 128), BF16)] * 2
@@ -297,18 +316,19 @@
             flops=4_000_000_000, bytes_accessed=5_000_000, transcendentals=3_200_000
         ),
         name="attention",
-    )(res_len, *slots, q_gain, k_gain)
+    )(res_len, *slots, short, part, q_gain, k_gain)
 
 
 def short_kernel(
-    dest_ref, move_ref, short_ref, g_ref, grad_ref, part_ref, qg_ref, kg_ref, out_ref, gain_ref
+    dest_ref, move_ref, short_ref, qg_ref, kg_ref, out_ref, gain_ref
 ):
     slot = lax.axis_index("head")
     move_len = move_ref[find_source(dest_ref, lax.axis_index("dp"))]
     count = WAYS * MOV
     lane = lax.broadcasted_iota(jnp.int32, (1, count), 1)
     bias = jnp.where(lane < move_len, 0.0, -1e30).astype(F32)
-    gain_ref[...] = part_ref[...]
+    gain_ref[...] = jnp.zeros_like(gain_ref)
+    zero = jnp.zeros((WAYS, MOV, 128), F32)
 
     def rows_at(values, first):
         return values[:, first : first + MOV].reshape(count, 128)
@@ -317,40 +337,34 @@
         cols = slice(head * 128, (head + 1) * 128)
         lines = short_ref[:, :, cols].astype(F32)
         q, k, v = rows_at(lines, 0), rows_at(lines, 8), rows_at(lines, 16)
-        g = rows_at(g_ref[:, :, cols].astype(F32), 8)
+        g = rows_at(lines, 24)
         dq, dk = grads(q.astype(BF16), k.astype(BF16), v.astype(BF16), g.astype(BF16), bias)
         dq = dq.astype(BF16).astype(F32)
         dk = (dk * SCALE).astype(BF16).astype(F32)
         for n, grad, norm, gains in ((0, dq, q, qg_ref), (1, dk, k, kg_ref)):
-            kept = grad_ref[:, n, :, cols].astype(F32)[:, 0:8]
-            both = jnp.concatenate([kept, grad.reshape(WAYS, MOV, 128)], axis=1)
+            both = jnp.concatenate([zero, grad.reshape(WAYS, MOV, 128)], axis=1)
             out_ref[:, n, :, cols] = both.astype(BF16)
             total = jnp.sum(grad * norm, axis=0, keepdims=True)
             total = total / gains[pl.ds(slot * HEADS + head, 1)]
-            gain_ref[n * HEADS + head : n * HEADS + head + 1] += total
-
-
-def short_attention(dest, move_len, short, short_g, grad, part, q_gain, k_gain):
-    tail = pl.BlockSpec((WAYS, 2, 16, LOCAL), lambda i: (0, 0, TAIL // 16, 0))
+            gain_ref[n * HEADS + head : n * HEADS + head + 1] = total
+
+
+def short_attention(dest, move_len, short, q_gain, k_gain):
     return pl.pallas_call(
         short_kernel,
         grid=(1,),
-        in_specs=[SMEM] * 2
-        + [whole_block((WAYS, 32, LOCAL)), whole_block((WAYS, 16, LOCAL))]
-        + [tail, whole_block((8, 128))]
-        + [whole_block((BLOCKS, 128))] * 2,
-        out_specs=[tail, whole_block((8, 128))],
+        in_specs=[SMEM] * 2 + [whole_block((WAYS, 32, LOCAL))] + [whole_block((BLOCKS, 128))] * 2,
+        out_specs=[whole_block((WAYS, 2, 16, LOCAL)), whole_block((8, 128))],
         out_shape=[
-            jax.ShapeDtypeStruct(grad.shape, BF16),
+            jax.ShapeDtypeStruct((WAYS, 2, 16, LOCAL), BF16),
             jax.ShapeDtypeStruct((8, 128), F32),
         ],
-        input_output_aliases={4: 0},
         compiler_params=params(1),
         cost_estimate=pl.CostEstimate(
             flops=20_000_000, bytes_accessed=1_000_000, transcendentals=12_000
         ),
         name="short_attention",
-    )(dest, move_len, short, short_g, grad, part, q_gain, k_gain)
+    )(dest, move_len, short, q_gain, k_gain)
 
 
 POST_ROWS = 64
@@ -398,8 +412,8 @@
     )(q_in, k_in, raw, q_gain, k_gain, back, back)
 
 
-EARLY = (4, 1)
-LATE = (6, 3, 5, 2, 7)
+EARLY = (4,)
+LATE = (6, 1, 3, 5, 2, 7)
 
 
 def swap_all(x, axis):
@@ -415,10 +429,11 @@
     res_len, move_len, step_index, dest_group, loss_weight,
 ):
     gain_q, gain_k = q_gain.reshape(1, HD), k_gain.reshape(1, HD)
+    steps = step_index.T.reshape(2 * GROUPS)
     packed, grad_rows = lax.optimization_barrier((pack_short(q_in, k_in, v_in), grad_out))
     spread = swap_all(packed, "dp")
     own, *outgoing = prepare(
-        dest_group, res_len, move_len, step_index.T.reshape(2 * GROUPS), loss_weight,
+        dest_group, res_len, move_len, steps, loss_weight,
         q_in, k_in, v_in, grad_rows, gain_q, gain_k,
     )
     slots = {0: own}
@@ -427,14 +442,14 @@
     spread, *held = lax.optimization_barrier((spread, *(slots[n] for n in EARLY)))
     slots.update(zip(EARLY, held, strict=True))
     routed = swap_all(scatter_short(dest_group, spread), "dp")
-    short, raw = unpack_short(routed, gain_q, gain_k)
+    short, raw = unpack_short(
+        dest_group, move_len, steps, loss_weight, routed, grad_rows, gain_q, gain_k
+    )
     short = swap_all(short, "head")
     gain_q_rows, gain_k_rows = q_gain.reshape(BLOCKS, 128), k_gain.reshape(BLOCKS, 128)
-    grad, part, short_g = attention(
-        res_len, [slots[n] for n in range(WAYS)], gain_q_rows, gain_k_rows
-    )
-    grad, part = short_attention(
-        dest_group, move_len, short, short_g, grad, part, gain_q_rows, gain_k_rows
+    short, part = short_attention(dest_group, move_len, short, gain_q_rows, gain_k_rows)
+    grad, part = attention(
+        res_len, [slots[n] for n in range(WAYS)], short, part, gain_q_rows, gain_k_rows
     )
     back = swap_all(grad, "head")
     total = gather_sum(gather_sum(part, ZRING), PLANE)

time: 167 us -> 172 us (1.030)
  blocking collectives: 37 us -> 59.2 us
  waiting for transfers between devices: 21.6 us -> 12.1 us
  starting transfers between devices: 71 us -> 62.9 us
    all_to_all x0 -> x1, blocking collectives: none -> 24 us  [swap_all(): return lax.all_to_all(x, axis, split_axis=0, concat_axis=0, tiled=True)]
    ppermute x7, waiting for transfers between devices: 20.3 us -> 11.1 us  [local(): lax.ppermute(outgoing[n - 1], 'head', [(i, i ^ n) for i in range(WAYS)])]
    all_to_all x4 -> x3, starting transfers between devices: 42.5 us -> 34.9 us  [swap_all(): return lax.all_to_all(x, axis, split_axis=0, concat_axis=0, tiled=True)]
    all_gather x2, blocking collectives: 37 us -> 35.2 us  [gather_sum(): return jnp.sum(lax.all_gather(x, 'dp', axis_index_groups=rings), axis=0)]
  transfers between devices with their start and end apart: 11 -> 10, of which waited for: 5 -> 2; matrix products, arithmetic and copies ran while one was open for 1% -> 1% of each run, Pallas kernels for 12% -> 7%
where the time goes in v6:
time: 172 us; the launch traced here: 171 us
  starting transfers between devices  62.9 us (37%)
  blocking collectives  59.2 us (34%)
  Pallas kernels  32.7 us (19%)
  waiting for transfers between devices  12.1 us (7%)
  local copies, waits for them, and re-layouts  3.33 us (2%)
    all_gather x2, blocking collectives, gather_sum(): return jnp.sum(lax.all_gather(x, 'dp', axis_index_groups=rings), axis=0)  35.2 us
    all_to_all x3, starting transfers between devices, swap_all(): return lax.all_to_all(x, axis, split_axis=0, concat_axis=0, tiled=True)  34.9 us
    ppermute x7, starting transfers between devices, local(): lax.ppermute(outgoing[n - 1], 'head', [(i, i ^ n) for i in range(WAYS)])  27.9 us
    all_to_all x1, blocking collectives, swap_all(): return lax.all_to_all(x, axis, split_axis=0, concat_axis=0, tiled=True)  24 us
    pallas_call x1, Pallas kernels, attention(): pl.pallas_call(attention_kernel, grid=(HEADS,), in_specs=[SMEM] + [pl.Blo...  13.8 us
    ppermute x7, waiting for transfers between devices, local(): lax.ppermute(outgoing[n - 1], 'head', [(i, i ^ n) for i in range(WAYS)])  11.1 us
    pallas_call x1, Pallas kernels, prepare(): pl.pallas_call(pre_kernel, grid=(TOK_DEV // PRE_ROWS,), in_specs=[SMEM] *...  5.18 us
    pallas_call x1, Pallas kernels, finish(): pl.pallas_call(post_kernel, grid=(TOK_DEV // POST_ROWS,), in_specs=[rows,...  3.72 us
  transfers between devices with their start and end apart: 10, of which 2 were waited for; matrix products, arithmetic and copies ran while one was open for 1% of the time, Pallas kernels for 7%

profile of v6, /device:TPU:1, one launch (start us, length us, event | category | flops | bytes accessed | tf_op | source)
XLA Modules:
  0.0 171.0 jit_solution(14442376075477649398)
XLA Ops:
  0.6 0.0 copy-start.5
  0.6 1.7 %pack_short.1 = bf16[64,16,128]{2,1,0:T(8,128)(2,1)} custom-call(bf16[128,3072]{1,0:T(8,128)(2,1)} %q_ref.5, bf16[128,3072]{1,0:T(8,128)(2,1)} %k_ref.5, bf16[128,3072]{1,0:T(8,128)(2,1)} %v_ref.3), custom_call_target="tpu_custom_call" | custom-call | tf_op jit(solution)/shard_map/pack_short/pallas_call | solution.py:62
  2.4 18.1 %all-to-all-start = ((bf16[64,16,128]{2,1,0:T(8,128)(2,1)}), bf16[64,16,128]{2,1,0:T(8,128)(2,1)S(1)}, u32[]{:S(2)}, u32[]{:S(2)}) async-start(bf16[64,16,128]{2,1,0:T(8,128)(2,1)} %pack_short.1), calls=%async_computation | async-start | bytes 524288 | tf_op jit(solution)/shard_map/all_to_all | solution.py:420
  20.4 0.0 copy-done.5
  20.5 0.6 reshape.29.step_ref
  21.1 5.2 %prepare.1 = (bf16[4,128,384]{2,1,0:T(8,128)(2,1)}, bf16[4,128,384]{2,1,0:T(8,128)(2,1)}, bf16[4,128,384]{2,1,0:T(8,128)(2,1)}, bf16[4,128,384]{2,1,0:T(8,128)(2...) custom-call(s32[64]{0:T(128)} %dest_ref.7, ...), custom_call_target="tpu_custom_call" | custom-call | flops 20000000 | bytes 6300000 | tf_op jit(solution)/shard_map/prepare/pallas_call | solution.py:176
  26.2 4.4 %collective-permute-start = (bf16[4,128,384]{2,1,0:T(8,128)(2,1)}, bf16[4,128,384]{2,1,0:T(8,128)(2,1)S(1)}, u32[]{:S(2)}, u32[]{:S(2)}) collective-permute-start(bf16[4,128,384]{2,1,0:T(8,128)(2,1)} %get-tuple-element.26), channel_id=1, source_target_pairs={{0,4},{1,5},{2,6},{3,7},{4,0},{5,1},{6,2},{7,3},{8,12},{9,13},{10,... | collective-permute-start | bytes 1179656 | tf_op jit(solution)/shard_map/ppermute | solution.py:441
  30.6 11.1 %collective-permute-done.rest_4_ = bf16[4,128,384]{2,1,0:T(8,128)(2,1)S(1)} collective-permute-done((bf16[4,128,384]{2,1,0:T(8,128)(2,1)}, bf16[4,128,384]{2,1,0:T(8,128)(2,1)S(1)}, u32[]{:S(2)}, u32[]{:S(2)}) %collective-permute-start) | collective-permute-done | bytes 393248 | tf_op jit(solution)/shard_map/ppermute | solution.py:441
  41.7 0.0 copy-start.3
  41.7 1.0 all-to-all-done.in_ref
  42.7 0.0 copy-start.1
  42.7 0.7 copy-done.1
  43.4 2.1 %scatter_short.1 = bf16[64,16,128]{2,1,0:T(8,128)(2,1)} custom-call(s32[64]{0:T(128)} %dest_ref.7, bf16[64,16,128]{2,1,0:T(8,128)(2,1)} %copy-done.1), custom_call_target="tpu_custom_call" | custom-call | tf_op jit(solution)/shard_map/scatter_short/pallas_call | solution.py:83
  45.5 12.6 %all-to-all-start.1 = ((bf16[64,16,128]{2,1,0:T(8,128)(2,1)}), bf16[64,16,128]{2,1,0:T(8,128)(2,1)S(1)}, u32[]{:S(2)}, u32[]{:S(2)}) async-start(bf16[64,16,128]{2,1,0:T(8,128)(2,1)} %scatter_short.1), calls=%async_computation.1 | async-start | bytes 524288 | tf_op jit(solution)/shard_map/all_to_all | solution.py:420
  58.0 3.2 %collective-permute-start.1 = (bf16[4,128,384]{2,1,0:T(8,128)(2,1)}, bf16[4,128,384]{2,1,0:T(8,128)(2,1)S(1)}, u32[]{:S(2)}, u32[]{:S(2)}) collective-permute-start(bf16[4,128,384]{2,1,0:T(8,128)(2,1)} %get-tuple-element.30), channel_id=1, source_target_pairs={{0,1},{1,0},{2,3},{3,2},{4,5},{5,4},{6,7},{7,6},{8,9},{9,8},{10,11... | collective-permute-start | bytes 1179656 | tf_op jit(solution)/shard_map/ppermute | solution.py:441
  61.2 4.5 %collective-permute-start.2 = (bf16[4,128,384]{2,1,0:T(8,128)(2,1)}, bf16[4,128,384]{2,1,0:T(8,128)(2,1)}, u32[]{:S(2)}, u32[]{:S(2)}) collective-permute-start(bf16[4,128,384]{2,1,0:T(8,128)(2,1)} %get-tuple-element.31), channel_id=1, source_target_pairs={{0,2},{1,3},{2,0},{3,1},{4,6},{5,7},{6,4},{7,5},{8,10},{9,11},{10,... | collective-permute-start | bytes 1179656 | tf_op jit(solution)/shard_map/ppermute | solution.py:441
  65.8 1.9 %collective-permute-start.3 = (bf16[4,128,384]{2,1,0:T(8,128)(2,1)}, bf16[4,128,384]{2,1,0:T(8,128)(2,1)}, u32[]{:S(2)}, u32[]{:S(2)}) collective-permute-start(bf16[4,128,384]{2,1,0:T(8,128)(2,1)} %get-tuple-element.32), channel_id=1, source_target_pairs={{0,3},{1,2},{2,1},{3,0},{4,7},{5,6},{6,5},{7,4},{8,11},{9,10},{10,... | collective-permute-start | bytes 1179656 | tf_op jit(solution)/shard_map/ppermute | solution.py:441
  67.7 3.9 %collective-permute-start.4 = (bf16[4,128,384]{2,1,0:T(8,128)(2,1)}, bf16[4,128,384]{2,1,0:T(8,128)(2,1)}, u32[]{:S(2)}, u32[]{:S(2)}) collective-permute-start(bf16[4,128,384]{2,1,0:T(8,128)(2,1)} %get-tuple-element.34), channel_id=1, source_target_pairs={{0,5},{1,4},{2,7},{3,6},{4,1},{5,0},{6,3},{7,2},{8,13},{9,12},{10,... | collective-permute-start | bytes 1179656 | tf_op jit(solution)/shard_map/ppermute | solution.py:441
  71.6 6.2 %collective-permute-start.5 = (bf16[4,128,384]{2,1,0:T(8,128)(2,1)}, bf16[4,128,384]{2,1,0:T(8,128)(2,1)}, u32[]{:S(2)}, u32[]{:S(2)}) collective-permute-start(bf16[4,128,384]{2,1,0:T(8,128)(2,1)} %get-tuple-element.35), channel_id=1, source_target_pairs={{0,6},{1,7},{2,4},{3,5},{4,2},{5,3},{6,0},{7,1},{8,14},{9,15},{10,... | collective-permute-start | bytes 1179656 | tf_op jit(solution)/shard_map/ppermute | solution.py:441
  77.8 0.0 collective-permute-done.1.rest_1_
  77.8 0.0 copy-start.4
  77.8 0.7 copy-done.4
  78.6 3.9 %collective-permute-start.6 = (bf16[4,128,384]{2,1,0:T(8,128)(2,1)}, bf16[4,128,384]{2,1,0:T(8,128)(2,1)}, u32[]{:S(2)}, u32[]{:S(2)}) collective-permute-start(bf16[4,128,384]{2,1,0:T(8,128)(2,1)} %get-tuple-element.36), channel_id=1, source_target_pairs={{0,7},{1,6},{2,5},{3,4},{4,3},{5,2},{6,1},{7,0},{8,15},{9,14},{10,... | collective-permute-start | bytes 1179656 | tf_op jit(solution)/shard_map/ppermute | solution.py:441
  82.4 0.0 all-to-all-done.1.in_ref
  82.4 0.0 copy-start
  82.5 0.7 copy-done
  83.2 2.5 %unpack_short.1 = (bf16[8,32,384]{2,1,0:T(8,128)(2,1)}, bf16[2,16,3072]{2,1,0:T(8,128)(2,1)}) custom-call(s32[64]{0:T(128)} %dest_ref.7, s32[64]{0:T(128)} %move_ref.5, s32[128]{0:T(128)} %reshape.29.step_ref, f32[1000]{0:T(1024)} %table_ref.3, bf16[64,16,128]{2,1,0:T(8,128)(2,1)} %copy-done, bf16[128,3072]{1,0:T(8,128)(2,1)} %go_ref.1, f32[1,3072]{1,0:T(1,128)} %bitcast.14, ...), custom_call_target="tpu_custom_call" | custom-call | tf_op jit(solution)/shard_map/unpack_short/pallas_call | solution.py:124
  85.6 24.0 %all_to_all.20.short_ref = bf16[8,32,384]{2,1,0:T(8,128)(2,1)} all-to-all(bf16[8,32,384]{2,1,0:T(8,128)(2,1)} %get-tuple-element.37), channel_id=1, replica_groups=mesh['dp'=64,'head'=8] {'head'}, dimensions={0} | all-to-all | bytes 393216 | tf_op jit(solution)/shard_map/all_to_all | solution.py:420
  109.6 3.7 %short_attention.1 = (bf16[8,2,16,384]{3,2,1,0:T(8,128)(2,1)}, f32[8,128]{1,0:T(8,128)}) custom-call(s32[64]{0:T(128)} %dest_ref.7, s32[64]{0:T(128)} %move_ref.5, bf16[8,32,384]{2,1,0:T(8,128)(2,1)} %all_to_all.20.short_ref, f32[24,128]{1,0:T(8,128)} %bitcast.15, f32[24,128]{1,0:T(8,128)} %bitcast.20), custom_call_target="tpu_custom_call" | custom-call | flops 20000000 | bytes 1000000 | tf_op jit(solution)/shard_map/short_attention/pallas_call | solution.py:353
  113.3 0.0 collective-permute-done.2.rest_2_
  113.3 0.0 collective-permute-done.3.rest_3_
  113.3 0.0 collective-permute-done.4.rest_5_
  113.3 0.0 collective-permute-done.5.rest_6_
  113.3 0.0 collective-permute-done.6.rest_7_
  113.3 0.0 copy-done.3
  113.3 13.8 %attention.1 = (bf16[8,2,128,384]{3,2,1,0:T(8,128)(2,1)}, f32[8,128]{1,0:T(8,128)}) custom-call(s32[64]{0:T(128)} %res_ref.3, bf16[4,128,384]{2,1,0:T(8,128)(2,1)} %get-tuple-element.29.rest_0_, bf16[4,128,384]{2,1,0:T(8,128)(2,1)} %copy-done.4, bf16[4,128,384]{2,1,0:T(8,128)(2,1)} %collective-permute-done.2.rest_2_, ...), custom_call_target="tpu_custom_call" | custom-call | flops 4000000000 | bytes 5000000 | tf_op jit(solution)/shard_map/attention/pallas_call | solution.py:293
  127.1 0.0 copy-start.2
  127.1 4.3 %all-to-all-start.3 = ((bf16[8,2,128,384]{3,2,1,0:T(8,128)(2,1)}), bf16[8,2,128,384]{3,2,1,0:T(8,128)(2,1)}, u32[]{:S(2)}, u32[]{:S(2)}) async-start(bf16[8,2,128,384]{3,2,1,0:T(8,128)(2,1)} %get-tuple-element.40), calls=%async_computation.3 | async-start | bytes 3145728 | tf_op jit(solution)/shard_map/all_to_all | solution.py:420
  131.5 0.0 copy-done.2
  131.5 25.0 %all-gather = f32[128,128]{1,0:T(8,128)S(1)} all-gather(f32[8,128]{1,0:T(8,128)S(1)} %copy-done.2), channel_id=2, replica_groups={{0,16,32,48,64,80,96,112,128,144,160,176,192,208,224,240},{8,24,40,56,7..., dimensions={0}, use_global_device_ids=true | all-gather | bytes 69632 | tf_op jit(solution)/shard_map/all_gather | solution.py:424
  156.5 10.2 %all-gather.1 = f32[32,128]{1,0:T(8,128)S(1)} all-gather(f32[8,128]{1,0:T(8,128)S(1)} %bitcast_reduce_fusion), channel_id=3, replica_groups={{0,8,256,264},{16,24,272,280},{32,40,288,296},{48,56,304,312},{64,72,32..., dimensions={0}, use_global_device_ids=true | all-gather | bytes 20480 | tf_op jit(solution)/shard_map/all_gather | solution.py:424
  166.7 0.6 slice_bitcast_fusion
  167.3 0.0 all-to-all-done.3.dq_ref.dk_ref
  167.3 3.7 %finish.1 = (bf16[128,3072]{1,0:T(8,128)(2,1)}, bf16[128,3072]{1,0:T(8,128)(2,1)}) custom-call(bf16[128,3072]{1,0:T(8,128)(2,1)} %q_ref.5, bf16[128,3072]{1,0:T(8,128)(2,1)} %k_ref.5, bf16[2,16,3072]{2,1,0:T(8,128)(2,1)} %get-tuple-element.28.raw_ref, f32[1,3072]{1,0:T(1,128)} %bitcast.17, f32[1,3072]{1,0:T(1,128)} %bitcast.22, ...), custom_call_target="tpu_custom_call" | custom-call | flops 20000000 | bytes 4800000 | tf_op jit(solution)/shard_map/finish/pallas_call | solution.py:395
  (2 shorter events, 0.0 us)
Async XLA Ops:
  0.6 19.8 %copy-start.5 = (s32[64,2]{0,1:T(2,128)S(1)}, s32[64,2]{0,1:T(2,128)}, u32[]{:S(2)}) copy-start(s32[64,2]{0,1:T(2,128)} %param.19) | copy-start | bytes 1540
  2.4 40.3 %all-to-all-start = ((bf16[64,16,128]{2,1,0:T(8,128)(2,1)}), bf16[64,16,128]{2,1,0:T(8,128)(2,1)S(1)}, u32[]{:S(2)}, u32[]{:S(2)}) async-start(bf16[64,16,128]{2,1,0:T(8,128)(2,1)} %pack_short.1), calls=%async_computation | async-start | bytes 524288 | tf_op jit(solution)/shard_map/all_to_all | solution.py:420
  26.2 15.5 %collective-permute-start = (bf16[4,128,384]{2,1,0:T(8,128)(2,1)}, bf16[4,128,384]{2,1,0:T(8,128)(2,1)S(1)}, u32[]{:S(2)}, u32[]{:S(2)}) collective-permute-start(bf16[4,128,384]{2,1,0:T(8,128)(2,1)} %get-tuple-element.26), channel_id=1, source_target_pairs={{0,4},{1,5},{2,6},{3,7},{4,0},{5,1},{6,2},{7,3},{8,12},{9,13},{10,... | collective-permute-start | bytes 1179656 | tf_op jit(solution)/shard_map/ppermute | solution.py:441
  41.7 71.6 %copy-start.3 = (bf16[4,128,384]{2,1,0:T(8,128)(2,1)}, bf16[4,128,384]{2,1,0:T(8,128)(2,1)S(1)}, u32[]{:S(2)}) copy-start(bf16[4,128,384]{2,1,0:T(8,128)(2,1)S(1)} %collective-permute-done.rest_4_) | copy-start | bytes 1179652
  42.7 0.7 copy-start.1
  45.5 37.0 %all-to-all-start.1 = ((bf16[64,16,128]{2,1,0:T(8,128)(2,1)}), bf16[64,16,128]{2,1,0:T(8,128)(2,1)S(1)}, u32[]{:S(2)}, u32[]{:S(2)}) async-start(bf16[64,16,128]{2,1,0:T(8,128)(2,1)} %scatter_short.1), calls=%async_computation.1 | async-start | bytes 524288 | tf_op jit(solution)/shard_map/all_to_all | solution.py:420
  58.0 19.8 %collective-permute-start.1 = (bf16[4,128,384]{2,1,0:T(8,128)(2,1)}, bf16[4,128,384]{2,1,0:T(8,128)(2,1)S(1)}, u32[]{:S(2)}, u32[]{:S(2)}) collective-permute-start(bf16[4,128,384]{2,1,0:T(8,128)(2,1)} %get-tuple-element.30), channel_id=1, source_target_pairs={{0,1},{1,0},{2,3},{3,2},{4,5},{5,4},{6,7},{7,6},{8,9},{9,8},{10,11... | collective-permute-start | bytes 1179656 | tf_op jit(solution)/shard_map/ppermute | solution.py:441
  61.2 52.0 %collective-permute-start.2 = (bf16[4,128,384]{2,1,0:T(8,128)(2,1)}, bf16[4,128,384]{2,1,0:T(8,128)(2,1)}, u32[]{:S(2)}, u32[]{:S(2)}) collective-permute-start(bf16[4,128,384]{2,1,0:T(8,128)(2,1)} %get-tuple-element.31), channel_id=1, source_target_pairs={{0,2},{1,3},{2,0},{3,1},{4,6},{5,7},{6,4},{7,5},{8,10},{9,11},{10,... | collective-permute-start | bytes 1179656 | tf_op jit(solution)/shard_map/ppermute | solution.py:441
  65.8 47.5 %collective-permute-start.3 = (bf16[4,128,384]{2,1,0:T(8,128)(2,1)}, bf16[4,128,384]{2,1,0:T(8,128)(2,1)}, u32[]{:S(2)}, u32[]{:S(2)}) collective-permute-start(bf16[4,128,384]{2,1,0:T(8,128)(2,1)} %get-tuple-element.32), channel_id=1, source_target_pairs={{0,3},{1,2},{2,1},{3,0},{4,7},{5,6},{6,5},{7,4},{8,11},{9,10},{10,... | collective-permute-start | bytes 1179656 | tf_op jit(solution)/shard_map/ppermute | solution.py:441
  67.7 45.5 %collective-permute-start.4 = (bf16[4,128,384]{2,1,0:T(8,128)(2,1)}, bf16[4,128,384]{2,1,0:T(8,128)(2,1)}, u32[]{:S(2)}, u32[]{:S(2)}) collective-permute-start(bf16[4,128,384]{2,1,0:T(8,128)(2,1)} %get-tuple-element.34), channel_id=1, source_target_pairs={{0,5},{1,4},{2,7},{3,6},{4,1},{5,0},{6,3},{7,2},{8,13},{9,12},{10,... | collective-permute-start | bytes 1179656 | tf_op jit(solution)/shard_map/ppermute | solution.py:441
  71.6 41.7 %collective-permute-start.5 = (bf16[4,128,384]{2,1,0:T(8,128)(2,1)}, bf16[4,128,384]{2,1,0:T(8,128)(2,1)}, u32[]{:S(2)}, u32[]{:S(2)}) collective-permute-start(bf16[4,128,384]{2,1,0:T(8,128)(2,1)} %get-tuple-element.35), channel_id=1, source_target_pairs={{0,6},{1,7},{2,4},{3,5},{4,2},{5,3},{6,0},{7,1},{8,14},{9,15},{10,... | collective-permute-start | bytes 1179656 | tf_op jit(solution)/shard_map/ppermute | solution.py:441
  77.8 0.7 copy-start.4
  78.6 34.7 %collective-permute-start.6 = (bf16[4,128,384]{2,1,0:T(8,128)(2,1)}, bf16[4,128,384]{2,1,0:T(8,128)(2,1)}, u32[]{:S(2)}, u32[]{:S(2)}) collective-permute-start(bf16[4,128,384]{2,1,0:T(8,128)(2,1)} %get-tuple-element.36), channel_id=1, source_target_pairs={{0,7},{1,6},{2,5},{3,4},{4,3},{5,2},{6,1},{7,0},{8,15},{9,14},{10,... | collective-permute-start | bytes 1179656 | tf_op jit(solution)/shard_map/ppermute | solution.py:441
  82.4 0.7 copy-start
  127.1 4.3 %copy-start.2 = (f32[8,128]{1,0:T(8,128)S(1)}, f32[8,128]{1,0:T(8,128)}, u32[]{:S(2)}) copy-start(f32[8,128]{1,0:T(8,128)} %get-tuple-element.43) | copy-start | bytes 12292
  127.1 40.1 %all-to-all-start.3 = ((bf16[8,2,128,384]{3,2,1,0:T(8,128)(2,1)}), bf16[8,2,128,384]{3,2,1,0:T(8,128)(2,1)}, u32[]{:S(2)}, u32[]{:S(2)}) async-start(bf16[8,2,128,384]{3,2,1,0:T(8,128)(2,1)} %get-tuple-element.40), calls=%async_computation.3 | async-start | bytes 3145728 | tf_op jit(solution)/shard_map/all_to_all | solution.py:420
